TPU v7x, 128 devices: a whole 4x4x4 slice. The times are simulated.
128 devices in a mesh: dp: 16 (over z_lo, x, core), seq: 8 (over y, z_hi).
Axes of the slice: x: 4, y: 4, z: 4 (z_hi: 2, z_lo: 2; z = z_hi * 2 + z_lo), core: 2. Of those that a mesh axis runs over, the one named last changes fastest.
Arguments:
- tokens: bfloat16 [1024, 16, 2048], P('seq', 'dp'), may hold values from -6 to 6
- cotangent: bfloat16 [1024, 16, 2048], P('seq', 'dp'), may hold values from -6 to 6
- w_qkv: bfloat16 [2048, 3, 2048], P(None, None, 'seq'), may hold values from -0.125 to 0.125
- w_out: bfloat16 [2048, 2048], P('seq'), may hold values from -4 to 4
- w_gate_up: bfloat16 [2048, 2, 5461], P('seq'), may hold values from -0.125 to 0.125
- w_down: bfloat16 [2048, 5461], P('seq'), may hold values from -0.4375 to 0.4375
- attn_gain: float32 [2048], replicated, may hold values from 0.5 to 1.5
- attn_bias: float32 [2048], replicated, may hold values from -1 to 1
- ffn_gain: float32 [2048], replicated, may hold values from 0.5 to 1.5
- ffn_bias: float32 [2048], replicated, may hold values from -1 to 1
- prefix_len: int32 [16], P('dp'), may hold values from 1 to 1024
- clusters: int32 [16], replicated, may hold values from 0 to 15
Outputs:
- output: bfloat16 [1024, 16, 2048], P('seq', 'dp')
- input_grad: float32 [1024, 16, 2048], P('seq', 'dp')
- grad_qkv: float32 [2048, 3, 2048], P(None, None, 'seq')
- grad_out: float32 [2048, 2048], P('seq')
- grad_gate_up: float32 [2048, 2, 5461], P('seq')
- grad_down: float32 [2048, 5461], P('seq')
- grad_attn_gain: float32 [2048], P('seq')
- grad_attn_bias: float32 [2048], P('seq')
- grad_ffn_gain: float32 [2048], P('seq')
- grad_ffn_bias: float32 [2048], P('seq')
All inputs are finite; a program needn't handle non-finite values.
Results may differ from a plain program's by a relative error of at most 0.03.
Values may be sent and summed in bfloat16 or wider, within the bound.
A program may use at most 192 MiB of HBM per device.

v0:
```python
import jax
import jax.numpy as jnp
from jax import lax
from jax.sharding import PartitionSpec as P

HEAD_DIM = 128


deep_alpha = 48.0**0.25
norm_eps = 1e-05
rotary_base = 10000.0


def rotary_tables(length, head_width):
    half_width = head_width // 2
    position = jnp.arange(length, dtype=jnp.float32)
    inverse = rotary_base ** (-jnp.arange(half_width, dtype=jnp.float32) * 2.0 / head_width)
    angles = position[:, None] * inverse[None, :]
    cosine_table = jnp.cos(angles)
    sine_table = jnp.sin(angles)
    return (
        jnp.concatenate([cosine_table, cosine_table], axis=1),
        jnp.concatenate([sine_table, sine_table], axis=1),
    )


def rotate(values_in, cosine_table, sine_table):
    half_width = values_in.shape[-1] // 2
    turned = jnp.concatenate([-values_in[..., half_width:], values_in[..., :half_width]], axis=-1)
    return values_in * cosine_table + turned * sine_table


def unrotate(values_in, cosine_table, sine_table):
    half_width = values_in.shape[-1] // 2
    turned = jnp.concatenate([-values_in[..., half_width:], values_in[..., :half_width]], axis=-1)
    return values_in * cosine_table - turned * sine_table


def norm_forward(row_total, gain, bias):
    center = row_total - jnp.mean(row_total, axis=-1, keepdims=True)
    spread = jnp.mean(center * center, axis=-1, keepdims=True)
    inverse = lax.rsqrt(spread + norm_eps)
    unit = center * inverse
    return (unit * gain + bias, unit, inverse)


def norm_backward(grad_result, unit, inverse, gain):
    grad_unit = grad_result * gain
    grad_total = inverse * (
        grad_unit
        - jnp.mean(grad_unit, axis=-1, keepdims=True)
        - unit * jnp.mean(grad_unit * unit, axis=-1, keepdims=True)
    )
    return (grad_total, jnp.sum(grad_result * unit, axis=(0, 1)), jnp.sum(grad_result, axis=(0, 1)))


def gelu_product(gate_part, up_part):
    return jax.nn.gelu(gate_part, approximate=False) * up_part


def on_device(
    tokens,
    cotangent,
    w_qkv,
    w_out,
    w_gate_up,
    w_down,
    attn_gain,
    attn_bias,
    ffn_gain,
    ffn_bias,
    prefix_len,
    clusters,
):
    seq_count = lax.axis_size("seq")
    rows_here, group_seqs, model_width = tokens.shape
    length = rows_here * seq_count
    own_width = w_qkv.shape[2]
    heads_here = own_width // HEAD_DIM
    pair_count = group_seqs * heads_here
    ff_total = w_down.shape[1]
    ff_cols = (ff_total + seq_count - 1) // seq_count
    ff_padded = ff_cols * seq_count
    score_scale = HEAD_DIM ** (-0.5)
    own_ids = lax.dynamic_slice_in_dim(clusters, lax.axis_index("dp") * group_seqs, group_seqs)
    same_cluster = (own_ids[:, None] == clusters[None, :]).astype(jnp.float32)
    seq_weight = 1.0 / jnp.sum(same_cluster, axis=1)
    stacked = jnp.concatenate([w_gate_up, w_down[:, None, :]], axis=1)
    stacked = jnp.pad(stacked, ((0, 0), (0, 0), (0, ff_padded - ff_total)))
    ffn_columns = lax.all_to_all(stacked, "seq", split_axis=2, concat_axis=0, tiled=True)
    gate_up_w = ffn_columns[:, :2]
    down_cols = ffn_columns[:, 2]
    tokens_all = lax.all_gather(tokens, "seq", axis=0, tiled=True)
    project = jnp.einsum("tsd,dch->tsch", tokens_all, w_qkv, preferred_element_type=jnp.float32)
    heads_split = project.reshape(length, group_seqs, 3, heads_here, HEAD_DIM)
    cosine_table, sine_table = rotary_tables(length, HEAD_DIM)
    cosine_wide = cosine_table[:, None, None, :]
    sine_wide = sine_table[:, None, None, :]
    queries = (rotate(heads_split[:, :, 0], cosine_wide, sine_wide) * score_scale).astype(
        jnp.bfloat16
    )
    key_rows = rotate(heads_split[:, :, 1], cosine_wide, sine_wide).astype(jnp.bfloat16)
    value_rows = heads_split[:, :, 2].astype(jnp.bfloat16)

    def by_pair(values_in):
        return values_in.transpose(1, 2, 0, 3).reshape(pair_count, length, HEAD_DIM)

    def by_rows(values_in):
        return values_in.reshape(group_seqs, heads_here, length, HEAD_DIM).transpose(2, 0, 1, 3)

    query_pairs = by_pair(queries)
    key_pairs = by_pair(key_rows)
    value_pairs = by_pair(value_rows)
    pair_prefix = jnp.repeat(prefix_len, heads_here)
    block_rows = min(512, length)
    num_blocks = length // block_rows
    positions = jnp.arange(length, dtype=jnp.int32)
    starts = jnp.arange(num_blocks, dtype=jnp.int32) * block_rows
    query_blocks = query_pairs.reshape(pair_count, num_blocks, block_rows, HEAD_DIM).transpose(
        1, 0, 2, 3
    )

    def masked_scores(query_block, first_row):
        scores = jnp.einsum(
            "gqe,gke->gqk", query_block, key_pairs, preferred_element_type=jnp.float32
        )
        row_pos = first_row + jnp.arange(block_rows, dtype=jnp.int32)
        visible = (positions[None, None, :] < pair_prefix[:, None, None]) | (
            positions[None, None, :] <= row_pos[None, :, None]
        )
        return jnp.where(visible, scores, -1e30)

    def forward_block(block_item):
        query_block, first_row = block_item
        scores = masked_scores(query_block, first_row)
        row_peak = jnp.max(scores, axis=-1, keepdims=True)
        exponent = jnp.exp(scores - row_peak)
        row_total = jnp.sum(exponent, axis=-1, keepdims=True)
        weights_low = (exponent / row_total).astype(jnp.bfloat16)
        result = jnp.einsum(
            "gqk,gke->gqe", weights_low, value_pairs, preferred_element_type=jnp.float32
        )
        return (result, (row_peak + jnp.log(row_total))[..., 0])

    attn_blocks, lse_blocks = lax.map(forward_block, (query_blocks, starts))
    mixed_pairs = attn_blocks.transpose(1, 0, 2, 3).reshape(pair_count, length, HEAD_DIM)
    heads_out = by_rows(mixed_pairs.astype(jnp.bfloat16)).reshape(length, group_seqs, own_width)
    piece_rows = heads_out
    attended = lax.psum_scatter(
        jnp.einsum("tsh,hd->tsd", piece_rows, w_out, preferred_element_type=jnp.float32).astype(
            jnp.bfloat16
        ),
        "seq",
        scatter_dimension=0,
        tiled=True,
    ).astype(jnp.float32)
    normed, unit_one, inverse_one = norm_forward(
        deep_alpha * tokens.astype(jnp.float32) + attended, attn_gain, attn_bias
    )
    normed_all = lax.all_gather(normed.astype(jnp.bfloat16), "seq", axis=0, tiled=True)
    gate_up = jnp.einsum("tsd,dcf->tscf", normed_all, gate_up_w, preferred_element_type=jnp.float32)
    hidden = gelu_product(gate_up[:, :, 0], gate_up[:, :, 1]).astype(jnp.bfloat16)
    piece_rows = hidden
    branch = lax.psum_scatter(
        jnp.einsum("tsf,df->tsd", piece_rows, down_cols, preferred_element_type=jnp.float32).astype(
            jnp.bfloat16
        ),
        "seq",
        scatter_dimension=0,
        tiled=True,
    ).astype(jnp.float32)
    result, unit_two, inverse_two = norm_forward(deep_alpha * normed + branch, ffn_gain, ffn_bias)
    output = result.astype(jnp.bfloat16)
    weighted = cotangent.astype(jnp.float32) * seq_weight[None, :, None]
    grad_z2, ffn_gain_part, ffn_bias_part = norm_backward(weighted, unit_two, inverse_two, ffn_gain)
    grad_z2_all = lax.all_gather(grad_z2.astype(jnp.bfloat16), "seq", axis=0, tiled=True)
    grad_hidden = jnp.einsum(
        "tsd,df->tsf", grad_z2_all, down_cols, preferred_element_type=jnp.float32
    )
    _, gelu_back = jax.vjp(gelu_product, gate_up[:, :, 0], gate_up[:, :, 1])
    grad_gate, grad_up = gelu_back(grad_hidden)
    grad_gu_low = jnp.stack([grad_gate, grad_up], axis=2).astype(jnp.bfloat16)
    down_grad = jnp.einsum("tsd,tsf->df", grad_z2_all, hidden, preferred_element_type=jnp.float32)
    gate_up_grad = jnp.einsum(
        "tsd,tscf->dcf", normed_all, grad_gu_low, preferred_element_type=jnp.float32
    )
    piece_rows = grad_gu_low
    grad_normed = deep_alpha * grad_z2 + lax.psum_scatter(
        jnp.einsum(
            "tscf,dcf->tsd", piece_rows, gate_up_w, preferred_element_type=jnp.float32
        ).astype(jnp.bfloat16),
        "seq",
        scatter_dimension=0,
        tiled=True,
    ).astype(jnp.float32)
    grad_z1, attn_gain_part, attn_bias_part = norm_backward(
        grad_normed, unit_one, inverse_one, attn_gain
    )
    grad_z1_all = lax.all_gather(grad_z1.astype(jnp.bfloat16), "seq", axis=0, tiled=True)
    grad_heads = jnp.einsum(
        "tsd,hd->tsh", grad_z1_all, w_out, preferred_element_type=jnp.float32
    ).astype(jnp.bfloat16)
    out_grad = jnp.einsum("tsh,tsd->hd", heads_out, grad_z1_all, preferred_element_type=jnp.float32)
    grad_pairs = by_pair(grad_heads.reshape(length, group_seqs, heads_here, HEAD_DIM))
    grad_blocks = grad_pairs.reshape(pair_count, num_blocks, block_rows, HEAD_DIM).transpose(
        1, 0, 2, 3
    )

    def backward_block(carried, block_item):
        key_grad, value_grad = carried
        query_block, grad_block, lse_block, first_row = block_item
        scores = masked_scores(query_block, first_row)
        weights_full = jnp.exp(scores - lse_block[..., None])
        grad_weights = jnp.einsum(
            "gqe,gke->gqk", grad_block, value_pairs, preferred_element_type=jnp.float32
        )
        inner_sum = jnp.sum(weights_full * grad_weights, axis=-1, keepdims=True)
        grad_scores = (weights_full * (grad_weights - inner_sum)).astype(jnp.bfloat16)
        query_grad = jnp.einsum(
            "gqk,gke->gqe", grad_scores, key_pairs, preferred_element_type=jnp.float32
        )
        key_grad = key_grad + jnp.einsum(
            "gqk,gqe->gke", grad_scores, query_block, preferred_element_type=jnp.float32
        )
        value_grad = value_grad + jnp.einsum(
            "gqk,gqe->gke",
            weights_full.astype(jnp.bfloat16),
            grad_block,
            preferred_element_type=jnp.float32,
        )
        return ((key_grad, value_grad), query_grad)

    zero_grads = jnp.zeros((pair_count, length, HEAD_DIM), jnp.float32)
    (key_grad, value_grad), query_grads = lax.scan(
        backward_block, (zero_grads, zero_grads), (query_blocks, grad_blocks, lse_blocks, starts)
    )
    query_grad = query_grads.transpose(1, 0, 2, 3).reshape(pair_count, length, HEAD_DIM)
    query_pre = unrotate(by_rows(query_grad) * score_scale, cosine_wide, sine_wide)
    key_pre = unrotate(by_rows(key_grad), cosine_wide, sine_wide)
    grad_project = jnp.stack([query_pre, key_pre, by_rows(value_grad)], axis=2).astype(jnp.bfloat16)
    grad_project = grad_project.reshape(length, group_seqs, 3, own_width)
    qkv_grad = jnp.einsum(
        "tsd,tsch->dch", tokens_all, grad_project, preferred_element_type=jnp.float32
    )
    piece_rows = grad_project
    input_grad = deep_alpha * grad_z1 + lax.psum_scatter(
        jnp.einsum("tsch,dch->tsd", piece_rows, w_qkv, preferred_element_type=jnp.float32).astype(
            jnp.bfloat16
        ),
        "seq",
        scatter_dimension=0,
        tiled=True,
    ).astype(jnp.float32)
    norm_part = jnp.stack([attn_gain_part, attn_bias_part, ffn_gain_part, ffn_bias_part], axis=1)
    ffn_grad = jnp.concatenate([gate_up_grad, down_grad[:, None, :]], axis=1)
    qkv_total, out_total, ffn_total, norm_total = (
        lax.psum(qkv_grad.astype(jnp.bfloat16), "dp").astype(jnp.float32),
        lax.psum(out_grad.astype(jnp.bfloat16), "dp").astype(jnp.float32),
        lax.psum(ffn_grad.astype(jnp.bfloat16), "dp").astype(jnp.float32),
        lax.psum(norm_part.astype(jnp.bfloat16), "dp").astype(jnp.float32),
    )
    ffn_rows_back, norm_rows_back = (
        lax.all_to_all(
            ffn_total.astype(jnp.bfloat16), "seq", split_axis=0, concat_axis=2, tiled=True
        ).astype(ffn_total.dtype),
        lax.all_to_all(
            norm_total[:, :, None].astype(jnp.bfloat16),
            "seq",
            split_axis=0,
            concat_axis=2,
            tiled=True,
        ).astype(jnp.float32),
    )
    ffn_whole = ffn_rows_back[:, :, :ff_total]
    norm_whole = jnp.sum(norm_rows_back, axis=2)
    return (
        output,
        input_grad,
        qkv_total,
        out_total,
        ffn_whole[:, :2],
        ffn_whole[:, 2],
        norm_whole[:, 0],
        norm_whole[:, 1],
        norm_whole[:, 2],
        norm_whole[:, 3],
    )


def solution(mesh):
    return jax.shard_map(
        on_device,
        mesh=mesh,
        in_specs=(
            P("seq", "dp", None),
            P("seq", "dp", None),
            P(None, None, "seq"),
            P("seq", None),
            P("seq", None, None),
            P("seq", None),
            P(),
            P(),
            P(),
            P(),
            P("dp"),
            P(),
        ),
        out_specs=(
            P("seq", "dp", None),
            P("seq", "dp", None),
            P(None, None, "seq"),
            P("seq", None),
            P("seq", None, None),
            P("seq", None),
            P("seq"),
            P("seq"),
            P("seq"),
            P("seq"),
        ),
        check_vma=False,
    )
```

profile of v0, /device:TPU:1, one launch (start us, length us, event | category | flops | bytes accessed | tf_op | source)
XLA Modules:
  0.0 1293.4 jit_solution(9938979925401404982)
XLA Ops:
  14.6 70.2 %all-gather.5.cloned.1.call-done = bf16[1024,1,2048]{2,0,1:T(8,128)(2,1)} async-done(((bf16[128,1,2048]{2,0,1:T(8,128)(2,1)}), bf16[1024,1,2048]{2,0,1:T(8,128)(2,1)}) %all-gather.5.cloned.1.call-update) | async-done | bytes 4194320 | tf_op jit(solution)/shard_map/all_gather | solution.py:93
  102.3 14.1 %while.30 = (s32[]{:T(128)}, bf16[2,2,512,128]{3,2,0,1:T(8,128)(2,1)}, f32[2,2,512]{2,1,0:T(2,128)S(1)}, s32[2]{0:T(128)S(1)}, bf16[2,2,512,128]{3,2,1,0:T(8,128...) while((s32[]{:T(128)}, ...), condition=%wide.region_3.4_spmd.clone.clone, body=%wide.region_0.3_spmd.clone.clone.sunk | while | flops 549979648 | bytes 20758716 | solution.py:145
  121.2 20.0 %copy.100 = bf16[256,1,5461]{0,1,2:T(2,128)(2,1)S(1)} copy(bf16[256,1,5461]{0,2,1:T(8,128)(2,1)} %bitcast.347) | data formatting | bytes 5592064 | tf_op jit(solution)/shard_map/broadcast_in_dim | solution.py:88
  141.2 22.1 %fusion.46 = bf16[256,3,5464]{0,1,2:T(4,128)(2,1)} fusion(bf16[256,1,5461]{0,1,2:T(2,128)(2,1)S(1)} %copy.100, bf16[256,2,5461]{0,1,2:T(2,128)(2,1)} %param.20), kind=kLoop, calls=%fused_computation.56 | loop fusion | flops 29374464 | bytes 16780800 | tf_op jit(solution)/shard_map/concatenate | solution.py:88
  168.8 141.7 %reduce-scatter.5.cloned.1.call-done = bf16[128,1,2048]{2,0,1:T(8,128)(2,1)} async-done(((bf16[1024,1,2048]{2,0,1:T(8,128)(2,1)}), bf16[128,1,2048]{2,0,1:T(8,128)(2,1)}) %reduce-scatter.5.cloned.1.call-update) | async-done | bytes 524304 | tf_op jit(solution)/shard_map/reduce_scatter | solution.py:149
  315.4 14.3 %all-to-all-done = bf16[256,3,5464]{0,1,2:T(4,128)(2,1)} async-done(((bf16[256,3,5464]{0,1,2:T(4,128)(2,1)}), bf16[256,3,5464]{0,1,2:T(4,128)(2,1)}, u32[]{:S(2)}, u32[]{:S(2)}) %all-to-all-start) | async-done | bytes 8392736 | tf_op jit(solution)/shard_map/all_to_all | solution.py:90
  329.7 8.7 copy.143
  338.4 9.8 all_to_all.30
  348.2 55.7 %all-gather.7.cloned.1.call-done = bf16[1024,1,2048]{2,0,1:T(8,128)(2,1)} async-done(((bf16[128,1,2048]{2,0,1:T(8,128)(2,1)}), bf16[1024,1,2048]{2,0,1:T(8,128)(2,1)}) %all-gather.7.cloned.1.call-update) | async-done | bytes 4194320 | tf_op jit(solution)/shard_map/all_gather | solution.py:160
  403.9 9.3 fusion.116
  413.2 6.3 fusion.84
  420.6 6.8 convert_bitcast_fusion
  430.6 79.1 %reduce-scatter.7.cloned.1.call-done = bf16[128,1,2048]{2,0,1:T(8,128)(2,1)} async-done(((bf16[1024,1,2048]{2,0,1:T(8,128)(2,1)}), bf16[128,1,2048]{2,0,1:T(8,128)(2,1)}) %reduce-scatter.7.cloned.1.call-update) | async-done | bytes 524304 | tf_op jit(solution)/shard_map/reduce_scatter | solution.py:164
  514.2 71.0 %all-gather.9.cloned.1.call-done = bf16[1024,1,2048]{2,0,1:T(8,128)(2,1)} async-done(((bf16[128,1,2048]{2,0,1:T(8,128)(2,1)}), bf16[1024,1,2048]{2,0,1:T(8,128)(2,1)}) %all-gather.9.cloned.1.call-update) | async-done | bytes 4194320 | tf_op jit(solution)/shard_map/all_gather | solution.py:176
  590.9 8.2 fusion.127
  603.7 8.4 fusion.51
  612.2 82.1 %reduce-scatter.9.cloned.1.call-done = bf16[128,1,2048]{2,0,1:T(8,128)(2,1)} async-done(((bf16[1024,1,2048]{2,0,1:T(8,128)(2,1)}), bf16[128,1,2048]{2,0,1:T(8,128)(2,1)}) %reduce-scatter.9.cloned.1.call-update) | async-done | bytes 524304 | tf_op jit(solution)/shard_map/reduce_scatter | solution.py:188
  704.7 8.0 convolution_convert_fusion
  712.7 6.8 pad_maximum_fusion
  719.5 49.8 %all-gather.11.cloned.1.call-done = bf16[1024,1,2048]{2,0,1:T(8,128)(2,1)} async-done(((bf16[128,1,2048]{2,0,1:T(8,128)(2,1)}), bf16[1024,1,2048]{2,0,1:T(8,128)(2,1)}) %all-gather.11.cloned.1.call-update) | async-done | bytes 4194320 | tf_op jit(solution)/shard_map/all_gather | solution.py:199
  775.6 21.6 %while.31 = (s32[]{:T(128)}, f32[2,1024,128]{2,1,0:T(8,128)S(1)}, f32[2,1024,128]{2,1,0:T(8,128)}, f32[2,2,512,128]{3,2,1,0:T(8,128)}, s32[2]{0:T(128)S(1)}, /*i...) while((s32[]{:T(128)}, f32[2,1024,128]{2,1,0:T(8,128)S(1)}, ...), condition=%wide.region_18.19_spmd.clone.clone, body=%wide.region_16.18_spmd.clone.clone.sunk | while | flops 1359480320 | bytes 61911392 | solution.py:234
  817.5 6.9 fusion.74
  824.5 52.0 %psum.31 = bf16[2048,4,1]{0,1,2:T(4,128)(2,1)S(1)} all-reduce(bf16[2048,4,1]{0,1,2:T(4,128)(2,1)S(1)} %maximum_bitcast_fusion), channel_id=1, replica_groups=mesh['dp'=16,'seq'=8] {'dp'}, use_global_device_ids=true, to_apply=%region_27.28 | all-reduce | flops 8192 | bytes 32768 | tf_op jit(solution)/shard_map/psum | solution.py:260
  878.0 11.5 reduce.21
  894.4 80.6 %all-reduce.4.cloned.1.call-done = (bf16[2048,3,256]{0,2,1:T(8,128)(2,1)}, bf16[256,2048]{1,0:T(8,128)(2,1)}, bf16[2048,3,683]{0,2,1:T(8,128)(2,1)}) async-done(((bf16[2048,3,256]{0,2,1:T(8,128)(2,1)}, bf16[256,2048]{1,0:T(8,128)(2,1)}, bf16[2048,3,683]{0,2,1:T(8,128)(2,1)}), (bf16[2048,3,256]{0,2,1:T(8,128)(2,1)}, bf16[256,2048]{1,0:T(8,128)(2,1)}, ...) | async-done | bytes 12587024 | tf_op jit(solution)/shard_map/psum | solution.py:257
  975.1 19.1 %copy.112 = bf16[2048,3,683]{2,1,0:T(4,128)(2,1)} copy(bf16[2048,3,683]{0,2,1:T(8,128)(2,1)} %get-tuple-element.412) | data formatting | bytes 16785408 | tf_op jit(solution)/shard_map/psum | solution.py:259
  994.1 6.9 all-to-all-start.1
  1004.6 188.4 %reduce-scatter.11.cloned.1.call-done = bf16[128,1,2048]{2,0,1:T(8,128)(2,1)} async-done(((bf16[1024,1,2048]{2,0,1:T(8,128)(2,1)}), bf16[128,1,2048]{2,0,1:T(8,128)(2,1)}) %reduce-scatter.11.cloned.1.call-update) | async-done | bytes 524304 | tf_op jit(solution)/shard_map/reduce_scatter | solution.py:246
  1203.5 21.3 %copy.113 = f32[8,256,3,683]{1,3,0,2:T(8,128)} copy(bf16[8,256,3,683]{3,2,1,0:T(4,128)(2,1)} %bitcast.83) | data formatting | bytes 25178112 | tf_op jit(solution)/shard_map/convert_element_type | solution.py:265
  1224.8 17.2 %reshape.719 = f32[256,3,5464]{0,2,1:T(8,128)} reshape(f32[256,3,8,683]{0,3,2,1:T(8,128)} %bitcast.334) | data formatting | bytes 33570816 | tf_op jit(solution)/shard_map/convert_element_type | solution.py:265
  1247.4 9.1 slice.105
  1256.6 29.9 %copy.117 = f32[256,2,5461]{0,1,2:T(2,128)} copy(f32[256,2,5461]{0,2,1:T(8,128)} %slice.105) | data formatting | bytes 22368256
  (239 shorter events, 155.8 us)
Async XLA Ops:
  7.2 110.7 %copy-start = (bf16[256,2048]{1,0:T(8,128)(2,1)S(1)}, bf16[256,2048]{1,0:T(8,128)(2,1)}, u32[]{:S(2)}) copy-start(bf16[256,2048]{1,0:T(8,128)(2,1)} %param.19) | copy-start | bytes 3145732
  7.2 77.7 %all-gather.5.cloned.1.call-start = ((), (), s32[]{:S(2)}) async-start(), calls=%async_computation.7 | async-start | bytes 4718592 | tf_op jit(solution)/shard_map/all_gather | solution.py:93
  7.9 302.5 %reduce-scatter.5.cloned.1.call-start = ((), (), s32[]{:S(2)}) async-start(), calls=%async_computation.8 | async-start | bytes 4718592 | tf_op jit(solution)/shard_map/reduce_scatter | solution.py:149
  14.6 81.7 %copy-start.12 = (f32[1024,128]{0,1:T(8,128)}, f32[1024,128]{0,1:T(8,128)S(1)}, u32[]{:S(2)}) copy-start(f32[1024,128]{0,1:T(8,128)S(1)} %get-tuple-element.441) | copy-start | bytes 1572868
  14.6 81.7 %copy-start.14 = (f32[1024,128]{0,1:T(8,128)}, f32[1024,128]{0,1:T(8,128)S(1)}, u32[]{:S(2)}) copy-start(f32[1024,128]{0,1:T(8,128)S(1)} %get-tuple-element.446) | copy-start | bytes 1572868
  116.4 4.8 copy-start.5
  163.3 147.1 %copy-start.3 = (bf16[128,1,2048]{2,0,1:T(8,128)(2,1)S(1)}, bf16[128,1,2048]{2,0,1:T(8,128)(2,1)}, u32[]{:S(2)}) copy-start(bf16[128,1,2048]{2,0,1:T(8,128)(2,1)} %param.16) | copy-start | bytes 1572868
  163.3 149.8 %copy-start.34 = (f32[2048]{0:T(1024)S(1)}, f32[2048]{0:T(1024)}, u32[]{:S(2)}) copy-start(f32[2048]{0:T(1024)} %param.22) | copy-start | bytes 24580
  163.3 149.8 %copy-start.35 = (f32[2048]{0:T(1024)S(1)}, f32[2048]{0:T(1024)}, u32[]{:S(2)}) copy-start(f32[2048]{0:T(1024)} %param.23) | copy-start | bytes 24580
  163.3 166.3 %all-to-all-start = ((bf16[256,3,5464]{0,1,2:T(4,128)(2,1)}), bf16[256,3,5464]{0,1,2:T(4,128)(2,1)}, u32[]{:S(2)}, u32[]{:S(2)}) async-start(bf16[256,3,5464]{0,1,2:T(4,128)(2,1)} %fusion.46), calls=%async_computation.1 | async-start | bytes 22380544 | tf_op jit(solution)/shard_map/all_to_all | solution.py:90
  168.7 235.2 %all-gather.7.cloned.1.call-start = ((), (), s32[]{:S(2)}) async-start(), calls=%async_computation.9 | async-start | bytes 4718592 | tf_op jit(solution)/shard_map/all_gather | solution.py:160
  315.3 194.4 %reduce-scatter.7.cloned.1.call-start = ((), (), s32[]{:S(2)}) async-start(), calls=%async_computation.10 | async-start | bytes 4718592 | tf_op jit(solution)/shard_map/reduce_scatter | solution.py:164
  413.2 6.3 copy-start.2
  427.5 82.3 %copy-start.4 = (bf16[128,1,2048]{2,0,1:T(8,128)(2,1)S(1)}, bf16[128,1,2048]{2,0,1:T(8,128)(2,1)}, u32[]{:S(2)}) copy-start(bf16[128,1,2048]{2,0,1:T(8,128)(2,1)} %reduce-scatter.5.cloned.1.call-done) | copy-start | bytes 1572868
  427.5 84.2 %copy-start.36 = (f32[2048]{0:T(1024)S(1)}, f32[2048]{0:T(1024)}, u32[]{:S(2)}) copy-start(f32[2048]{0:T(1024)} %param.24) | copy-start | bytes 24580
  427.5 84.7 %copy-start.37 = (f32[2048]{0:T(1024)S(1)}, f32[2048]{0:T(1024)}, u32[]{:S(2)}) copy-start(f32[2048]{0:T(1024)} %param.25) | copy-start | bytes 24580
  427.5 157.6 %all-gather.9.cloned.1.call-start = ((), (), s32[]{:S(2)}) async-start(), calls=%async_computation.11 | async-start | bytes 4718592 | tf_op jit(solution)/shard_map/all_gather | solution.py:176
  514.1 180.1 %reduce-scatter.9.cloned.1.call-start = ((), (), s32[]{:S(2)}) async-start(), calls=%async_computation.12 | async-start | bytes 4718592 | tf_op jit(solution)/shard_map/reduce_scatter | solution.py:188
  590.9 12.8 slice-start
  590.9 12.7 slice-start.1
  612.1 157.2 %all-gather.11.cloned.1.call-start = ((), (), s32[]{:S(2)}) async-start(), calls=%async_computation.13 | async-start | bytes 4718592 | tf_op jit(solution)/shard_map/all_gather | solution.py:199
  698.3 276.8 %all-reduce.4.cloned.1.call-start = ((), (), s32[]{:S(2)}) async-start(), calls=%async_computation.15 | async-start | bytes 25296896 | tf_op jit(solution)/shard_map/psum | solution.py:257
  698.7 5.9 copy-start.23
  698.7 5.9 copy-start.25
  698.8 5.9 copy-start.39
  807.8 4.6 copy-start.31
  807.8 4.6 copy-start.38
  817.4 375.6 %reduce-scatter.11.cloned.1.call-start = ((), (), s32[]{:S(2)}) async-start(), calls=%async_computation.14 | async-start | bytes 4718592 | tf_op jit(solution)/shard_map/reduce_scatter | solution.py:246
  890.9 103.2 %all-to-all-start.2 = ((bf16[8,2,512]{2,1,0:T(2,128)(2,1)}), bf16[8,2,512]{2,1,0:T(2,128)(2,1)S(1)}, u32[]{:S(2)}, u32[]{:S(2)}) async-start(bf16[8,2,512]{2,1,0:T(2,128)(2,1)} %reshape.731), calls=%async_computation.6 | async-start | bytes 32768 | tf_op jit(solution)/shard_map/all_to_all | solution.py:266
  994.1 209.4 %all-to-all-start.1 = ((bf16[2048,3,683]{2,1,0:T(4,128)(2,1)}), bf16[2048,3,683]{2,1,0:T(4,128)(2,1)}, u32[]{:S(2)}, u32[]{:S(2)}) async-start(bf16[2048,3,683]{2,1,0:T(4,128)(2,1)} %copy.112), calls=%async_computation.5 | async-start | bytes 25165824 | tf_op jit(solution)/shard_map/all_to_all | solution.py:263
  1003.7 192.9 %copy-start.26 = (bf16[256,2048]{1,0:T(8,128)(2,1)S(1)}, bf16[256,2048]{1,0:T(8,128)(2,1)}, u32[]{:S(2)}) copy-start(bf16[256,2048]{1,0:T(8,128)(2,1)} %get-tuple-element.411) | copy-start | bytes 3145732
  1256.6 29.9 %copy-start.1 = (bf16[256,2048]{1,0:T(8,128)(2,1)S(1)}, bf16[256,2048]{1,0:T(8,128)(2,1)}, u32[]{:S(2)}) copy-start(bf16[256,2048]{1,0:T(8,128)(2,1)} %param.19) | copy-start | bytes 3145732
  (32 other events, 58.8 us)
Sparse Core Ops, SparseCore 0:
  10.4 74.4 all-gather.4
  121.3 189.0 reduce-scatter.4
  315.5 88.4 all-gather.6
  427.6 82.1 reduce-scatter.6
  514.2 70.8 all-gather.8
  612.2 81.9 reduce-scatter.8
  698.4 70.8 all-gather.10
  817.6 157.4 all-reduce.3
  979.5 213.4 reduce-scatter.10
where the time goes:
time: 1300 us; the launch traced here: 1290 us
  waiting for transfers between devices  834 us (64%)
  local copies, waits for them, and re-layouts  185 us (14%)
  other arithmetic  97.4 us (7%)
  matrix products  91.8 us (7%)
  blocking collectives  52 us (4%)
  starting transfers between devices  16.8 us (1%)
  between operations  15.6 us (1%)
    reduce_scatter x1, waiting for transfers between devices, on_device(): lax.psum_scatter(jnp.einsum('tsch,dch->tsd', piece_rows, w_qkv, preferred...  188 us
    reduce_scatter x1, waiting for transfers between devices, on_device(): lax.psum_scatter(jnp.einsum('tsh,hd->tsd', piece_rows, w_out, preferred_e...  142 us
    reduce_scatter x1, waiting for transfers between devices, on_device(): lax.psum_scatter(jnp.einsum('tscf,dcf->tsd', piece_rows, gate_up_w, prefe...  82.1 us
    psum x1, waiting for transfers between devices, on_device(): lax.psum(qkv_grad.astype(jnp.bfloat16), 'dp').astype(jnp.float32)  80.6 us
    reduce_scatter x1, waiting for transfers between devices, on_device(): lax.psum_scatter(jnp.einsum('tsf,df->tsd', piece_rows, down_cols, preferr...  79.1 us
    all_gather x1, waiting for transfers between devices, on_device(): lax.all_gather(grad_z2.astype(jnp.bfloat16), 'seq', axis=0, tiled=True)  71 us
    all_gather x1, waiting for transfers between devices, on_device(): tokens_all = lax.all_gather(tokens, 'seq', axis=0, tiled=True)  70.2 us
    all_gather x1, waiting for transfers between devices, on_device(): lax.all_gather(normed.astype(jnp.bfloat16), 'seq', axis=0, tiled=True)  55.7 us
  transfers between devices with their start and end apart: 12, of which 10 were waited for; matrix products, arithmetic and copies ran while one was open for 11% of the time, Pallas kernels for 0%

commit v1 on v0

v1 whole, which is shorter than its diff:
```python
import functools

import jax
import jax.numpy as jnp
import numpy as np
from jax import lax
from jax.experimental import pallas as pl
from jax.experimental.pallas import tpu as pltpu
from jax.sharding import PartitionSpec as P

MESH = pl.DeviceIdType.MESH
F32, BF16 = jnp.float32, jnp.bfloat16
HEAD_DIM = 128
ROWS = 128
WIDE = 2048
COLS = 768
LEN = 1024
VMEM_BYTES = 60 * 1024 * 1024
deep_alpha = 48.0**0.25
norm_eps = 1e-05
rotary_base = 10000.0

ORDER = (0, 1, 2, 3, 4, 5, 6, 7)


def rotary_tables(length, head_width):
    half_width = head_width // 2
    position = np.arange(length, dtype=np.float64)
    inverse = rotary_base ** (-np.arange(half_width, dtype=np.float64) * 2.0 / head_width)
    angles = position[:, None] * inverse[None, :]
    cosine_table = np.cos(angles)
    sine_table = np.sin(angles)
    return (
        np.concatenate([cosine_table, cosine_table], axis=1).astype(np.float32),
        np.concatenate([-sine_table, sine_table], axis=1).astype(np.float32),
    )


class Links:
    def __init__(self, send, recv):
        self.send, self.recv, self.count = send, recv, 0
        dp, seq = lax.axis_index("dp"), lax.axis_index("seq")
        y, z_hi = seq // 2, seq % 2
        self.y, self.z_hi = y, z_hi
        self.up = (dp, lax.rem(y + 1, 4) * 2 + z_hi)
        self.down = (dp, lax.rem(y + 3, 4) * 2 + z_hi)
        self.across = (dp, y * 2 + 1 - z_hi)

    def barrier(self):
        gate = pltpu.get_barrier_semaphore()
        for where in (self.up, self.down, self.across):
            pl.semaphore_signal(gate, inc=1, device_id=where, device_id_type=MESH)
        pl.semaphore_wait(gate, 3)

    def start(self, src, dst, where):
        copy = pltpu.make_async_remote_copy(
            src_ref=src,
            dst_ref=dst,
            send_sem=self.send.at[self.count],
            recv_sem=self.recv.at[self.count],
            device_id=where,
            device_id_type=MESH,
        )
        self.count += 1
        copy.start()
        return copy

    def first_row(self, slot):
        step = (0, 3, 1, 2)[slot % 4]
        half = self.z_hi if slot < 4 else 1 - self.z_hi
        return pl.multiple_of((lax.rem(self.y + step, 4) * 2 + half) * ROWS, ROWS)


A, B = pl.ds(0, 80), pl.ds(80, 48)
A0, A1 = pl.ds(0, 48), pl.ds(48, 32)
B0, B1 = pl.ds(80, 16), pl.ds(96, 32)
GATHER_COPIES = 22
SCATTER_COPIES = 19


def gather(links, buf, work):
    go, up, down, across = links.start, links.up, links.down, links.across
    sent = []

    def send(src, dst, where):
        copy = go(buf.at[src[0], src[1]], buf.at[dst, src[1]], where)
        sent.append(copy)
        return copy

    u_a = send((0, A), 1, up)
    d_a = send((0, A), 2, down)
    z_a = send((0, A), 4, across)
    u_b = send((0, B), 1, up)
    d_b = send((0, B), 2, down)
    z_b = send((0, B), 4, across)
    u_a.wait_recv()
    u_a2 = send((1, A0), 3, up)
    d_a.wait_recv()
    d_a2 = send((2, A1), 3, down)
    z_a.wait_recv()
    u_p = send((4, A), 5, up)
    d_p = send((4, A), 6, down)
    u_b.wait_recv()
    z_b1 = send((1, B), 5, across)
    u_b2 = send((1, B0), 3, up)
    d_b.wait_recv()
    z_b2 = send((2, B), 6, across)
    d_b2 = send((2, B1), 3, down)
    work((0, 1))
    u_a2.wait_recv()
    d_a2.wait_recv()
    u_p.wait_recv()
    u_p2 = send((5, A0), 7, up)
    d_p.wait_recv()
    d_p2 = send((6, A1), 7, down)
    u_b2.wait_recv()
    z_b3 = send((3, B0), 7, across)
    d_b2.wait_recv()
    z_b4 = send((3, B1), 7, across)
    work((2, 3))
    z_b.wait_recv()
    z_b1.wait_recv()
    work((4, 5))
    z_b2.wait_recv()
    u_p2.wait_recv()
    d_p2.wait_recv()
    z_b3.wait_recv()
    z_b4.wait_recv()
    work((6, 7))
    for copy in sent:
        copy.wait_send()


def add_into(target, at, other, other_at):
    target[at] = (target[at].astype(F32) + other[other_at].astype(F32)).astype(BF16)


SCATTER_SCRATCH = (
    pltpu.VMEM((8, ROWS, WIDE), BF16),
    pltpu.VMEM((4, 48, WIDE), BF16),
    pltpu.VMEM((48, WIDE), BF16),
    pltpu.VMEM((2, 48, WIDE), BF16),
    pltpu.VMEM((2, 80, WIDE), BF16),
    pltpu.VMEM((2, 2, 80, WIDE), BF16),
    pltpu.VMEM((80, WIDE), BF16),
)


def scatter(links, bufs, compute, total):
    sums, from_z, b_far, b_near, a_far, a_near, a_z = bufs
    go, up, down, across = links.start, links.up, links.down, links.across
    sent = []

    def send(src, dst, where):
        copy = go(src, dst, where)
        sent.append(copy)
        return copy

    def far_a(o):
        half = o // 4
        return (
            send(sums.at[o + 3, A0], a_far.at[half, pl.ds(0, 48)], up),
            send(sums.at[o + 3, A1], a_far.at[half, pl.ds(48, 32)], down),
        )

    def near_a(o, far):
        half = o // 4
        far[0].wait_recv()
        sums[o + 2, 0:48] = (
            sums[o + 2, 0:48].astype(F32) + a_far[half, 0:48].astype(F32)
        ).astype(BF16)
        one = send(sums.at[o + 2, A], a_near.at[half, 0], up)
        far[1].wait_recv()
        sums[o + 1, 48:80] = (
            sums[o + 1, 48:80].astype(F32) + a_far[half, 48:80].astype(F32)
        ).astype(BF16)
        two = send(sums.at[o + 1, A], a_near.at[half, 1], down)
        return one, two

    def cross_b(j):
        return send(sums.at[4 + j, B], from_z.at[j], across)

    def take_b(j, copy):
        copy.wait_recv()
        sums[j, 80:128] = (sums[j, 80:128].astype(F32) + from_z[j].astype(F32)).astype(BF16)

    compute((7, 3))
    z3 = cross_b(3)
    far_other = far_a(4)
    far_own = far_a(0)
    compute((5, 6))
    z1 = cross_b(1)
    z2 = cross_b(2)
    compute((1, 2))
    take_b(3, z3)
    far_b = (
        send(sums.at[3, B0], b_far.at[pl.ds(0, 16)], up),
        send(sums.at[3, B1], b_far.at[pl.ds(16, 32)], down),
    )
    near_other = near_a(4, far_other)
    compute((4, 0))
    z0 = cross_b(0)
    near_own = near_a(0, far_own)
    for copy in near_other:
        copy.wait_recv()
    sums[4, 0:80] = (
        sums[4, 0:80].astype(F32) + a_near[1, 0].astype(F32) + a_near[1, 1].astype(F32)
    ).astype(BF16)
    z_a = send(sums.at[4, A], a_z, across)
    take_b(2, z2)
    far_b[0].wait_recv()
    sums[2, 80:96] = (sums[2, 80:96].astype(F32) + b_far[0:16].astype(F32)).astype(BF16)
    near_b0 = send(sums.at[2, B], b_near.at[0], up)
    take_b(1, z1)
    far_b[1].wait_recv()
    sums[1, 96:128] = (sums[1, 96:128].astype(F32) + b_far[16:48].astype(F32)).astype(BF16)
    near_b1 = send(sums.at[1, B], b_near.at[1], down)
    z0.wait_recv()
    near_b0.wait_recv()
    near_b1.wait_recv()
    total[80:128] = (
        sums[0, 80:128].astype(F32)
        + from_z[0].astype(F32)
        + b_near[0].astype(F32)
        + b_near[1].astype(F32)
    )
    for copy in near_own:
        copy.wait_recv()
    z_a.wait_recv()
    total[0:80] = (
        sums[0, 0:80].astype(F32)
        + a_near[0, 0].astype(F32)
        + a_near[0, 1].astype(F32)
        + a_z[...].astype(F32)
    )
    for copy in sent:
        copy.wait_send()


def dot(a, b):
    return jnp.dot(a, b, preferred_element_type=F32)


def dot_t(a, b):
    return lax.dot_general(a, b, (((1,), (1,)), ((), ())), preferred_element_type=F32)


def dot_rows(a, b):
    return lax.dot_general(a, b, (((0,), (0,)), ((), ())), preferred_element_type=F32)


def pair_of(ref, pair):
    return jnp.concatenate([ref[pair[0]], ref[pair[1]]], axis=0)


def by_chunks(body):
    def step(i, carry):
        body(pl.ds(pl.multiple_of(i * 16, 16), 16))
        return carry

    lax.fori_loop(0, ROWS // 16, step, 0)


def norm_parts(row_total):
    center = row_total - jnp.mean(row_total, axis=-1, keepdims=True)
    spread = jnp.mean(center * center, axis=-1, keepdims=True)
    inverse = lax.rsqrt(spread + norm_eps)
    return center * inverse, inverse


def norm_backward(grad_result, unit, inverse, gain):
    grad_unit = grad_result * gain
    return inverse * (
        grad_unit
        - jnp.mean(grad_unit, axis=-1, keepdims=True)
        - unit * jnp.mean(grad_unit * unit, axis=-1, keepdims=True)
    )


def rows8(values):
    return values[0:8] + values[8:16]


def call(body, name, ident, outs, operands, spaces, scratch, copies, flops=0):
    vmem = pl.BlockSpec(memory_space=pltpu.VMEM)
    kinds = {"v": vmem, "s": pl.BlockSpec(memory_space=pltpu.SMEM), "h": pl.BlockSpec(memory_space=pl.ANY)}
    sems = [pltpu.SemaphoreType.DMA((copies,)), pltpu.SemaphoreType.DMA((copies,))]
    return pl.pallas_call(
        body,
        name=name,
        out_shape=tuple(jax.ShapeDtypeStruct(s, d) for s, d in outs),
        in_specs=[kinds[k] for k in spaces],
        out_specs=tuple(vmem for _ in outs),
        scratch_shapes=[*scratch, *sems],
        compiler_params=pltpu.CompilerParams(
            collective_id=ident, has_side_effects=True, vmem_limit_bytes=VMEM_BYTES
        ),
        cost_estimate=pl.CostEstimate(flops=flops, bytes_accessed=20_000_000, transcendentals=0),
    )(*operands)


def project_kernel(x_ref, w_ref, cos_ref, sin_ref, all_ref, q_ref, k_ref, v_ref, send, recv):
    links = Links(send, recv)
    all_ref[0] = x_ref[...]
    links.barrier()

    def work(pair):
        rows = pair_of(all_ref, pair)
        for part, out in enumerate((q_ref, k_ref, v_ref)):
            result = dot(rows, w_ref[:, part * 256 : part * 256 + 256])
            for i, slot in enumerate(pair):
                at = pl.ds(links.first_row(slot), ROWS)
                piece = result[i * ROWS : (i + 1) * ROWS]
                if part == 2:
                    out[at] = piece.astype(BF16)
                    continue
                cosine, sine = cos_ref[at], sin_ref[at]
                for head in range(2):
                    lanes = slice(head * 128, head * 128 + 128)
                    turned = piece[:, lanes] * cosine + pltpu.roll(piece[:, lanes], 64, 1) * sine
                    if part == 0:
                        turned = turned * HEAD_DIM**-0.5
                    out[at, lanes] = turned.astype(BF16)

    gather(links, all_ref, work)


def attend_kernel(prefix_ref, q_ref, k_ref, v_ref, out_ref, lse_ref):
    block = q_ref.shape[0]
    first = pl.program_id(1) * block
    scores = dot_t(k_ref[...], q_ref[...])
    key = lax.broadcasted_iota(jnp.int32, scores.shape, 0)
    query = lax.broadcasted_iota(jnp.int32, (1, block), 1) + first
    limit = jnp.maximum(query, prefix_ref[0] - 1)
    scores = jnp.where(key <= limit, scores, -1e30)
    peak = jnp.max(scores, axis=0, keepdims=True)
    exponent = jnp.exp(scores - peak)
    total = jnp.sum(exponent, axis=0, keepdims=True)
    weights = (exponent * (1.0 / total)).astype(BF16)
    out_ref[...] = dot_rows(weights, v_ref[...]).astype(BF16)
    lse_ref[0] = peak + jnp.log(total)


def attend(prefix, q, k, v):
    block = 512
    return pl.pallas_call(
        attend_kernel,
        name="attend",
        grid=(2, LEN // block),
        in_specs=[
            pl.BlockSpec(memory_space=pltpu.SMEM),
            pl.BlockSpec((block, 128), lambda h, b: (b, h)),
            pl.BlockSpec((LEN, 128), lambda h, b: (0, h)),
            pl.BlockSpec((LEN, 128), lambda h, b: (0, h)),
        ],
        out_specs=(
            pl.BlockSpec((block, 128), lambda h, b: (b, h)),
            pl.BlockSpec((1, 1, block), lambda h, b: (h, 0, b)),
        ),
        out_shape=(
            jax.ShapeDtypeStruct((LEN, 256), BF16),
            jax.ShapeDtypeStruct((2, 1, LEN), F32),
        ),
        compiler_params=pltpu.CompilerParams(vmem_limit_bytes=VMEM_BYTES),
    )(prefix, q, k, v)


def attend_back_kernel(
    prefix_ref, q_ref, k_ref, v_ref, g_ref, lse_ref, cos_ref, sin_ref, cosq_ref, sinq_ref,
    dq_ref, dk_ref, dv_ref, dk_sum, dv_sum
):
    block = q_ref.shape[0]
    step = pl.program_id(1)
    scores = dot_t(k_ref[...], q_ref[...])
    key = lax.broadcasted_iota(jnp.int32, scores.shape, 0)
    query = lax.broadcasted_iota(jnp.int32, (1, block), 1) + step * block
    limit = jnp.maximum(query, prefix_ref[0] - 1)
    weights = jnp.where(key <= limit, jnp.exp(scores - lse_ref[0]), 0.0)
    grad_weights = dot_t(v_ref[...], g_ref[...])
    inner = jnp.sum(weights * grad_weights, axis=0, keepdims=True)
    grad_scores = (weights * (grad_weights - inner)).astype(BF16)
    d_query = dot_rows(grad_scores, k_ref[...]) * HEAD_DIM**-0.5
    dq_ref[...] = (d_query * cosq_ref[...] - pltpu.roll(d_query, 64, 1) * sinq_ref[...]).astype(BF16)
    d_key = dot(grad_scores, q_ref[...])
    d_value = dot(weights.astype(BF16), g_ref[...])

    @pl.when(step == 0)
    def _():
        dk_sum[...] = d_key
        dv_sum[...] = d_value

    @pl.when(step > 0)
    def _():
        dk_sum[...] += d_key
        dv_sum[...] += d_value

    @pl.when(step == pl.num_programs(1) - 1)
    def _():
        total = dk_sum[...]
        dk_ref[...] = (total * cos_ref[...] - pltpu.roll(total, 64, 1) * sin_ref[...]).astype(BF16)
        dv_ref[...] = dv_sum[...].astype(BF16)


def attend_back(prefix, q, k, v, g, lse, cosine, sine):
    block = 512
    part = pl.BlockSpec((block, 128), lambda h, b: (b, h))
    whole = pl.BlockSpec((LEN, 128), lambda h, b: (0, h))
    table = pl.BlockSpec((LEN, 128), lambda h, b: (0, 0))
    table_part = pl.BlockSpec((block, 128), lambda h, b: (b, 0))
    return pl.pallas_call(
        attend_back_kernel,
        name="attend_back",
        grid=(2, LEN // block),
        in_specs=[
            pl.BlockSpec(memory_space=pltpu.SMEM), part, whole, whole, part,
            pl.BlockSpec((1, 1, block), lambda h, b: (h, 0, b)),
            table, table, table_part, table_part,
        ],
        out_specs=(part, whole, whole),
        out_shape=tuple(jax.ShapeDtypeStruct((LEN, 256), BF16) for _ in range(3)),
        scratch_shapes=[pltpu.VMEM((LEN, 128), F32), pltpu.VMEM((LEN, 128), F32)],
        compiler_params=pltpu.CompilerParams(vmem_limit_bytes=VMEM_BYTES),
    )(prefix, q, k, v, g, lse, cosine, sine, cosine, sine)


def attended_kernel(
    heads_ref, w_ref, x_ref, gain_ref, bias_ref, normed_ref, unit_ref, inverse_ref, total, *rest
):
    bufs, (send, recv) = rest[:7], rest[7:]
    links = Links(send, recv)
    links.barrier()

    def compute(pair):
        rows = jnp.concatenate([heads_ref[pl.ds(links.first_row(s), ROWS)] for s in pair], axis=0)
        result = dot(rows, w_ref[...]).astype(BF16)
        for i, slot in enumerate(pair):
            bufs[0][slot] = result[i * ROWS : (i + 1) * ROWS]

    scatter(links, bufs, compute, total)

    def finish(at):
        unit, inverse = norm_parts(deep_alpha * x_ref[at].astype(F32) + total[at])
        unit_ref[at] = unit
        inverse_ref[at] = jnp.broadcast_to(inverse, (16, 128))
        normed_ref[at] = unit * gain_ref[...] + bias_ref[...]

    by_chunks(finish)


def load_weights(w_hbm, w_vmem, sem, parts):
    copies = [
        pltpu.make_async_copy(
            w_hbm.at[d, pl.ds(0, parts)], w_vmem.at[:, :, pl.ds(d * 16, 16)], sem.at[d]
        )
        for d in range(16)
    ]
    for copy in copies:
        copy.start()
    return copies


def feed_kernel(
    normed_ref, cot_ref, weight_ref, w_hbm, gain_ref, bias_ref,
    out_ref, all_ref, hidden_ref, gz_all_ref, ggu_ref, gz_ref, vec_ref,
    w, act, slope, total, w_sem, *rest,
):
    bufs, (send, recv) = rest[:7], rest[7:]
    links = Links(send, recv)
    loads = load_weights(w_hbm, w, w_sem, 3)

    def to_low(at):
        all_ref[0, at] = normed_ref[at].astype(BF16)

    by_chunks(to_low)
    links.barrier()
    for copy in loads:
        copy.wait()

    def forward(pair):
        rows = pair_of(all_ref, pair)
        for c in range(0, COLS, 256):
            cols = slice(c, c + 256)
            gate = dot(rows, w[0, :, :, cols].reshape(WIDE, 256))
            up = dot(rows, w[1, :, :, cols].reshape(WIDE, 256))
            bell = 0.5 + 0.5 * lax.erf(gate * np.float32(np.sqrt(0.5)))
            gelu = gate * bell
            turn = bell + gate * (jnp.exp(-0.5 * gate * gate) * np.float32(1.0 / np.sqrt(2.0 * np.pi)))
            hidden = (gelu * up).astype(BF16)
            turn = turn * up
            for i, slot in enumerate(pair):
                part = slice(i * ROWS, (i + 1) * ROWS)
                act[slot, :, cols] = gelu[part]
                slope[slot, :, cols] = turn[part]
                hidden_ref[slot, :, cols] = hidden[part]

    gather(links, all_ref, forward)

    def compute(pair):
        rows = pair_of(hidden_ref, pair)
        for d in range(8):
            result = dot_t(rows, w[2, d]).astype(BF16)
            for i, slot in enumerate(pair):
                bufs[0][slot, :, d * 256 : d * 256 + 256] = result[i * ROWS : (i + 1) * ROWS]

    scatter(links, bufs, compute, total)
    vec_ref[...] = jnp.zeros_like(vec_ref)

    def finish(at):
        unit, inverse = norm_parts(deep_alpha * normed_ref[at] + total[at])
        out_ref[at] = (unit * gain_ref[...] + bias_ref[...]).astype(BF16)
        grad = cot_ref[at].astype(F32) * weight_ref[0]
        grad_z = norm_backward(grad, unit, inverse, gain_ref[...])
        gz_ref[at] = grad_z
        gz_all_ref[0, at] = grad_z.astype(BF16)
        vec_ref[0] += rows8(grad * unit)
        vec_ref[1] += rows8(grad)

    by_chunks(finish)

    def backward(pair):
        rows = pair_of(gz_all_ref, pair)
        for c in range(0, COLS, 256):
            cols = slice(c, c + 256)
            grad_hidden = dot(rows, w[2, :, :, cols].reshape(WIDE, 256))
            for i, slot in enumerate(pair):
                part = grad_hidden[i * ROWS : (i + 1) * ROWS]
                ggu_ref[slot, :, cols] = (part * slope[slot, :, cols]).astype(BF16)
                ggu_ref[slot, :, COLS + c : COLS + c + 256] = (part * act[slot, :, cols]).astype(BF16)

    gather(links, gz_all_ref, backward)


def feed_back_kernel(
    ggu_ref, gz_ref, w_hbm, unit_ref, inverse_ref, gain_ref, w_out_ref,
    gz1_ref, all_ref, grad_heads_ref, vec_ref,
    w, total, w_sem, *rest,
):
    bufs, (send, recv) = rest[:7], rest[7:]
    links = Links(send, recv)
    loads = load_weights(w_hbm, w, w_sem, 2)
    links.barrier()
    for copy in loads:
        copy.wait()

    def compute(pair):
        rows = pair_of(ggu_ref, pair)
        for d in range(8):
            result = dot_t(rows[:, :COLS], w[0, d]) + dot_t(rows[:, COLS:], w[1, d])
            result = result.astype(BF16)
            for i, slot in enumerate(pair):
                bufs[0][slot, :, d * 256 : d * 256 + 256] = result[i * ROWS : (i + 1) * ROWS]

    scatter(links, bufs, compute, total)
    vec_ref[...] = jnp.zeros_like(vec_ref)

    def finish(at):
        grad = deep_alpha * gz_ref[at] + total[at]
        unit = unit_ref[at]
        grad_z = norm_backward(grad, unit, inverse_ref[at][:, 0:1], gain_ref[...])
        gz1_ref[at] = grad_z
        all_ref[0, at] = grad_z.astype(BF16)
        vec_ref[0] += rows8(grad * unit)
        vec_ref[1] += rows8(grad)

    by_chunks(finish)

    def work(pair):
        result = dot_t(pair_of(all_ref, pair), w_out_ref[...]).astype(BF16)
        for i, slot in enumerate(pair):
            grad_heads_ref[pl.ds(links.first_row(slot), ROWS)] = result[i * ROWS : (i + 1) * ROWS]

    gather(links, all_ref, work)


def input_kernel(dq_ref, dk_ref, dv_ref, w_ref, gz1_ref, out_ref, total, *rest):
    bufs, (send, recv) = rest[:7], rest[7:]
    links = Links(send, recv)
    links.barrier()

    def compute(pair):
        result = 0.0
        for part, ref in enumerate((dq_ref, dk_ref, dv_ref)):
            rows = jnp.concatenate([ref[pl.ds(links.first_row(s), ROWS)] for s in pair], axis=0)
            result = result + dot_t(rows, w_ref[:, part * 256 : part * 256 + 256])
        result = result.astype(BF16)
        for i, slot in enumerate(pair):
            bufs[0][slot] = result[i * ROWS : (i + 1) * ROWS]

    scatter(links, bufs, compute, total)

    def finish(at):
        out_ref[at] = deep_alpha * gz1_ref[at] + total[at]

    by_chunks(finish)


def feed_weight_kernel(normed_ref, gz_ref, ggu_ref, hidden_ref, out_ref):
    gate_up = dot_rows(normed_ref[...], ggu_ref[...]).astype(BF16)
    down = dot_rows(gz_ref[...], hidden_ref[...]).astype(BF16)
    out_ref[:, 0, 0] = gate_up[:, :COLS].reshape(16, 16, COLS)
    out_ref[:, 1, 0] = gate_up[:, COLS:].reshape(16, 16, COLS)
    out_ref[:, 2, 0] = down.reshape(16, 16, COLS)


def feed_weights(normed_all, gz_all, ggu, hidden):
    flat = lambda v: v.reshape(LEN, v.shape[-1])
    lhs = pl.BlockSpec((LEN, 256), lambda s: (0, s))
    return pl.pallas_call(
        feed_weight_kernel,
        name="feed_weights",
        grid=(8,),
        in_specs=[
            lhs,
            lhs,
            pl.BlockSpec((LEN, 2 * COLS), lambda s: (0, 0)),
            pl.BlockSpec((LEN, COLS), lambda s: (0, 0)),
        ],
        out_specs=pl.BlockSpec((16, 3, 1, 16, COLS), lambda s: (0, 0, s, 0, 0)),
        out_shape=jax.ShapeDtypeStruct((16, 3, 8, 16, COLS), BF16),
        compiler_params=pltpu.CompilerParams(vmem_limit_bytes=VMEM_BYTES),
    )(flat(normed_all), flat(gz_all), flat(ggu), flat(hidden))


def in_order(values):
    seq = lax.axis_index("seq")
    y, z_hi = seq // 2, seq % 2
    place = jnp.array([0, 2, 3, 1], jnp.int32)
    position = jnp.arange(8, dtype=jnp.int32)
    slot = (position % 2 ^ z_hi) * 4 + place[(position // 2 - y) % 4]
    return jnp.take(values, slot, axis=0)


def on_device(
    tokens, cotangent, w_qkv, w_out, w_gate_up, w_down,
    attn_gain, attn_bias, ffn_gain, ffn_bias, prefix_len, clusters,
):
    x = tokens.reshape(ROWS, WIDE)
    cot = cotangent.reshape(ROWS, WIDE)
    dp = lax.axis_index("dp")
    own_id = lax.dynamic_slice_in_dim(clusters, dp, 1)
    seq_weight = 1.0 / jnp.sum((own_id[:, None] == clusters[None, :]).astype(F32), axis=1)
    cosine, sine = (jnp.asarray(t) for t in rotary_tables(LEN, HEAD_DIM))
    row = lambda v: v.reshape(1, WIDE)
    ff_total = w_down.shape[1]
    pad = 8 * COLS - ff_total

    own_rows = lax.dynamic_slice_in_dim(w_gate_up, dp * 16, 16, axis=0)
    own_down = lax.dynamic_slice_in_dim(w_down, dp * 16, 16, axis=0)
    piece = jnp.concatenate([own_rows.transpose(1, 0, 2), own_down[None]], axis=0)
    piece = jnp.pad(piece, ((0, 0), (0, 0), (0, pad))).reshape(3, 16, 8, COLS).transpose(2, 0, 1, 3)
    piece = lax.all_to_all(piece, "seq", split_axis=0, concat_axis=0, tiled=True)
    piece = piece.transpose(1, 0, 2, 3)
    ffn_w = lax.all_gather(piece, "dp", axis=0)

    w_in = w_qkv.reshape(WIDE, 768)
    tokens_all, q, k, v = call(
        project_kernel, "project", 0,
        [((8, ROWS, WIDE), BF16)] + [((LEN, 256), BF16)] * 3,
        (x, w_in, cosine, sine), "vvvv", (), GATHER_COPIES, 2 * LEN * WIDE * 768,
    )
    heads_out, lse = attend(prefix_len, q, k, v)
    normed, unit_one, inverse_one = call(
        attended_kernel, "attended", 1,
        [((ROWS, WIDE), F32), ((ROWS, WIDE), F32), ((ROWS, 128), F32)],
        (heads_out, w_out, x, row(attn_gain), row(attn_bias)), "vvvvv",
        (pltpu.VMEM((ROWS, WIDE), F32), *SCATTER_SCRATCH), SCATTER_COPIES, 2 * LEN * WIDE * 256,
    )
    weight_scratch = lambda n: pltpu.VMEM((n, 8, 256, COLS), BF16)
    output, normed_all, hidden, gz_all, ggu, grad_z2, ffn_vec = call(
        feed_kernel, "feed", 2,
        [
            ((ROWS, WIDE), BF16), ((8, ROWS, WIDE), BF16), ((8, ROWS, COLS), BF16),
            ((8, ROWS, WIDE), BF16), ((8, ROWS, 2 * COLS), BF16), ((ROWS, WIDE), F32),
            ((2, 8, WIDE), F32),
        ],
        (normed, cot, seq_weight, ffn_w, row(ffn_gain), row(ffn_bias)), "vvshvv",
        (
            weight_scratch(3), pltpu.VMEM((8, ROWS, COLS), F32), pltpu.VMEM((8, ROWS, COLS), F32),
            pltpu.VMEM((ROWS, WIDE), F32), pltpu.SemaphoreType.DMA((16,)), *SCATTER_SCRATCH,
        ),
        2 * GATHER_COPIES + SCATTER_COPIES, 2 * LEN * WIDE * COLS * 4,
    )
    ffn_grad = feed_weights(normed_all, gz_all, ggu, hidden)
    ffn_part = lax.psum_scatter(ffn_grad, "dp", scatter_dimension=0, tiled=False)
    grad_z1, gz1_all, grad_heads, attn_vec = call(
        feed_back_kernel, "feed_back", 3,
        [((ROWS, WIDE), F32), ((8, ROWS, WIDE), BF16), ((LEN, 256), BF16), ((2, 8, WIDE), F32)],
        (ggu, grad_z2, ffn_w, unit_one, inverse_one, row(attn_gain), w_out), "vvhvvvv",
        (
            weight_scratch(2), pltpu.VMEM((ROWS, WIDE), F32), pltpu.SemaphoreType.DMA((16,)),
            *SCATTER_SCRATCH,
        ),
        GATHER_COPIES + SCATTER_COPIES, 2 * LEN * WIDE * COLS * 2,
    )
    dq, dk, dv = attend_back(prefix_len, q, k, v, grad_heads, lse, cosine, sine)
    (input_grad,) = call(
        input_kernel, "input", 4, [((ROWS, WIDE), F32)],
        (dq, dk, dv, w_in, grad_z1), "vvvvv",
        (pltpu.VMEM((ROWS, WIDE), F32), *SCATTER_SCRATCH), SCATTER_COPIES, 2 * LEN * WIDE * 768,
    )

    tokens_rows = in_order(tokens_all).reshape(LEN, WIDE)
    gz1_rows = in_order(gz1_all).reshape(LEN, WIDE)
    grad_project = jnp.concatenate([dq, dk, dv], axis=1)
    qkv_grad = jnp.einsum("td,tc->dc", tokens_rows, grad_project, preferred_element_type=F32)
    out_grad = jnp.einsum("th,td->hd", heads_out, gz1_rows, preferred_element_type=F32)
    vec = jnp.concatenate([attn_vec.sum(1), ffn_vec.sum(1)], axis=0)
    vec = lax.psum_scatter(vec, "seq", scatter_dimension=1, tiled=True)
    vec = lax.psum(vec, "dp")

    def over_dp(value):
        part = lax.psum_scatter(value.astype(BF16), "dp", scatter_dimension=0, tiled=True)
        return lax.all_gather(part, "dp", axis=0, tiled=True).astype(F32)

    grad_qkv = over_dp(qkv_grad).reshape(WIDE, 3, 256)
    grad_out = over_dp(out_grad)

    ffn_part = ffn_part.transpose(1, 0, 2, 3)
    ffn_part = lax.all_to_all(ffn_part, "seq", split_axis=0, concat_axis=0, tiled=True)
    ffn_whole = lax.all_gather(ffn_part, "dp", axis=0)
    ffn_whole = ffn_whole.transpose(0, 3, 2, 1, 4).reshape(256, 3, 8 * COLS)[:, :, :ff_total]
    ffn_whole = ffn_whole.astype(F32)
    return (
        output.reshape(tokens.shape),
        input_grad.reshape(tokens.shape),
        grad_qkv,
        grad_out,
        ffn_whole[:, :2],
        ffn_whole[:, 2],
        vec[0],
        vec[1],
        vec[2],
        vec[3],
    )


def solution(mesh):
    return jax.shard_map(
        on_device,
        mesh=mesh,
        in_specs=(
            P("seq", "dp", None), P("seq", "dp", None), P(None, None, "seq"), P("seq", None),
            P("seq", None, None), P("seq", None), P(), P(), P(), P(), P("dp"), P(),
        ),
        out_specs=(
            P("seq", "dp", None), P("seq", "dp", None), P(None, None, "seq"), P("seq", None),
            P("seq", None, None), P("seq", None), P("seq"), P("seq"), P("seq"), P("seq"),
        ),
        check_vma=False,
    )
```

time: 1300 us -> 849 us (0.65)
  waiting for transfers between devices: 834 us -> 283 us
  Pallas kernels: 0 us -> 324 us
  matrix products: 91.8 us -> 10.1 us
  other arithmetic: 97.4 us -> 20.8 us
  local copies, waits for them, and re-layouts: 185 us -> 120 us
  starting transfers between devices: 16.8 us -> 0.32 us
    pallas_call x0 -> x8, Pallas kernels: none -> 324 us  [the longest x5 286 us: call(): pl.pallas_call(body, name=name, out_shape=tuple((jax.ShapeDtypeStruct(s,...]
    reduce_scatter x4 -> x3, waiting for transfers between devices: 491 us -> 174 us  [the longest x2 95.5 us: over_dp(): lax.psum_scatter(value.astype(BF16), 'dp', scatter_dimension=0, tiled=True)]
    all_gather x4, waiting for transfers between devices: 247 us -> 86.5 us  [the longest x1 47.1 us: on_device(): ffn_whole = lax.all_gather(ffn_part, 'dp', axis=0)]
    dot_general x26 -> x2, matrix products: 91.8 us -> 10.1 us  [the longest x1 7.81 us: on_device(): jnp.einsum('td,tc->dc', tokens_rows, grad_project, preferred_element_type...]
    psum x1 -> x0, waiting for transfers between devices: 80.6 us -> none  [on_device(): lax.psum(qkv_grad.astype(jnp.bfloat16), 'dp').astype(jnp.float32)]
    convert_element_type x2 -> x0, local copies, waits for them, and re-layouts: 38.5 us -> none  [on_device(): ffn_rows_back, norm_rows_back = (lax.all_to_all(ffn_total.astype(jnp.bflo...]
    all_to_all x0 -> x2, blocking collectives: none -> 34.9 us  [the longest x1 19.3 us: on_device(): lax.all_to_all(piece, 'seq', split_axis=0, concat_axis=0, tiled=True)]
    concatenate x2, other arithmetic: 28.9 us -> 0.06 us  [the longest x1 0.04 us: on_device(): jnp.concatenate([own_rows.transpose(1, 0, 2), own_down[None]], axis=0)]
  transfers between devices with their start and end apart: 12 -> 8, of which waited for: 10 -> 7; matrix products, arithmetic and copies ran while one was open for 11% -> 6% of each run, Pallas kernels for 0% -> 20%
where the time goes in v1:
time: 849 us; the launch traced here: 838 us
  Pallas kernels  324 us (38%)
  waiting for transfers between devices  283 us (33%)
  local copies, waits for them, and re-layouts  120 us (14%)
  blocking collectives  64 us (8%)
  other arithmetic  20.8 us (2%)
  between operations  16.1 us (2%)
  matrix products  10.1 us (1%)
    pallas_call x5, Pallas kernels, call(): pl.pallas_call(body, name=name, out_shape=tuple((jax.ShapeDtypeStruct(s,...  286 us
    reduce_scatter x2, waiting for transfers between devices, over_dp(): lax.psum_scatter(value.astype(BF16), 'dp', scatter_dimension=0, tiled=True)  95.5 us
    reduce_scatter x1, waiting for transfers between devices, on_device(): lax.psum_scatter(ffn_grad, 'dp', scatter_dimension=0, tiled=False)  78.9 us
    unnamed x27, local copies, waits for them, and re-layouts  48.7 us
    all_gather x1, waiting for transfers between devices, on_device(): ffn_whole = lax.all_gather(ffn_part, 'dp', axis=0)  47.1 us
    all_gather x2, waiting for transfers between devices, over_dp(): return lax.all_gather(part, 'dp', axis=0, tiled=True).astype(F32)  39.4 us
    psum x1, blocking collectives, on_device(): vec = lax.psum(vec, 'dp')  29.1 us
    unnamed x9, waiting for transfers between devices  22.3 us
  transfers between devices with their start and end apart: 8, of which 7 were waited for; matrix products, arithmetic and copies ran while one was open for 6% of the time, Pallas kernels for 20%

profile of v1, /device:TPU:1, one launch (start us, length us, event | category | flops | bytes accessed | tf_op | source)
XLA Modules:
  0.0 838.4 jit_solution(4011075616222872323)
XLA Ops:
  12.2 5.4 constant_dynamic-slice_fusion.1
  20.9 19.3 %all_to_all.10 = bf16[8,3,16,768]{3,2,1,0:T(8,128)(2,1)S(1)} all-to-all(bf16[8,3,16,768]{3,2,1,0:T(8,128)(2,1)S(1)} %copy.75), channel_id=1, replica_groups=mesh['dp'=16,'seq'=8] {'seq'}, dimensions={0} | all-to-all | bytes 1179648 | tf_op jit(solution)/shard_map/all_to_all | solution.py:651
  46.4 4.9 copy.72.w_ref
  54.6 57.8 %project.1 = (bf16[8,128,2048]{2,1,0:T(8,128)(2,1)}, bf16[1024,256]{1,0:T(8,128)(2,1)}, bf16[1024,256]{1,0:T(8,128)(2,1)}, bf16[1024,256]{1,0:T(8,128)(2,1)}) custom-call(bf16[128,2048]{1,0:T(8,128)(2,1)} %bitcast.80, bf16[2048,768]{1,0:T(8,128)(2,1)} %copy.72.w_ref, f32[1024,128]{1,0:T(8,128)} %constant.106.clone.cos_ref.cosq_ref, ...), custom_call_target="tpu_custom_call" | custom-call | flops 3221225472 | bytes 20000000 | tf_op jit(solution)/shard_map/project/pallas_call | solution.py:288
  112.4 5.1 gather_fusion.1
  117.5 8.4 %attend.1 = (bf16[1024,256]{1,0:T(8,128)(2,1)}, f32[2,1,1024]{2,1,0:T(1,128)}) custom-call(s32[1]{0:T(128)S(6)} %copy.93.prefix_ref, bf16[1024,256]{1,0:T(8,128)(2,1)} %get-tuple-element.34.q_ref, bf16[1024,256]{1,0:T(8,128)(2,1)} %get-tuple-element.35.k_ref, bf16[1024,256]{1,0:T(8,128)(2,1)} %get-tuple-element.36.v_ref), custom_call_target="tpu_custom_call" | custom-call | tf_op jit(solution)/shard_map/attend/pallas_call | solution.py:346
  125.9 34.5 %attended.1 = (f32[128,2048]{1,0:T(8,128)}, f32[128,2048]{1,0:T(8,128)}, f32[128,128]{1,0:T(8,128)}) custom-call(bf16[1024,256]{1,0:T(8,128)(2,1)} %get-tuple-element.37.heads_ref, bf16[256,2048]{1,0:T(8,128)(2,1)} %w_out_ref.1, bf16[128,2048]{1,0:T(8,128)(2,1)} %bitcast.81, f32[1,2048]{1,0:T(1,128)} %bitcast.86, f32[1,2048]{1,0:T(1,128)} %bitcast.83), custom_call_target="tpu_custom_call" | custom-call | flops 1073741824 | bytes 20000000 | tf_op jit(solution)/shard_map/attended/pallas_call | solution.py:288
  160.4 94.6 %feed.1 = (bf16[128,2048]{1,0:T(8,128)(2,1)}, bf16[8,128,2048]{2,1,0:T(8,128)(2,1)}, bf16[8,128,768]{2,1,0:T(8,128)(2,1)}, bf16[8,128,2048]{2,1,0:T(8,128)(2,1)}...) custom-call(f32[128,2048]{1,0:T(8,128)} %get-tuple-element.38.normed_ref, ...), custom_call_target="tpu_custom_call" | custom-call | flops 12884901888 | bytes 20000000 | tf_op jit(solution)/shard_map/feed/pallas_call | solution.py:288
  255.0 62.9 %feed_back.1 = (f32[128,2048]{1,0:T(8,128)}, bf16[8,128,2048]{2,1,0:T(8,128)(2,1)}, bf16[1024,256]{1,0:T(8,128)(2,1)}, f32[2,8,2048]{2,1,0:T(8,128)}) custom-call(bf16[8,128,1536]{2,1,0:T(8,128)(2,1)} %get-tuple-element.40.ggu_ref, f32[128,2048]{1,0:T(8,128)} %get-tuple-element.41.gz_ref, bf16[16,3,8,16,768]{4,3,2,1,0:T(8,128)(2,1)} %bitcast.79, ...), custom_call_target="tpu_custom_call" | custom-call | flops 6442450944 | bytes 20000000 | tf_op jit(solution)/shard_map/feed_back/pallas_call | solution.py:288
  317.8 5.0 gather_fusion.2
  322.9 6.3 broadcast_select_fusion
  331.5 13.2 %attend_back.1 = (bf16[1024,256]{1,0:T(8,128)(2,1)}, bf16[1024,256]{1,0:T(8,128)(2,1)}, bf16[1024,256]{1,0:T(8,128)(2,1)}) custom-call(s32[1]{0:T(128)S(6)} %copy.93.prefix_ref, bf16[1024,256]{1,0:T(8,128)(2,1)} %get-tuple-element.34.q_ref, bf16[1024,256]{1,0:T(8,128)(2,1)} %get-tuple-element.35.k_ref, bf16[1024,256]{1,0:T(8,128)(2,1)} %get-tuple-element.36.v_ref, ...), custom_call_target="tpu_custom_call" | custom-call | tf_op jit(solution)/shard_map/attend_back/pallas_call | solution.py:410
  344.8 7.8 convolution_convert_fusion
  352.6 16.0 %feed_weights.1 = bf16[16,3,8,16,768]{4,3,2,1,0:T(8,128)(2,1)} custom-call(bf16[1024,2048]{1,0:T(8,128)(2,1)} %bitcast.61, bf16[1024,2048]{1,0:T(8,128)(2,1)} %bitcast.62, bf16[1024,1536]{1,0:T(8,128)(2,1)} %bitcast.63, bf16[1024,768]{1,0:T(8,128)(2,1)} %bitcast.67), custom_call_target="tpu_custom_call" | custom-call | tf_op jit(solution)/shard_map/feed_weights/pallas_call | solution.py:608
  371.1 28.8 %reduce-scatter.9.cloned.1.call-done = bf16[16,2048]{1,0:T(8,128)(2,1)} async-done(((bf16[256,2048]{1,0:T(8,128)(2,1)}), bf16[16,2048]{1,0:T(8,128)(2,1)}) %reduce-scatter.9.cloned.1.call-update) | async-done | bytes 65552 | tf_op jit(solution)/shard_map/reduce_scatter | solution.py:712
  400.0 66.8 %reduce-scatter.7.cloned.1.call-done = bf16[128,768]{1,0:T(8,128)(2,1)} async-done(((bf16[2048,768]{1,0:T(8,128)(2,1)}), bf16[128,768]{1,0:T(8,128)(2,1)}) %reduce-scatter.7.cloned.1.call-update) | async-done | bytes 196624 | tf_op jit(solution)/shard_map/reduce_scatter | solution.py:712
  466.8 78.9 %reduce-scatter.11.cloned.1.call-done = bf16[1,3,8,16,768]{4,3,2,1,0:T(8,128)(2,1)} async-done(((bf16[16,3,8,16,768]{4,3,2,1,0:T(8,128)(2,1)}), bf16[1,3,8,16,768]{4,3,2,1,0:T(8,128)(2,1)}) %reduce-scatter.11.cloned.1.call-update) | async-done | bytes 589840 | tf_op jit(solution)/shard_map/reduce_scatter | solution.py:684
  546.8 15.6 %all_to_all.11 = bf16[8,3,16,768]{3,2,1,0:T(8,128)(2,1)} all-to-all(bf16[8,3,16,768]{3,2,1,0:T(8,128)(2,1)S(1)} %copy.79), channel_id=1, replica_groups=mesh['dp'=16,'seq'=8] {'seq'}, dimensions={0} | all-to-all | bytes 1179648 | tf_op jit(solution)/shard_map/all_to_all | solution.py:719
  562.4 36.1 %input.1 = f32[128,2048]{1,0:T(8,128)} custom-call(bf16[1024,256]{1,0:T(8,128)(2,1)} %get-tuple-element.46.dq_ref, bf16[1024,256]{1,0:T(8,128)(2,1)} %get-tuple-element.47.dk_ref, bf16[1024,256]{1,0:T(8,128)(2,1)} %get-tuple-element.48.dv_ref, bf16[2048,768]{1,0:T(8,128)(2,1)} %copy.72.w_ref, f32[128,2048]{1,0:T(8,128)} %get-tuple-element.49.gz1_ref), custom_call_target="tpu_custom_call" | custom-call | flops 3221225472 | bytes 20000000 | tf_op jit(solution)/shard_map/input/pallas_call | solution.py:288
  601.9 22.2 %reduce-scatter.13.cloned.1.call-done = f32[256,4]{1,0:T(8,128)} async-done(((f32[2048,4]{1,0:T(8,128)}), f32[256,4]{1,0:T(8,128)}) %reduce-scatter.13.cloned.1.call-update) | async-done | bytes 4112
  625.0 29.1 %psum.7 = f32[4,256]{1,0:T(4,128)S(1)} all-reduce(f32[4,256]{1,0:T(4,128)S(1)} %copy.86), channel_id=1, replica_groups=mesh['dp'=16,'seq'=8] {'dp'}, use_global_device_ids=true, to_apply=%region_7.9 | all-reduce | flops 1024 | bytes 8192 | tf_op jit(solution)/shard_map/psum | solution.py:709
  662.1 34.7 %all-gather.7.cloned.1.call-done = bf16[2048,768]{1,0:T(8,128)(2,1)} async-done(((bf16[128,768]{1,0:T(8,128)(2,1)}), bf16[2048,768]{1,0:T(8,128)(2,1)}) %all-gather.7.cloned.1.call-update) | async-done | bytes 3145744 | tf_op jit(solution)/shard_map/all_gather | solution.py:713
  696.9 5.4 copy.78
  702.2 6.6 copy.82
  708.8 47.1 %all-gather.13.cloned.1.call-done = bf16[128,3,16,768]{3,2,1,0:T(8,128)(2,1)} async-done(((bf16[8,3,16,768]{3,2,1,0:T(8,128)(2,1)}), bf16[128,3,16,768]{3,2,1,0:T(8,128)(2,1)}) %all-gather.13.cloned.1.call-update) | async-done | bytes 9437200 | tf_op jit(solution)/shard_map/all_gather | solution.py:720
  755.9 11.8 %copy.91 = bf16[16,8,3,16,768]{4,1,3,0,2:T(8,128)(2,1)} copy(bf16[16,8,3,16,768]{4,3,2,1,0:T(8,128)(2,1)} %bitcast.57) | data formatting | bytes 18874368 | tf_op jit(solution)/shard_map/all_gather | solution.py:720
  767.7 14.1 %reshape.188 = bf16[256,3,6144]{2,0,1:T(8,128)(2,1)} reshape(bf16[16,16,3,8,768]{4,3,1,0,2:T(8,128)(2,1)} %bitcast.54) | data formatting | bytes 18874368 | tf_op jit(solution)/shard_map/reshape | solution.py:721
  781.8 10.3 %slice_convert_fusion = f32[256,3,5461]{2,0,1:T(8,128)} fusion(bf16[256,3,6144]{2,0,1:T(8,128)(2,1)} %reshape.188), kind=kLoop, calls=%fused_computation.4 | loop fusion | flops 4194048 | bytes 25164288 | tf_op jit(solution)/shard_map/convert_element_type | solution.py:722
  792.1 5.4 slice_bitcast_fusion
  797.5 9.2 %slice.35 = f32[256,2,5461]{2,0,1:T(8,128)} slice(f32[256,3,5461]{2,0,1:T(8,128)} %slice_convert_fusion), slice={[0:256], [0:2], [0:5461]} | slice | bytes 22368256 | tf_op jit(solution)/shard_map/slice | solution.py:728
  806.7 17.5 %copy.83 = f32[256,2,5461]{0,1,2:T(2,128)} copy(f32[256,2,5461]{2,0,1:T(8,128)} %slice.35) | data formatting | bytes 22368256
  824.2 6.2 copy.84
  (61 shorter events, 35.4 us)
Async XLA Ops:
  7.2 1.8 copy-start
  7.2 153.2 %all-gather.11.cloned.1.call-start = ((), (), s32[]{:S(2)}) async-start(), calls=%async_computation.11 | async-start | bytes 10027008 | tf_op jit(solution)/shard_map/all_gather | solution.py:653
  41.1 358.9 %reduce-scatter.9.cloned.1.call-start = ((), (), s32[]{:S(2)}) async-start(), calls=%async_computation.8 | async-start | bytes 1114112 | tf_op jit(solution)/shard_map/reduce_scatter | solution.py:712
  46.4 4.9 copy-start.7
  46.4 7.5 copy-start.2
  322.9 6.3 copy-start.6
  331.5 135.3 %reduce-scatter.7.cloned.1.call-start = ((), (), s32[]{:S(2)}) async-start(), calls=%async_computation.6 | async-start | bytes 3342336 | tf_op jit(solution)/shard_map/reduce_scatter | solution.py:712
  352.6 193.1 %reduce-scatter.11.cloned.1.call-start = ((), (), s32[]{:S(2)}) async-start(), calls=%async_computation.10 | async-start | bytes 10027008 | tf_op jit(solution)/shard_map/reduce_scatter | solution.py:684
  368.7 0.9 copy-start.5
  368.7 1.0 copy-start.4
  368.7 255.3 %reduce-scatter.13.cloned.1.call-start = ((), (), s32[]{:S(2)}) async-start(), calls=%async_computation.13 | async-start | bytes 1179648
  371.1 288.3 %all-gather.9.cloned.1.call-start = ((), (), s32[]{:S(2)}) async-start(), calls=%async_computation.9 | async-start | bytes 1114112 | tf_op jit(solution)/shard_map/all_gather | solution.py:713
  399.9 296.9 %all-gather.7.cloned.1.call-start = ((), (), s32[]{:S(2)}) async-start(), calls=%async_computation.7 | async-start | bytes 3342336 | tf_op jit(solution)/shard_map/all_gather | solution.py:713
  466.8 289.2 %all-gather.13.cloned.1.call-start = ((), (), s32[]{:S(2)}) async-start(), calls=%async_computation.12 | async-start | bytes 10027008 | tf_op jit(solution)/shard_map/all_gather | solution.py:720
  806.7 24.5 %copy-start.1 = (bf16[256,5461]{0,1:T(8,128)(2,1)S(1)}, bf16[256,5461]{0,1:T(8,128)(2,1)}, u32[]{:S(2)}) copy-start(bf16[256,5461]{0,1:T(8,128)(2,1)} %param.23) | copy-start | bytes 8388100
  824.2 6.2 copy-start.3
Sparse Core Ops, SparseCore 0:
  41.2 80.3 all-gather.10
  331.6 68.2 reduce-scatter.8
  403.0 63.6 reduce-scatter.6
  469.7 75.9 reduce-scatter.10
  550.2 73.8 reduce-scatter.12
  625.6 33.7 all-gather.8
  661.0 35.7 all-gather.6
  698.6 57.3 all-gather.12

commit v2 on v1

v2 whole, which is shorter than its diff:
```python
import functools

import jax
import jax.numpy as jnp
import numpy as np
from jax import lax
from jax.experimental import pallas as pl
from jax.experimental.pallas import tpu as pltpu
from jax.sharding import PartitionSpec as P

MESH = pl.DeviceIdType.MESH
F32, BF16 = jnp.float32, jnp.bfloat16
HEAD_DIM = 128
ROWS = 128
WIDE = 2048
COLS = 768
LEN = 1024
VMEM_BYTES = 60 * 1024 * 1024
deep_alpha = 48.0**0.25
norm_eps = 1e-05
rotary_base = 10000.0


def rotary_tables(length, head_width):
    half_width = head_width // 2
    position = np.arange(length, dtype=np.float64)
    inverse = rotary_base ** (-np.arange(half_width, dtype=np.float64) * 2.0 / head_width)
    angles = position[:, None] * inverse[None, :]
    cosine_table = np.cos(angles)
    sine_table = np.sin(angles)
    return (
        np.concatenate([cosine_table, cosine_table], axis=1).astype(np.float32),
        np.concatenate([-sine_table, sine_table], axis=1).astype(np.float32),
    )


FF = 704
PART = 176


class Links:
    def __init__(self, send, recv):
        self.send, self.recv, self.count = send, recv, 0
        dp, seq = lax.axis_index("dp"), lax.axis_index("seq")
        y, z_hi = seq // 2, lax.rem(seq, 2)
        z_lo, x, core = dp // 8, lax.rem(dp // 2, 4), lax.rem(dp, 2)
        self.y, self.z_hi, self.z_lo, self.x, self.core = y, z_hi, z_lo, x, core
        self.z = z_hi * 2 + z_lo

    def to(self, x=0, y=0, z=0, sibling=False):
        z_hi, z_lo = self.z_at(z)
        x, y = lax.rem(self.x + x, 4), lax.rem(self.y + y, 4)
        core = 1 - self.core if sibling else self.core
        return (z_lo * 8 + x * 2 + core, y * 2 + z_hi)

    def z_at(self, offset):
        z = lax.rem(self.z + offset, 4)
        return z // 2, lax.rem(z, 2)

    def part(self, offset):
        return pl.ds(pl.multiple_of(lax.rem(self.x + offset, 4) * PART, 16), PART)

    def barrier(self, *where):
        gate = pltpu.get_barrier_semaphore()
        for device in where:
            pl.semaphore_signal(gate, inc=1, device_id=device, device_id_type=MESH)
        pl.semaphore_wait(gate, len(where))

    def start(self, src, dst, where):
        copy = pltpu.make_async_remote_copy(
            src_ref=src,
            dst_ref=dst,
            send_sem=self.send.at[self.count],
            recv_sem=self.recv.at[self.count],
            device_id=where,
            device_id_type=MESH,
        )
        self.count += 1
        copy.start()
        return copy

    def first_row(self, slot):
        step = (0, 3, 1, 2)[slot % 4]
        half = self.z_hi if slot < 4 else 1 - self.z_hi
        return pl.multiple_of((lax.rem(self.y + step, 4) * 2 + half) * ROWS, ROWS)


def together(*tasks):
    due = [[next(task), i, task] for i, task in enumerate(tasks)]
    while due:
        due.sort(key=lambda entry: entry[:2])
        try:
            due[0][0] = next(due[0][2])
        except StopIteration:
            due.pop(0)


def received(*copies):
    for copy in copies:
        copy.wait_recv()


def sent(copies):
    for copy in copies:
        copy.wait_send()


H0, H1 = pl.ds(0, 64), pl.ds(64, 64)


def gather(links, buf, work):
    up, down, across = links.to(y=1), links.to(y=3), links.to(z=2)
    copies = []

    def send(slot, rows, dst, where):
        copies.append(links.start(buf.at[slot, rows], buf.at[dst, rows], where))
        return copies[-1]

    u0, d1 = send(0, H0, 1, up), send(0, H1, 2, down)
    z0, z1 = send(0, H0, 4, across), send(0, H1, 4, across)
    u1, d0 = send(0, H1, 1, up), send(0, H0, 2, down)
    yield 6
    received(u0)
    fu = send(1, H0, 3, up)
    received(d1)
    fd = send(2, H1, 3, down)
    yield 12
    received(z0)
    pu0 = send(4, H0, 5, up)
    received(z1)
    pd1 = send(4, H1, 6, down)
    pu1, pd0 = send(4, H1, 5, up), send(4, H0, 6, down)
    received(u1, d0)
    work((0, 1))
    yield 19
    received(fu, fd)
    work((2, 3))
    yield 24
    received(pu0)
    gu = send(5, H0, 7, up)
    received(pd1)
    gd = send(6, H1, 7, down)
    yield 29
    received(pu1, pd0)
    work((4, 5))
    yield 36
    received(gu, gd)
    work((6, 7))
    sent(copies)


def gather_near(links, buf, work):
    up, down, side = links.to(y=1), links.to(y=3), links.to(sibling=True)
    copies = []

    def send(slot, rows, dst, where):
        copies.append(links.start(buf.at[slot, rows], buf.at[dst, rows], where))
        return copies[-1]

    every = pl.ds(0, ROWS)
    u0, d1 = send(0, H0, 1, up), send(0, H1, 2, down)
    u1, d0 = send(0, H1, 1, up), send(0, H0, 2, down)
    s0 = send(0, every, 4, side)
    yield 1
    received(s0)
    work((0, 4))
    yield 6
    received(u0)
    fu = send(1, H0, 3, up)
    received(d1)
    fd = send(2, H1, 3, down)
    yield 11
    received(u1)
    s1 = send(1, every, 5, side)
    received(d0)
    s2 = send(2, every, 6, side)
    work((1, 2))
    yield 13
    received(s1, s2)
    work((5, 6))
    yield 17
    received(fu)
    s30 = send(3, H0, 7, side)
    received(fd)
    s31 = send(3, H1, 7, side)
    yield 18
    received(s30, s31)
    work((3, 7))
    sent(copies)


A, B = pl.ds(0, 80), pl.ds(80, 48)
A0, A1 = pl.ds(0, 48), pl.ds(48, 32)
B0, B1 = pl.ds(80, 16), pl.ds(96, 32)
SCATTER_SCRATCH = (
    pltpu.VMEM((8, ROWS, WIDE), BF16),
    pltpu.VMEM((4, 48, WIDE), BF16),
    pltpu.VMEM((48, WIDE), BF16),
    pltpu.VMEM((2, 48, WIDE), BF16),
    pltpu.VMEM((2, 80, WIDE), BF16),
    pltpu.VMEM((2, 2, 80, WIDE), BF16),
    pltpu.VMEM((80, WIDE), BF16),
)


def add_rows(target, slot, rows, *others):
    value = target[slot, rows].astype(F32)
    for other in others:
        value = value + other.astype(F32)
    target[slot, rows] = value.astype(BF16)


def scatter(links, bufs, compute, total):
    sums, from_z, b_far, b_near, a_far, a_near, a_z = bufs
    up, down, across = links.to(y=1), links.to(y=3), links.to(z=2)
    copies = []

    def send(src, dst, where):
        copies.append(links.start(src, dst, where))
        return copies[-1]

    def far_a(o):
        half = o // 4
        return (
            send(sums.at[o + 3, A0], a_far.at[half, pl.ds(0, 48)], up),
            send(sums.at[o + 3, A1], a_far.at[half, pl.ds(48, 32)], down),
        )

    def near_a(o, far):
        half = o // 4
        received(far[0])
        add_rows(sums, o + 2, A0, a_far[half, 0:48])
        one = send(sums.at[o + 2, A], a_near.at[half, 0], up)
        received(far[1])
        add_rows(sums, o + 1, A1, a_far[half, 48:80])
        return one, send(sums.at[o + 1, A], a_near.at[half, 1], down)

    def cross_b(j):
        return send(sums.at[4 + j, B], from_z.at[j], across)

    compute((7, 3))
    z3 = cross_b(3)
    far_other = far_a(4)
    far_own = far_a(0)
    compute((5, 6))
    z1, z2 = cross_b(1), cross_b(2)
    compute((1, 2))
    yield 8
    received(z3)
    add_rows(sums, 3, B, from_z[3])
    far_b = (
        send(sums.at[3, B0], b_far.at[pl.ds(0, 16)], up),
        send(sums.at[3, B1], b_far.at[pl.ds(16, 32)], down),
    )
    near_other = near_a(4, far_other)
    compute((4, 0))
    z0 = cross_b(0)
    yield 12
    near_own = near_a(0, far_own)
    yield 18
    received(*near_other)
    add_rows(sums, 4, A, a_near[1, 0], a_near[1, 1])
    z_a = send(sums.at[4, A], a_z, across)
    yield 20
    received(z2)
    add_rows(sums, 2, B, from_z[2])
    received(far_b[0])
    add_rows(sums, 2, B0, b_far[0:16])
    near_b0 = send(sums.at[2, B], b_near.at[0], up)
    received(z1)
    add_rows(sums, 1, B, from_z[1])
    received(far_b[1])
    add_rows(sums, 1, B1, b_far[16:48])
    near_b1 = send(sums.at[1, B], b_near.at[1], down)
    yield 27
    received(z0, near_b0, near_b1)
    total[80:128] = (
        sums[0, B].astype(F32)
        + from_z[0].astype(F32)
        + b_near[0].astype(F32)
        + b_near[1].astype(F32)
    )
    received(*near_own)
    yield 30
    received(z_a)
    total[0:80] = (
        sums[0, A].astype(F32)
        + a_near[0, 0].astype(F32)
        + a_near[0, 1].astype(F32)
        + a_z[...].astype(F32)
    )
    sent(copies)


NEAR_SCRATCH = (
    pltpu.VMEM((8, ROWS, WIDE), BF16),
    pltpu.VMEM((4, ROWS, WIDE), BF16),
    pltpu.VMEM((ROWS, WIDE), BF16),
    pltpu.VMEM((2, ROWS, WIDE), BF16),
)


def scatter_near(links, bufs, compute, total):
    sums, from_side, far, near = bufs
    up, down, side = links.to(y=1), links.to(y=3), links.to(sibling=True)
    copies = []

    def send(src, dst, where):
        copies.append(links.start(src, dst, where))
        return copies[-1]

    every = pl.ds(0, ROWS)
    compute((7, 3))
    s3 = send(sums.at[7], from_side.at[3], side)
    compute((5, 6))
    s1 = send(sums.at[5], from_side.at[1], side)
    s2 = send(sums.at[6], from_side.at[2], side)
    received(s3)
    add_rows(sums, 3, every, from_side[3])
    fu = send(sums.at[3, H0], far.at[H0], up)
    fd = send(sums.at[3, H1], far.at[H1], down)
    compute((1, 2))
    received(s1, s2)
    add_rows(sums, 2, every, from_side[2])
    nu1 = send(sums.at[2, H1], near.at[0, H1], up)
    add_rows(sums, 1, every, from_side[1])
    nd0 = send(sums.at[1, H0], near.at[1, H0], down)
    compute((4, 0))
    s0 = send(sums.at[4], from_side.at[0], side)
    yield 8
    received(fu)
    add_rows(sums, 2, H0, far[0:64])
    nu0 = send(sums.at[2, H0], near.at[0, H0], up)
    received(fd)
    add_rows(sums, 1, H1, far[64:128])
    nd1 = send(sums.at[1, H1], near.at[1, H1], down)
    yield 17
    received(s0, nu1, nd0, nu0, nd1)
    total[...] = (
        sums[0].astype(F32)
        + from_side[0].astype(F32)
        + near[0].astype(F32)
        + near[1].astype(F32)
    )
    sent(copies)


Y0, Y1 = pl.ds(0, 2), pl.ds(2, 2)
GU = pl.ds(0, 2)


def spread(links, piece, w, local):
    xp, xm, zp, zm = links.to(x=1), links.to(x=3), links.to(z=1), links.to(z=3)
    copies = []

    def at(k, z, x, y=pl.ds(0, 4)):
        z_hi, z_lo = links.z_at(z)
        return w.at[k, z_hi, y, z_lo, links.part(x)]

    def send(ref, where):
        copies.append(links.start(ref, ref, where))
        return copies[-1]

    def own():
        return w.at[:, links.z_hi, links.y, links.z_lo, links.part(0)]

    keep = pltpu.make_async_copy(piece.at[links.y], own(), local)
    keep.start()
    first = []
    for step in (2, 1, 3):
        copies.append(
            links.start(piece.at[lax.rem(links.y + step, 4)], own(), links.to(y=step))
        )
        first.append(copies[-1])
    yield 9
    keep.wait()
    received(*first)
    zu, zd = send(at(GU, 0, 0), zp), send(at(GU, 0, 0), zm)
    du, dd = send(at(2, 0, 0), xp), send(at(2, 0, 0), xm)
    gx = [(send(at(GU, 0, 0), xp), send(at(GU, 0, 0), xm))]
    dz = [(send(at(2, 0, 0), zp), send(at(2, 0, 0), zm))]
    yield 16
    received(du)
    fdu = send(at(2, 0, 3, Y0), xp)
    dz.append((send(at(2, 0, 3), zp), send(at(2, 0, 3), zm)))
    received(dd)
    fdd = send(at(2, 0, 1, Y1), xm)
    dz.append((send(at(2, 0, 1), zp), send(at(2, 0, 1), zm)))
    yield 20
    received(zu)
    fzu = send(at(0, 3, 0), zp)
    gx.append((send(at(GU, 3, 0), xp), send(at(GU, 3, 0), xm)))
    received(zd)
    fzd = send(at(1, 1, 0), zm)
    gx.append((send(at(GU, 1, 0), xp), send(at(GU, 1, 0), xm)))
    yield 25
    received(*gx[0])
    gf = [(send(at(0, 0, 3), xp), send(at(1, 0, 1), xm))]
    yield 28
    received(*dz[0])
    df = [(send(at(2, 3, 0, Y0), zp), send(at(2, 1, 0, Y1), zm))]
    received(fdu, fdd)
    dz.append((send(at(2, 0, 2), zp), send(at(2, 0, 2), zm)))
    yield 30
    received(fzu, fzd)
    gx.append((send(at(GU, 2, 0), xp), send(at(GU, 2, 0), xm)))
    yield 35
    received(*gx[1])
    gf.append((send(at(0, 3, 3), xp), send(at(1, 3, 1), xm)))
    received(*dz[1])
    df.append((send(at(2, 3, 3, Y0), zp), send(at(2, 1, 3, Y1), zm)))
    yield 42
    received(*gx[2])
    gf.append((send(at(0, 1, 3), xp), send(at(1, 1, 1), xm)))
    received(*dz[2])
    df.append((send(at(2, 3, 1, Y0), zp), send(at(2, 1, 1, Y1), zm)))
    yield 48
    received(*dz[3])
    df.append((send(at(2, 3, 2, Y0), zp), send(at(2, 1, 2, Y1), zm)))
    received(*gx[3])
    gf.append((send(at(0, 2, 3), xp), send(at(1, 2, 1), xm)))
    yield 60
    for pair in gf + df:
        received(*pair)
    sent(copies)


BLOCKS = pltpu.VMEM((2, 2, 4, 2, PART, 128), BF16)
REDUCE_SCRATCH = (
    pltpu.VMEM((3, 2, 4, 2, FF, 128), BF16),
    BLOCKS,
    pltpu.VMEM((2, 2, 2, 4, 2, PART, 128), BF16),
    pltpu.VMEM((2, 4, PART, 128), BF16),
    pltpu.VMEM((2, 2, 4, PART, 128), BF16),
    pltpu.VMEM((4, FF, 128), BF16),
    pltpu.VMEM((2, 4, FF, 128), BF16),
    pltpu.VMEM((4, PART, 128), BF16),
    pltpu.VMEM((2, 4, PART, 128), BF16),
)


def accumulate(count, target, *others):
    def step(i, carry):
        ref = target(i)
        value = ref[...].astype(F32)
        for other in others:
            value = value + other(i)[...].astype(F32)
        ref[...] = value.astype(BF16)
        return carry

    lax.fori_loop(0, count, step, 0)


def reduce(links, bufs, shard):
    g, fx, nx, fz, nz, fz2, nz2, fx2, nx2 = bufs
    xp, xm, zp, zm = links.to(x=1), links.to(x=3), links.to(z=1), links.to(z=3)
    copies = []
    every = pl.ds(0, 4)

    def send(src, dst, where):
        copies.append(links.start(src, dst, where))
        return copies[-1]

    def along_x(k, x):
        return g.at[k, :, :, :, links.part(x)]

    def block_x(k, x):
        return lambda i: g.at[k, i // 8, lax.rem(i // 2, 4), lax.rem(i, 2), links.part(x)]

    def plain(ref):
        return lambda i: ref.at[i // 8, lax.rem(i // 2, 4), lax.rem(i, 2)]

    def along_z(k, z, y=every, rows=pl.ds(0, FF)):
        z_hi, z_lo = links.z_at(z)
        return g.at[k, z_hi, y, z_lo, rows]

    def block_z(k, z, rows, first=0):
        z_hi, z_lo = links.z_at(z)
        return lambda i: g.at[k, z_hi, i + first, z_lo, rows]

    def shift(ref, first=0):
        return lambda i: ref.at[i + first]

    here = links.part(0)
    whole = pl.ds(0, FF)
    c1, c2 = send(along_x(0, 2), fx.at[0], xp), send(along_x(1, 2), fx.at[1], xm)
    e1 = send(along_z(2, 2, Y0), fz2.at[Y0], zp)
    e2 = send(along_z(2, 2, Y1), fz2.at[Y1], zm)
    c3, c4 = send(along_x(1, 1), nx.at[0, 1], xp), send(along_x(0, 3), nx.at[1, 0], xm)
    e3 = send(along_z(2, 1, Y1), nz2.at[0, Y1], zp)
    e4 = send(along_z(2, 3, Y0), nz2.at[1, Y0], zm)
    yield 9
    received(e1)
    accumulate(2, block_z(2, 1, whole), shift(fz2))
    e5 = send(along_z(2, 1, Y0), nz2.at[0, Y0], zp)
    received(e2)
    accumulate(2, block_z(2, 3, whole, 2), shift(fz2, 2))
    e6 = send(along_z(2, 3, Y1), nz2.at[1, Y1], zm)
    yield 17
    received(c1)
    accumulate(16, block_x(0, 1), plain(fx.at[0]))
    c5 = send(along_x(0, 1), nx.at[0, 0], xp)
    received(c2)
    accumulate(16, block_x(1, 3), plain(fx.at[1]))
    c6 = send(along_x(1, 3), nx.at[1, 1], xm)
    yield 26
    received(e3, e4, e5, e6)
    accumulate(4, block_z(2, 0, whole), shift(nz2.at[0]), shift(nz2.at[1]))
    d1 = send(along_z(2, 0, Y0, links.part(2)), fx2.at[Y0], xp)
    d2 = send(along_z(2, 0, Y1, links.part(2)), fx2.at[Y1], xm)
    d3 = send(along_z(2, 0, Y1, links.part(1)), nx2.at[0, Y1], xp)
    d4 = send(along_z(2, 0, Y0, links.part(3)), nx2.at[1, Y0], xm)
    yield 46
    received(c3, c4, c5, c6)
    for k in range(2):
        accumulate(16, block_x(k, 0), plain(nx.at[0, k]), plain(nx.at[1, k]))
    f1 = send(along_z(0, 2, every, here), fz.at[0], zp)
    f2 = send(along_z(1, 2, every, here), fz.at[1], zm)
    f3 = send(along_z(1, 1, every, here), nz.at[0, 1], zp)
    f4 = send(along_z(0, 3, every, here), nz.at[1, 0], zm)
    received(d1)
    accumulate(2, block_z(2, 0, links.part(1)), shift(fx2))
    d5 = send(along_z(2, 0, Y0, links.part(1)), nx2.at[0, Y0], xp)
    received(d2)
    accumulate(2, block_z(2, 0, links.part(3), 2), shift(fx2, 2))
    d6 = send(along_z(2, 0, Y1, links.part(3)), nx2.at[1, Y1], xm)
    yield 52
    received(f1)
    accumulate(4, block_z(0, 1, here), shift(fz.at[0]))
    f5 = send(along_z(0, 1, every, here), nz.at[0, 0], zp)
    received(f2)
    accumulate(4, block_z(1, 3, here), shift(fz.at[1]))
    f6 = send(along_z(1, 3, every, here), nz.at[1, 1], zm)
    yield 58
    received(d3, d4, d5, d6)
    accumulate(4, block_z(2, 0, here), shift(nx2.at[0]), shift(nx2.at[1]))
    received(f3, f4, f5, f6)
    for k in range(2):
        accumulate(4, block_z(k, 0, here), shift(nz.at[0, k]), shift(nz.at[1, k]))
    for k in range(3):
        shard[k] = along_z(k, 0, every, here)[...]
    sent(copies)


def regather(links, at, half, times):
    xp, xm, side = links.to(x=1), links.to(x=3), links.to(sibling=True)
    beside = (lax.rem(lax.axis_index("dp") + 8, 16), lax.axis_index("seq"))
    copies, sides = [], []

    def send(ref, where):
        copies.append(links.start(ref, ref, where))
        return copies[-1]

    def share(ref):
        sides.append(send(ref, side))

    z = send(at(0, 0), beside)
    near = [(send(at(0, 0), xp), send(at(0, 0), xm))]
    share(at(0, 0))
    yield times[0]
    received(z)
    near.append((send(at(1, 0), xp), send(at(1, 0), xm)))
    share(at(1, 0))
    for i in range(2):
        yield times[1 + 2 * i]
        received(near[i][0])
        far_up = send(half(at(i, 3), 0), xp)
        share(at(i, 3))
        received(near[i][1])
        far_down = send(half(at(i, 1), 1), xm)
        share(at(i, 1))
        yield times[2 + 2 * i]
        received(far_up, far_down)
        share(at(i, 2))
    received(*sides)
    sent(copies)


def collect(links, shard, out, local, late):
    copies = []

    def own(y):
        return out.at[:, y, links.core, links.z_lo, links.part(0)]

    keep = pltpu.make_async_copy(shard.at[:, links.y], own(links.y), local)
    keep.start()
    for step in (2, 1, 3):
        there = lax.rem(links.y + step, 4)
        copies.append(links.start(shard.at[:, there], own(links.y), links.to(y=step)))
    yield 7
    keep.wait()
    received(*copies)

    def at(z, x):
        return out.at[:, :, links.core, lax.rem(links.z_lo + z, 2), links.part(x)]

    def half(ref, i):
        return ref.at[:, pl.ds(2 * i, 2)]

    yield from regather(links, at, half, [t + late for t in (12, 18, 24, 32, 45)])
    sent(copies)


SHARE_SCRATCH = (
    pltpu.VMEM((2, 2, 4, 512, 256), BF16),
    pltpu.VMEM((2, 4, 512, 256), BF16),
    pltpu.VMEM((2, 512, 256), BF16),
    pltpu.VMEM((2, 2, 512, 256), BF16),
    pltpu.VMEM((512, 256), BF16),
)


def share(links, bufs, out, late):
    q, from_side, far, near, from_z = bufs
    xp, xm, side = links.to(x=1), links.to(x=3), links.to(sibling=True)
    beside = (lax.rem(lax.axis_index("dp") + 8, 16), lax.axis_index("seq"))
    core, z_lo = links.core, links.z_lo
    copies = []

    def send(src, dst, where):
        copies.append(links.start(src, dst, where))
        return copies[-1]

    def there(x):
        return lax.rem(links.x + x, 4)

    def rows(ref):
        return lambda i: ref.at[pl.ds(pl.multiple_of(i * 64, 64), 64)]

    s = send(q.at[1 - core], from_side, side)
    yield late
    received(s)
    for z in range(2):
        for x in range(4):
            accumulate(8, rows(q.at[core, z, x]), rows(from_side.at[z, x]))
    a1, a2 = send(q.at[core, 0, there(2)], far.at[0], xp), send(q.at[core, 1, there(2)], far.at[1], xm)
    a3 = send(q.at[core, 1, there(1)], near.at[0, 1], xp)
    a4 = send(q.at[core, 0, there(3)], near.at[1, 0], xm)
    yield late + 8
    received(a1)
    accumulate(8, rows(q.at[core, 0, there(1)]), rows(far.at[0]))
    a5 = send(q.at[core, 0, there(1)], near.at[0, 0], xp)
    received(a2)
    accumulate(8, rows(q.at[core, 1, there(3)]), rows(far.at[1]))
    a6 = send(q.at[core, 1, there(3)], near.at[1, 1], xm)
    yield late + 20
    received(a3, a4, a5, a6)
    for z in range(2):
        accumulate(8, rows(q.at[core, z, there(0)]), rows(near.at[0, z]), rows(near.at[1, z]))
    b = send(q.at[core, 1 - z_lo, there(0)], from_z, beside)
    yield late + 26
    received(b)

    def finish(i, carry):
        at = pl.ds(pl.multiple_of(i * 64, 64), 64)
        value = q[core, z_lo, links.x, at].astype(F32) + from_z[at].astype(F32)
        out[core, z_lo, links.x, at] = value.astype(BF16)
        return carry

    lax.fori_loop(0, 8, finish, 0)

    def at(z, x):
        return out.at[core, lax.rem(z_lo + z, 2), there(x)]

    def half(ref, i):
        return ref.at[pl.ds(256 * i, 256)]

    yield from regather(links, at, half, [t + late for t in (33, 36, 42, 46, 54)])
    sent(copies)


def agree(links, vec, bufs):
    y, x = links.y, links.x
    copies = []
    steps = (
        links.to(sibling=True),
        links.to(y=1 + 2 * lax.rem(y, 2)),
        links.to(y=2),
        links.to(z=2),
        links.to(x=1 + 2 * lax.rem(x, 2)),
        links.to(x=2),
        (lax.rem(lax.axis_index("dp") + 8, 16), lax.axis_index("seq")),
    )
    held, got = bufs
    held[0] = vec[...]
    for i, where in enumerate(steps):
        copies.append(links.start(held.at[i], got.at[i], where))
        yield 6 + 6 * i
        received(copies[-1])
        if i < len(steps) - 1:
            held[i + 1] = held[i] + got[i]
        else:
            vec[...] = held[i] + got[i]
    sent(copies)


def dot(a, b):
    return jnp.dot(a, b, preferred_element_type=F32)


def dot_t(a, b):
    return lax.dot_general(a, b, (((1,), (1,)), ((), ())), preferred_element_type=F32)


def dot_rows(a, b):
    return lax.dot_general(a, b, (((0,), (0,)), ((), ())), preferred_element_type=F32)


def pair_of(ref, pair):
    return jnp.concatenate([ref[pair[0]], ref[pair[1]]], axis=0)


def by_chunks(body):
    def step(i, carry):
        body(pl.ds(pl.multiple_of(i * 16, 16), 16))
        return carry

    lax.fori_loop(0, ROWS // 16, step, 0)


def norm_parts(row_total):
    center = row_total - jnp.mean(row_total, axis=-1, keepdims=True)
    spread = jnp.mean(center * center, axis=-1, keepdims=True)
    inverse = lax.rsqrt(spread + norm_eps)
    return center * inverse, inverse


def norm_backward(grad_result, unit, inverse, gain):
    grad_unit = grad_result * gain
    return inverse * (
        grad_unit
        - jnp.mean(grad_unit, axis=-1, keepdims=True)
        - unit * jnp.mean(grad_unit * unit, axis=-1, keepdims=True)
    )


def rows8(values):
    return values[0:8] + values[8:16]


VMEM = pl.BlockSpec(memory_space=pltpu.VMEM)
HBM = pl.BlockSpec(memory_space=pl.ANY)
SMEM = pl.BlockSpec(memory_space=pltpu.SMEM)
KINDS = {"v": VMEM, "s": SMEM, "h": HBM}


def call(body, name, ident, outs, operands, spaces, scratch, copies, flops=0):
    sems = [pltpu.SemaphoreType.DMA((copies,)), pltpu.SemaphoreType.DMA((copies,))]
    return pl.pallas_call(
        body,
        name=name,
        out_shape=tuple(jax.ShapeDtypeStruct(s, d) for s, d, _ in outs),
        in_specs=[KINDS[k] for k in spaces],
        out_specs=tuple(KINDS[k] for _, _, k in outs),
        scratch_shapes=[*scratch, *sems],
        compiler_params=pltpu.CompilerParams(
            collective_id=ident, has_side_effects=True, vmem_limit_bytes=VMEM_BYTES
        ),
        cost_estimate=pl.CostEstimate(flops=flops, bytes_accessed=20_000_000, transcendentals=0),
    )(*operands)


def piece_kernel(place_ref, gate_up_ref, down_ref, out_ref):
    chunk = (pl.program_id(0) * 2 + place_ref[0]) * 4 + place_ref[1]
    total = place_ref[3]
    row = lax.broadcasted_iota(jnp.int32, (PART, 128), 0) + chunk * PART
    inside = row < total
    both = gate_up_ref[...].astype(F32)
    out_ref[0, 0] = jnp.where(inside, both[:, 0], 0.0).astype(BF16)
    out_ref[0, 1] = jnp.where(inside, both[:, 1], 0.0).astype(BF16)
    out_ref[0, 2] = jnp.where(inside, down_ref[...].astype(F32), 0.0).astype(BF16)


def piece_of(gate_up, down, place):
    def chunk(y, place):
        return (y * 2 + place[0]) * 4 + place[1]

    return pl.pallas_call(
        piece_kernel,
        name="piece",
        grid_spec=pltpu.PrefetchScalarGridSpec(
            num_scalar_prefetch=1,
            grid=(4,),
            in_specs=[
                pl.BlockSpec((PART, 2, 128), lambda y, p: (chunk(y, p), 0, p[2])),
                pl.BlockSpec((PART, 128), lambda y, p: (chunk(y, p), p[2])),
            ],
            out_specs=pl.BlockSpec((1, 3, PART, 128), lambda y, p: (y, 0, 0, 0)),
        ),
        out_shape=jax.ShapeDtypeStruct((4, 3, PART, 128), BF16),
    )(place, gate_up, down)


def project_kernel(
    x_ref, w_ref, cos_ref, sin_ref, piece_ref, all_ref, q_ref, k_ref, v_ref, w_all_ref, local, send, recv
):
    links = Links(send, recv)
    all_ref[0] = x_ref[...]
    to = links.to
    links.barrier(to(y=1), to(y=3), to(z=2), to(y=2), to(x=1), to(x=3), to(z=1), to(z=3))

    def work(pair):
        rows = pair_of(all_ref, pair)
        for part, out in enumerate((q_ref, k_ref, v_ref)):
            result = dot(rows, w_ref[part])
            for i, slot in enumerate(pair):
                at = pl.ds(links.first_row(slot), ROWS)
                piece = result[i * ROWS : (i + 1) * ROWS]
                if part == 2:
                    out[at] = piece.astype(BF16)
                    continue
                cosine, sine = cos_ref[at], sin_ref[at]
                for head in range(2):
                    lanes = slice(head * 128, head * 128 + 128)
                    turned = piece[:, lanes] * cosine + pltpu.roll(piece[:, lanes], 64, 1) * sine
                    if part == 0:
                        turned = turned * HEAD_DIM**-0.5
                    out[at, lanes] = turned.astype(BF16)

    together(gather(links, all_ref, work), spread(links, piece_ref, w_all_ref, local))


def attend_kernel(prefix_ref, q_ref, k_ref, v_ref, out_ref, lse_ref):
    block = q_ref.shape[0]
    first = pl.program_id(1) * block
    scores = dot_t(k_ref[...], q_ref[...])
    key = lax.broadcasted_iota(jnp.int32, scores.shape, 0)
    query = lax.broadcasted_iota(jnp.int32, (1, block), 1) + first
    limit = jnp.maximum(query, prefix_ref[0] - 1)
    scores = jnp.where(key <= limit, scores, -1e30)
    peak = jnp.max(scores, axis=0, keepdims=True)
    exponent = jnp.exp(scores - peak)
    total = jnp.sum(exponent, axis=0, keepdims=True)
    weights = (exponent * (1.0 / total)).astype(BF16)
    out_ref[...] = dot_rows(weights, v_ref[...]).astype(BF16)
    lse_ref[0] = peak + jnp.log(total)


def attend(prefix, q, k, v):
    block = 512
    return pl.pallas_call(
        attend_kernel,
        name="attend",
        grid=(2, LEN // block),
        in_specs=[
            SMEM,
            pl.BlockSpec((block, 128), lambda h, b: (b, h)),
            pl.BlockSpec((LEN, 128), lambda h, b: (0, h)),
            pl.BlockSpec((LEN, 128), lambda h, b: (0, h)),
        ],
        out_specs=(
            pl.BlockSpec((block, 128), lambda h, b: (b, h)),
            pl.BlockSpec((1, 1, block), lambda h, b: (h, 0, b)),
        ),
        out_shape=(
            jax.ShapeDtypeStruct((LEN, 256), BF16),
            jax.ShapeDtypeStruct((2, 1, LEN), F32),
        ),
        compiler_params=pltpu.CompilerParams(vmem_limit_bytes=VMEM_BYTES),
    )(prefix, q, k, v)


def attend_back_kernel(
    prefix_ref, q_ref, k_ref, v_ref, g_ref, lse_ref, cos_ref, sin_ref, cosq_ref, sinq_ref,
    dq_ref, dk_ref, dv_ref, dk_sum, dv_sum
):
    block = q_ref.shape[0]
    step = pl.program_id(1)
    scores = dot_t(k_ref[...], q_ref[...])
    key = lax.broadcasted_iota(jnp.int32, scores.shape, 0)
    query = lax.broadcasted_iota(jnp.int32, (1, block), 1) + step * block
    limit = jnp.maximum(query, prefix_ref[0] - 1)
    weights = jnp.where(key <= limit, jnp.exp(scores - lse_ref[0]), 0.0)
    grad_weights = dot_t(v_ref[...], g_ref[...])
    inner = jnp.sum(weights * grad_weights, axis=0, keepdims=True)
    grad_scores = (weights * (grad_weights - inner)).astype(BF16)
    d_query = dot_rows(grad_scores, k_ref[...]) * HEAD_DIM**-0.5
    dq_ref[...] = (d_query * cosq_ref[...] - pltpu.roll(d_query, 64, 1) * sinq_ref[...]).astype(BF16)
    d_key = dot(grad_scores, q_ref[...])
    d_value = dot(weights.astype(BF16), g_ref[...])

    @pl.when(step == 0)
    def _():
        dk_sum[...] = d_key
        dv_sum[...] = d_value

    @pl.when(step > 0)
    def _():
        dk_sum[...] += d_key
        dv_sum[...] += d_value

    @pl.when(step == pl.num_programs(1) - 1)
    def _():
        total = dk_sum[...]
        dk_ref[...] = (total * cos_ref[...] - pltpu.roll(total, 64, 1) * sin_ref[...]).astype(BF16)
        dv_ref[...] = dv_sum[...].astype(BF16)


def attend_back(prefix, q, k, v, g, lse, cosine, sine):
    block = 512
    part = pl.BlockSpec((block, 128), lambda h, b: (b, h))
    whole = pl.BlockSpec((LEN, 128), lambda h, b: (0, h))
    table = pl.BlockSpec((LEN, 128), lambda h, b: (0, 0))
    table_part = pl.BlockSpec((block, 128), lambda h, b: (b, 0))
    return pl.pallas_call(
        attend_back_kernel,
        name="attend_back",
        grid=(2, LEN // block),
        in_specs=[
            SMEM, part, whole, whole, part,
            pl.BlockSpec((1, 1, block), lambda h, b: (h, 0, b)),
            table, table, table_part, table_part,
        ],
        out_specs=(part, whole, whole),
        out_shape=tuple(jax.ShapeDtypeStruct((LEN, 256), BF16) for _ in range(3)),
        scratch_shapes=[pltpu.VMEM((LEN, 128), F32), pltpu.VMEM((LEN, 128), F32)],
        compiler_params=pltpu.CompilerParams(vmem_limit_bytes=VMEM_BYTES),
    )(prefix, q, k, v, g, lse, cosine, sine, cosine, sine)


def attended_kernel(
    heads_ref, w_ref, x_ref, gain_ref, bias_ref, normed_ref, unit_ref, inverse_ref, total, *rest
):
    bufs, (send, recv) = rest[:7], rest[7:]
    links = Links(send, recv)
    links.barrier(links.to(y=1), links.to(y=3), links.to(z=2))

    def compute(pair):
        rows = jnp.concatenate([heads_ref[pl.ds(links.first_row(s), ROWS)] for s in pair], axis=0)
        result = dot(rows, w_ref[...]).astype(BF16)
        for i, slot in enumerate(pair):
            bufs[0][slot] = result[i * ROWS : (i + 1) * ROWS]

    together(scatter(links, bufs, compute, total))

    def finish(at):
        unit, inverse = norm_parts(deep_alpha * x_ref[at].astype(F32) + total[at])
        unit_ref[at] = unit
        inverse_ref[at] = jnp.broadcast_to(inverse, (16, 128))
        normed_ref[at] = unit * gain_ref[...] + bias_ref[...]

    by_chunks(finish)


def load_weights(w_hbm, w, sem, parts):
    copies = []
    for k in range(parts):
        for i in range(16):
            src = w_hbm.at[k, lax.rem(i // 2, 2), i // 4, lax.rem(i, 2)]
            copies.append(
                pltpu.make_async_copy(src, w.at[k, pl.ds(0, FF), pl.ds(i * 128, 128)], sem.at[k, i])
            )
    for copy in copies:
        copy.start()
    for k in range(parts):
        w[k, FF:COLS] = jnp.zeros((COLS - FF, WIDE), BF16)
    return copies


def feed_kernel(
    normed_ref, cot_ref, weight_ref, w_hbm, gain_ref, bias_ref,
    out_ref, all_ref, gz_all_ref, act_ref, gz_ref, vec_ref,
    w, gelu_ref, slope, total, w_sem, *rest,
):
    bufs, (send, recv) = rest[:4], rest[4:]
    links = Links(send, recv)
    loads = load_weights(w_hbm, w, w_sem, 3)

    def to_low(at):
        all_ref[0, at] = normed_ref[at].astype(BF16)

    by_chunks(to_low)
    links.barrier(links.to(y=1), links.to(y=3), links.to(sibling=True))
    for copy in loads:
        copy.wait()

    def forward(pair):
        rows = pair_of(all_ref, pair)
        for c in range(0, COLS, 256):
            cols = slice(c, c + 256)
            gate = dot_t(rows, w[0, cols])
            up = dot_t(rows, w[1, cols])
            bell = 0.5 + 0.5 * lax.erf(gate * np.float32(np.sqrt(0.5)))
            gelu = gate * bell
            turn = bell + gate * (jnp.exp(-0.5 * gate * gate) * np.float32(1.0 / np.sqrt(2.0 * np.pi)))
            hidden = (gelu * up).astype(BF16)
            turn = turn * up
            for i, slot in enumerate(pair):
                part = slice(i * ROWS, (i + 1) * ROWS)
                gelu_ref[slot, :, cols] = gelu[part]
                slope[slot, :, cols] = turn[part]
                act_ref[slot, :, 2 * COLS + c : 2 * COLS + c + 256] = hidden[part]

    together(gather_near(links, all_ref, forward))

    def compute(pair):
        rows = jnp.concatenate([act_ref[slot, :, 2 * COLS :] for slot in pair], axis=0)
        for d in range(0, WIDE, 512):
            result = dot(rows, w[2, :, d : d + 512]).astype(BF16)
            for i, slot in enumerate(pair):
                bufs[0][slot, :, d : d + 512] = result[i * ROWS : (i + 1) * ROWS]

    together(scatter_near(links, bufs, compute, total))
    vec_ref[...] = jnp.zeros_like(vec_ref)

    def finish(at):
        unit, inverse = norm_parts(deep_alpha * normed_ref[at] + total[at])
        out_ref[at] = (unit * gain_ref[...] + bias_ref[...]).astype(BF16)
        grad = cot_ref[at].astype(F32) * weight_ref[0]
        grad_z = norm_backward(grad, unit, inverse, gain_ref[...])
        gz_ref[at] = grad_z
        gz_all_ref[0, at] = grad_z.astype(BF16)
        vec_ref[0] += rows8(grad * unit)
        vec_ref[1] += rows8(grad)

    by_chunks(finish)

    def backward(pair):
        rows = pair_of(gz_all_ref, pair)
        for c in range(0, COLS, 256):
            cols = slice(c, c + 256)
            grad_hidden = dot_t(rows, w[2, cols])
            for i, slot in enumerate(pair):
                part = grad_hidden[i * ROWS : (i + 1) * ROWS]
                act_ref[slot, :, cols] = (part * slope[slot, :, cols]).astype(BF16)
                act_ref[slot, :, COLS + c : COLS + c + 256] = (part * gelu_ref[slot, :, cols]).astype(BF16)

    together(gather_near(links, gz_all_ref, backward))


def feed_back_kernel(
    act_ref, gz_ref, w_hbm, g_hbm, unit_ref, inverse_ref, gain_ref, w_out_ref,
    gz1_ref, all_ref, grad_heads_ref, vec_ref, shard_ref,
    w, total, w_sem, g_sem, *rest,
):
    bufs, more, (send, recv) = rest[:4], rest[4:13], rest[13:]
    links = Links(send, recv)
    loads = load_weights(w_hbm, w, w_sem, 2)
    for k in range(3):
        for i in range(16):
            dst = more[0].at[k, lax.rem(i // 2, 2), i // 4, lax.rem(i, 2)]
            src = g_hbm.at[k, pl.ds(0, FF), pl.ds(i * 128, 128)]
            loads.append(pltpu.make_async_copy(src, dst, g_sem.at[k, i]))
            loads[-1].start()
    to = links.to
    links.barrier(
        to(y=1), to(y=3), to(z=2), to(x=1), to(x=3), to(z=1), to(z=3), to(sibling=True)
    )
    for copy in loads:
        copy.wait()

    def compute(pair):
        rows = jnp.concatenate([act_ref[slot, :, : 2 * COLS] for slot in pair], axis=0)
        for d in range(0, WIDE, 512):
            cols = slice(d, d + 512)
            result = dot(rows[:, :COLS], w[0, :, cols]) + dot(rows[:, COLS:], w[1, :, cols])
            result = result.astype(BF16)
            for i, slot in enumerate(pair):
                bufs[0][slot, :, cols] = result[i * ROWS : (i + 1) * ROWS]

    def finish(at):
        grad = deep_alpha * gz_ref[at] + total[at]
        unit = unit_ref[at]
        grad_z = norm_backward(grad, unit, inverse_ref[at][:, 0:1], gain_ref[...])
        gz1_ref[at] = grad_z
        all_ref[0, at] = grad_z.astype(BF16)
        vec_ref[0] += rows8(grad * unit)
        vec_ref[1] += rows8(grad)

    def work(pair):
        result = dot_t(pair_of(all_ref, pair), w_out_ref[...]).astype(BF16)
        for i, slot in enumerate(pair):
            grad_heads_ref[pl.ds(links.first_row(slot), ROWS)] = result[i * ROWS : (i + 1) * ROWS]

    def chain():
        yield from scatter_near(links, bufs, compute, total)
        vec_ref[...] = jnp.zeros_like(vec_ref)
        by_chunks(finish)
        for time in gather(links, all_ref, work):
            yield time + 22

    together(reduce(links, more, shard_ref), chain())


def input_kernel(
    dq_ref, dk_ref, dv_ref, w_ref, gz1_ref, tokens_ref, heads_ref, gz_all_ref, shard_ref, vec_in_ref,
    out_ref, q_out_ref, vec_ref, feed_ref,
    total, grads, heads, held, got, local, *rest,
):
    bufs, more, (send, recv) = rest[:7], rest[7:12], rest[12:]
    links = Links(send, recv)
    to = links.to
    beside = (lax.rem(lax.axis_index("dp") + 8, 16), lax.axis_index("seq"))
    links.barrier(
        to(y=1), to(y=2), to(y=3), to(z=2), to(x=1), to(x=2), to(x=3), to(sibling=True), beside
    )
    for slot in range(8):
        at = pl.ds(links.first_row(slot), ROWS)
        heads[slot] = heads_ref[at]
        for part, ref in enumerate((dq_ref, dk_ref, dv_ref)):
            grads[slot, :, part * 256 : part * 256 + 256] = ref[at]
    vec_ref[...] = vec_in_ref[...]

    def compute(pair):
        rows = pair_of(grads, pair)
        result = 0.0
        for part in range(3):
            result = result + dot_t(rows[:, part * 256 : part * 256 + 256], w_ref[part])
        result = result.astype(BF16)
        for i, slot in enumerate(pair):
            bufs[0][slot] = result[i * ROWS : (i + 1) * ROWS]

    def qkv():
        flat = more[0]
        right = grads[...].reshape(LEN, 768)
        for d in range(8):
            left = tokens_ref[:, :, d * 256 : d * 256 + 256].reshape(LEN, 256)
            result = dot_rows(left, right).astype(BF16)
            for part in range(3):
                chunk = part * 4 + d // 2
                flat[chunk // 8, chunk // 4 % 2, chunk % 4, d % 2 * 256 : d % 2 * 256 + 256] = result[
                    :, part * 256 : part * 256 + 256
                ]
        result = dot_rows(heads[...].reshape(LEN, 256), gz_all_ref[...].reshape(LEN, WIDE)).astype(BF16)
        for d in range(8):
            chunk = 12 + d // 2
            flat[chunk // 8, chunk // 4 % 2, chunk % 4, d % 2 * 256 : d % 2 * 256 + 256] = result[
                :, d * 256 : d * 256 + 256
            ]

    def shared():
        yield 9
        qkv()
        yield from share(links, more, q_out_ref, 16)

    together(
        collect(links, shard_ref, feed_ref, local, 0),
        scatter(links, bufs, compute, total),
        shared(),
        agree(links, vec_ref, (held, got)),
    )

    def finish(at):
        out_ref[at] = deep_alpha * gz1_ref[at] + total[at]

    by_chunks(finish)


def feed_weight_kernel(act_ref, normed_ref, gz_ref, out_ref):
    @pl.when(pl.program_id(0) < 6)
    def _():
        out_ref[0] = dot_rows(act_ref[...], normed_ref[...]).astype(BF16)

    @pl.when(pl.program_id(0) >= 6)
    def _():
        out_ref[0] = dot_rows(act_ref[...], gz_ref[...]).astype(BF16)


def feed_weights(act, normed_all, gz_all):
    flat = lambda v: v.reshape(LEN, v.shape[-1])
    return pl.pallas_call(
        feed_weight_kernel,
        name="feed_weights",
        grid=(9,),
        in_specs=[pl.BlockSpec((LEN, 256), lambda i: (0, i)), VMEM, VMEM],
        out_specs=pl.BlockSpec((1, 256, WIDE), lambda i: (i // 3, i % 3, 0)),
        out_shape=jax.ShapeDtypeStruct((3, COLS, WIDE), BF16),
        compiler_params=pltpu.CompilerParams(vmem_limit_bytes=VMEM_BYTES),
    )(flat(act), flat(normed_all), flat(gz_all))


def feed_out_kernel(feed_ref, gate_up_ref, down_ref):
    for z in range(2):
        lanes = slice(z * 128, z * 128 + 128)
        gate_up_ref[:, 0, lanes] = feed_ref[0, 0, 0, z].astype(F32)
        gate_up_ref[:, 1, lanes] = feed_ref[1, 0, 0, z].astype(F32)
        down_ref[:, lanes] = feed_ref[2, 0, 0, z].astype(F32)


def feed_out(feed, total):
    return pl.pallas_call(
        feed_out_kernel,
        name="feed_out",
        grid=(8,),
        in_specs=[pl.BlockSpec((3, 1, 1, 2, FF, 128), lambda i: (0, i // 2, i % 2, 0, 0, 0))],
        out_specs=(
            pl.BlockSpec((FF, 2, 256), lambda i: (i, 0, 0)),
            pl.BlockSpec((FF, 256), lambda i: (i, 0)),
        ),
        out_shape=(
            jax.ShapeDtypeStruct((total, 2, 256), F32),
            jax.ShapeDtypeStruct((total, 256), F32),
        ),
        compiler_params=pltpu.CompilerParams(vmem_limit_bytes=VMEM_BYTES),
    )(feed)


def on_device(
    tokens, cotangent, w_qkv, w_out, w_gate_up, w_down,
    attn_gain, attn_bias, ffn_gain, ffn_bias, prefix_len, clusters,
):
    x = tokens.reshape(ROWS, WIDE)
    cot = cotangent.reshape(ROWS, WIDE)
    dp, seq = lax.axis_index("dp"), lax.axis_index("seq")
    own_id = lax.dynamic_slice_in_dim(clusters, dp, 1)
    seq_weight = 1.0 / jnp.sum((own_id[:, None] == clusters[None, :]).astype(F32), axis=1)
    cosine, sine = (jnp.asarray(t) for t in rotary_tables(LEN, HEAD_DIM))
    row = lambda v: v.reshape(1, WIDE)
    ff_total = w_down.shape[1]
    place = jnp.stack([dp % 2, dp // 2 % 4, dp // 8, jnp.int32(ff_total)]).astype(jnp.int32)
    piece = piece_of(w_gate_up.transpose(2, 1, 0), w_down.T, place)
    w_in = w_qkv.transpose(1, 0, 2)
    low, full = BF16, F32
    blocks = (8, ROWS, WIDE)

    tokens_all, q, k, v, ffn_w = call(
        project_kernel, "project", 0,
        [(blocks, low, "v")] + [((LEN, 256), low, "v")] * 3 + [((3, 2, 4, 2, FF, 128), low, "h")],
        (x, w_in, cosine, sine, piece), "vvvvv", (pltpu.SemaphoreType.DMA,), 67,
        2 * LEN * WIDE * 768,
    )
    heads_out, lse = attend(prefix_len, q, k, v)
    normed, unit_one, inverse_one = call(
        attended_kernel, "attended", 1,
        [((ROWS, WIDE), full, "v"), ((ROWS, WIDE), full, "v"), ((ROWS, 128), full, "v")],
        (heads_out, w_out, x, row(attn_gain), row(attn_bias)), "vvvvv",
        (pltpu.VMEM((ROWS, WIDE), F32), *SCATTER_SCRATCH), 19, 2 * LEN * WIDE * 256,
    )
    output, normed_all, gz_all, act, grad_z2, ffn_vec = call(
        feed_kernel, "feed", 2,
        [
            ((ROWS, WIDE), low, "v"), (blocks, low, "v"), (blocks, low, "v"),
            ((8, ROWS, 3 * COLS), low, "v"), ((ROWS, WIDE), full, "v"), ((2, 8, WIDE), full, "v"),
        ],
        (normed, cot, seq_weight, ffn_w, row(ffn_gain), row(ffn_bias)), "vvshvv",
        (
            pltpu.VMEM((3, COLS, WIDE), BF16), pltpu.VMEM((8, ROWS, COLS), F32),
            pltpu.VMEM((8, ROWS, COLS), F32), pltpu.VMEM((ROWS, WIDE), F32),
            pltpu.SemaphoreType.DMA((3, 16)), *NEAR_SCRATCH,
        ),
        34, 2 * LEN * WIDE * COLS * 4,
    )
    ffn_grad = feed_weights(act, normed_all, gz_all)
    grad_z1, gz1_all, grad_heads, attn_vec, shard = call(
        feed_back_kernel, "feed_back", 3,
        [
            ((ROWS, WIDE), full, "v"), (blocks, low, "v"), ((LEN, 256), low, "v"),
            ((2, 8, WIDE), full, "v"), ((3, 4, PART, 128), low, "v"),
        ],
        (act, grad_z2, ffn_w, ffn_grad, unit_one, inverse_one, row(attn_gain), w_out), "vvhhvvvv",
        (
            pltpu.VMEM((2, COLS, WIDE), BF16), pltpu.VMEM((ROWS, WIDE), F32),
            pltpu.SemaphoreType.DMA((2, 16)), pltpu.SemaphoreType.DMA((3, 16)),
            *NEAR_SCRATCH, *REDUCE_SCRATCH,
        ),
        52, 2 * LEN * WIDE * COLS * 2,
    )
    dq, dk, dv = attend_back(prefix_len, q, k, v, grad_heads, lse, cosine, sine)
    vec = jnp.concatenate([attn_vec.sum(1), ffn_vec.sum(1), jnp.zeros((4, WIDE), F32)], axis=0)
    steps = pltpu.VMEM((7, 8, WIDE), F32)
    input_grad, qkv_out, vec, ffn_whole = call(
        input_kernel, "input", 4,
        [
            ((ROWS, WIDE), full, "v"), ((2, 2, 4, 512, 256), low, "v"), ((8, WIDE), full, "v"),
            ((3, 4, 2, 2, FF, 128), low, "h"),
        ],
        (dq, dk, dv, w_in, grad_z1, tokens_all, heads_out, gz1_all, shard, vec), "vvvvvvvvvv",
        (
            pltpu.VMEM((ROWS, WIDE), F32), pltpu.VMEM((8, ROWS, 768), BF16),
            pltpu.VMEM((8, ROWS, 256), BF16), steps, steps, pltpu.SemaphoreType.DMA,
            *SCATTER_SCRATCH, *SHARE_SCRATCH,
        ),
        77, 2 * LEN * WIDE * 768,
    )
    grad_gate_up, grad_down = feed_out(ffn_whole, ff_total)
    qkv_out = qkv_out.reshape(8192, 256).astype(F32)
    grad_qkv = qkv_out[:6144].reshape(3, WIDE, 256).transpose(1, 0, 2)
    grad_out = qkv_out[6144:].reshape(8, 256, 256).transpose(1, 0, 2).reshape(256, WIDE)
    own = lax.dynamic_slice_in_dim(vec, seq * 256, 256, axis=1)
    return (
        output.reshape(tokens.shape),
        input_grad.reshape(tokens.shape),
        grad_qkv,
        grad_out,
        grad_gate_up.transpose(2, 1, 0),
        grad_down.T,
        own[0],
        own[1],
        own[2],
        own[3],
    )


def solution(mesh):
    return jax.shard_map(
        on_device,
        mesh=mesh,
        in_specs=(
            P("seq", "dp", None), P("seq", "dp", None), P(None, None, "seq"), P("seq", None),
            P("seq", None, None), P("seq", None), P(), P(), P(), P(), P("dp"), P(),
        ),
        out_specs=(
            P("seq", "dp", None), P("seq", "dp", None), P(None, None, "seq"), P("seq", None),
            P("seq", None, None), P("seq", None), P("seq"), P("seq"), P("seq"), P("seq"),
        ),
        check_vma=False,
    )
```

time: 849 us -> 484 us (0.57)
  waiting for transfers between devices: 283 us -> 0 us
  Pallas kernels: 324 us -> 454 us
  local copies, waits for them, and re-layouts: 120 us -> 11.7 us
  blocking collectives: 64 us -> 0 us
  between operations: 16.1 us -> 2.49 us
  other arithmetic: 20.8 us -> 7.95 us
  matrix products: 10.1 us -> 0 us
    reduce_scatter x3 -> x0, waiting for transfers between devices: 174 us -> none  [the longest x2 95.5 us: over_dp(): lax.psum_scatter(value.astype(BF16), 'dp', scatter_dimension=0, tiled=True)]
    pallas_call x5, Pallas kernels: 286 us -> 398 us  [call(): pl.pallas_call(body, name=name, out_shape=tuple((jax.ShapeDtypeStruct(s,...]
    all_gather x4 -> x0, waiting for transfers between devices: 86.5 us -> none  [the longest x1 47.1 us: on_device(): ffn_whole = lax.all_gather(ffn_part, 'dp', axis=0)]
    unnamed x27 -> x5, local copies, waits for them, and re-layouts: 48.7 us -> 5.67 us
    all_to_all x2 -> x0, blocking collectives: 34.9 us -> none  [the longest x1 19.3 us: on_device(): lax.all_to_all(piece, 'seq', split_axis=0, concat_axis=0, tiled=True)]
    psum x1 -> x0, blocking collectives: 29.1 us -> none  [on_device(): vec = lax.psum(vec, 'dp')]
    reshape x3 -> x0, local copies, waits for them, and re-layouts: 24.4 us -> none  [the longest x1 14.1 us: on_device(): ffn_whole.transpose(0, 3, 2, 1, 4).reshape(256, 3, 8 * COLS)]
    unnamed x9 -> x0, waiting for transfers between devices: 22.3 us -> none
  transfers between devices with their start and end apart: 8 -> 0, of which waited for: 7 -> 0; matrix products, arithmetic and copies ran while one was open for 6% -> 0% of each run, Pallas kernels for 20% -> 0%
where the time goes in v2:
time: 484 us; the launch traced here: 476 us
  Pallas kernels  454 us (94%)
  local copies, waits for them, and re-layouts  11.7 us (2%)
  other arithmetic  7.95 us (2%)
    pallas_call x5, Pallas kernels, call(): pl.pallas_call(body, name=name, out_shape=tuple((jax.ShapeDtypeStruct(s,...  398 us
    pallas_call x1, Pallas kernels, feed_weights(): pl.pallas_call(feed_weight_kernel, name='feed_weights', grid=(9,), in_spe...  16.9 us
    pallas_call x1, Pallas kernels, attend_back(): pl.pallas_call(attend_back_kernel, name='attend_back', grid=(2, LEN // bl...  13.5 us
    pallas_call x1, Pallas kernels, feed_out(): pl.pallas_call(feed_out_kernel, name='feed_out', grid=(8,), in_specs=[pl....  13.2 us

profile of v2, /device:TPU:1, one launch (start us, length us, event | category | flops | bytes accessed | tf_op | source)
XLA Modules:
  0.0 476.0 jit_solution(16128834962403227090)
XLA Ops:
  1.3 0.6 pad_add_fusion.place_ref
  1.9 1.2 dynamic_slice.6
  3.2 1.9 fusion
  5.8 0.1 pad.2.clone
  5.8 4.2 piece.1.piece_ref
  10.1 83.2 %project.1 = (bf16[8,128,2048]{2,1,0:T(8,128)(2,1)}, bf16[1024,256]{1,0:T(8,128)(2,1)}, bf16[1024,256]{1,0:T(8,128)(2,1)}, bf16[1024,256]{1,0:T(8,128)(2,1)}, bf16[3,2,4,2,704,128]{5,4,3,2,1,0:T(8,128)(2,1)}) custom-call(bf16[128,2048]{1,0:T(8,128)(2,1)} %bitcast.57, bf16[3,2048,256]{2,1,0:T(8,128)(2,1)} %bitcast.43, ...), custom_call_target="tpu_custom_call" | custom-call | flops 3221225472 | bytes 20000000 | tf_op jit(solution)/shard_map/project/pallas_call | solution.py:749
  93.2 8.4 %attend.1 = (bf16[1024,256]{1,0:T(8,128)(2,1)}, f32[2,1,1024]{2,1,0:T(1,128)}) custom-call(s32[1]{0:T(128)S(6)} %copy.29.prefix_ref, bf16[1024,256]{1,0:T(8,128)(2,1)} %get-tuple-element.40.q_ref, bf16[1024,256]{1,0:T(8,128)(2,1)} %get-tuple-element.41.k_ref, bf16[1024,256]{1,0:T(8,128)(2,1)} %get-tuple-element.42.v_ref), custom_call_target="tpu_custom_call" | custom-call | tf_op jit(solution)/shard_map/attend/pallas_call | solution.py:841
  101.7 33.6 %attended.1 = (f32[128,2048]{1,0:T(8,128)}, f32[128,2048]{1,0:T(8,128)}, f32[128,128]{1,0:T(8,128)}) custom-call(bf16[1024,256]{1,0:T(8,128)(2,1)} %get-tuple-element.43.heads_ref, bf16[256,2048]{1,0:T(8,128)(2,1)} %w_out_ref.1, bf16[128,2048]{1,0:T(8,128)(2,1)} %bitcast.58, f32[1,2048]{1,0:T(1,128)} %bitcast.49, f32[1,2048]{1,0:T(1,128)} %bitcast.60), custom_call_target="tpu_custom_call" | custom-call | flops 1073741824 | bytes 20000000 | tf_op jit(solution)/shard_map/attended/pallas_call | solution.py:749
  135.2 97.5 %feed.1 = (bf16[128,2048]{1,0:T(8,128)(2,1)}, bf16[8,128,2048]{2,1,0:T(8,128)(2,1)}, bf16[8,128,2048]{2,1,0:T(8,128)(2,1)}, bf16[8,128,2304]{2,1,0:T(8,128)(2,1)...) custom-call(f32[128,2048]{1,0:T(8,128)} %get-tuple-element.44.normed_ref, bf16[128,2048]{1,0:T(8,128)(2,1)} %bitcast.59, ...), custom_call_target="tpu_custom_call" | custom-call | flops 12884901888 | bytes 20000000 | tf_op jit(solution)/shard_map/feed/pallas_call | solution.py:749
  232.8 1.0 reduce_sum.29
  233.7 16.9 %feed_weights.1.g_hbm = bf16[3,768,2048]{2,1,0:T(8,128)(2,1)} custom-call(bf16[1024,2304]{1,0:T(8,128)(2,1)} %bitcast.37, bf16[1024,2048]{1,0:T(8,128)(2,1)} %bitcast.41, bf16[1024,2048]{1,0:T(8,128)(2,1)} %bitcast.42), custom_call_target="tpu_custom_call" | custom-call | tf_op jit(solution)/shard_map/feed_weights/pallas_call | solution.py:1161
  250.6 78.2 %feed_back.1 = (f32[128,2048]{1,0:T(8,128)}, bf16[8,128,2048]{2,1,0:T(8,128)(2,1)}, bf16[1024,256]{1,0:T(8,128)(2,1)}, f32[2,8,2048]{2,1,0:T(8,128)}, bf16[3,4,176,128]{3,2,1,0:T(8,128)(2,1)}) custom-call(bf16[8,128,2304]{2,1,0:T(8,128)(2,1)} %get-tuple-element.47.act_ref, f32[128,2048]{1,0:T(8,128)} %get-tuple-element.48.gz_ref, ...), custom_call_target="tpu_custom_call" | custom-call | flops 6442450944 | bytes 20000000 | tf_op jit(solution)/shard_map/feed_back/pallas_call | solution.py:749
  328.8 13.5 %attend_back.1 = (bf16[1024,256]{1,0:T(8,128)(2,1)}, bf16[1024,256]{1,0:T(8,128)(2,1)}, bf16[1024,256]{1,0:T(8,128)(2,1)}) custom-call(s32[1]{0:T(128)S(6)} %copy.29.prefix_ref, bf16[1024,256]{1,0:T(8,128)(2,1)} %get-tuple-element.40.q_ref, bf16[1024,256]{1,0:T(8,128)(2,1)} %get-tuple-element.41.k_ref, bf16[1024,256]{1,0:T(8,128)(2,1)} %get-tuple-element.42.v_ref, ...), custom_call_target="tpu_custom_call" | custom-call | tf_op jit(solution)/shard_map/attend_back/pallas_call | solution.py:905
  342.3 1.0 reduce_sum.28
  343.2 0.7 maximum_maximum_fusion.vec_in_ref
  343.9 105.2 %input.1 = (f32[128,2048]{1,0:T(8,128)}, bf16[2,2,4,512,256]{4,3,2,1,0:T(8,128)(2,1)}, f32[8,2048]{1,0:T(8,128)}, bf16[3,4,2,2,704,128]{5,4,3,2,1,0:T(8,128)(2,1)}) custom-call(bf16[1024,256]{1,0:T(8,128)(2,1)} %get-tuple-element.55.dq_ref, bf16[1024,256]{1,0:T(8,128)(2,1)} %get-tuple-element.56.dk_ref, bf16[1024,256]{1,0:T(8,128)(2,1)} %get-tuple-element.57.dv_ref, ...), custom_call_target="tpu_custom_call" | custom-call | flops 3221225472 | bytes 20000000 | tf_op jit(solution)/shard_map/input/pallas_call | solution.py:749
  449.2 3.3 copy.25
  452.4 1.5 fusion.1
  453.9 2.8 bitcast_convert_fusion
  456.8 0.1 slice.25
  456.9 3.1 slice.24
  460.0 1.6 copy.26
  461.6 0.0 copy-start
  461.6 13.2 %feed_out.1 = (f32[5461,2,256]{2,1,0:T(2,128)}, f32[5461,256]{1,0:T(8,128)}) custom-call(bf16[3,4,2,2,704,128]{5,4,3,2,1,0:T(8,128)(2,1)} %get-tuple-element.66.feed_ref), custom_call_target="tpu_custom_call" | custom-call | tf_op jit(solution)/shard_map/feed_out/pallas_call | solution.py:1181
  474.8 0.0 copy-done
  474.8 0.8 copy.30
  (1 shorter events, 0.0 us)
Async XLA Ops:
  461.6 13.2 %copy-start = (bf16[128,2048]{1,0:T(8,128)(2,1)S(1)}, bf16[128,2048]{1,0:T(8,128)(2,1)}, u32[]{:S(2)}) copy-start(bf16[128,2048]{1,0:T(8,128)(2,1)} %get-tuple-element.46) | copy-start | bytes 1572868

commit v3 on v2

--- a/solution.py
+++ b/solution.py
@@ -349,79 +349,90 @@
 GU = pl.ds(0, 2)
 
 
-def spread(links, piece, w, local):
-    xp, xm, zp, zm = links.to(x=1), links.to(x=3), links.to(z=1), links.to(z=3)
+def two_rings(links, at, first, second, times):
+    up, down = first
+    right, left = second
     copies = []
-
-    def at(k, z, x, y=pl.ds(0, 4)):
-        z_hi, z_lo = links.z_at(z)
-        return w.at[k, z_hi, y, z_lo, links.part(x)]
 
     def send(ref, where):
         copies.append(links.start(ref, ref, where))
         return copies[-1]
 
+    def both(a):
+        return send(at(a, 0), right), send(at(a, 0), left)
+
+    def onward(a):
+        return send(at(a, 3, Y0), right), send(at(a, 1, Y1), left)
+
+    u, d = send(at(0, 0), up), send(at(0, 0), down)
+    near = [both(0)]
+    yield times[0]
+    received(u)
+    fu = send(at(3, 0, Y0), up)
+    near.append(both(3))
+    received(d)
+    fd = send(at(1, 0, Y1), down)
+    near.append(both(1))
+    yield times[1]
+    received(*near[0])
+    far = [*onward(0)]
+    received(fu, fd)
+    near.append(both(2))
+    for i, a in enumerate((3, 1, 2)):
+        yield times[2 + i]
+        received(*near[1 + i])
+        far += onward(a)
+    yield times[5]
+    received(*far)
+    sent(copies)
+
+
+def across_y(links, piece, own, local):
+    keep = pltpu.make_async_copy(piece(links.y), own(), local)
+    keep.start()
+    copies = []
+    for step in (2, 1, 3):
+        there = lax.rem(links.y + step, 4)
+        copies.append(links.start(piece(there), own(), links.to(y=step)))
+    return keep, copies
+
+
+def spread(links, piece, w, matrices, local):
+    along_x = (links.to(x=1), links.to(x=3))
+    along_z = (links.to(z=1), links.to(z=3))
+    every = pl.ds(0, 4)
+
+    def place(k, z, x, y):
+        z_hi, z_lo = links.z_at(z)
+        return w.at[k, z_hi, y, z_lo, links.part(x)]
+
     def own():
         return w.at[:, links.z_hi, links.y, links.z_lo, links.part(0)]
 
-    keep = pltpu.make_async_copy(piece.at[links.y], own(), local)
-    keep.start()
-    first = []
-    for step in (2, 1, 3):
-        copies.append(
-            links.start(piece.at[lax.rem(links.y + step, 4)], own(), links.to(y=step))
+    keep, copies = across_y(links, lambda y: piece.at[y, matrices], own, local)
+    yield 8
+    keep.wait()
+    received(*copies)
+    count = matrices.size
+    rings = [
+        two_rings(
+            links, lambda a, b, y=every: place(0, a, b, y), along_z, along_x, (14, 19, 24, 29, 34, 39)
         )
-        first.append(copies[-1])
-    yield 9
-    keep.wait()
-    received(*first)
-    zu, zd = send(at(GU, 0, 0), zp), send(at(GU, 0, 0), zm)
-    du, dd = send(at(2, 0, 0), xp), send(at(2, 0, 0), xm)
-    gx = [(send(at(GU, 0, 0), xp), send(at(GU, 0, 0), xm))]
-    dz = [(send(at(2, 0, 0), zp), send(at(2, 0, 0), zm))]
-    yield 16
-    received(du)
-    fdu = send(at(2, 0, 3, Y0), xp)
-    dz.append((send(at(2, 0, 3), zp), send(at(2, 0, 3), zm)))
-    received(dd)
-    fdd = send(at(2, 0, 1, Y1), xm)
-    dz.append((send(at(2, 0, 1), zp), send(at(2, 0, 1), zm)))
-    yield 20
-    received(zu)
-    fzu = send(at(0, 3, 0), zp)
-    gx.append((send(at(GU, 3, 0), xp), send(at(GU, 3, 0), xm)))
-    received(zd)
-    fzd = send(at(1, 1, 0), zm)
-    gx.append((send(at(GU, 1, 0), xp), send(at(GU, 1, 0), xm)))
-    yield 25
-    received(*gx[0])
-    gf = [(send(at(0, 0, 3), xp), send(at(1, 0, 1), xm))]
-    yield 28
-    received(*dz[0])
-    df = [(send(at(2, 3, 0, Y0), zp), send(at(2, 1, 0, Y1), zm))]
-    received(fdu, fdd)
-    dz.append((send(at(2, 0, 2), zp), send(at(2, 0, 2), zm)))
-    yield 30
-    received(fzu, fzd)
-    gx.append((send(at(GU, 2, 0), xp), send(at(GU, 2, 0), xm)))
-    yield 35
-    received(*gx[1])
-    gf.append((send(at(0, 3, 3), xp), send(at(1, 3, 1), xm)))
-    received(*dz[1])
-    df.append((send(at(2, 3, 3, Y0), zp), send(at(2, 1, 3, Y1), zm)))
-    yield 42
-    received(*gx[2])
-    gf.append((send(at(0, 1, 3), xp), send(at(1, 1, 1), xm)))
-    received(*dz[2])
-    df.append((send(at(2, 3, 1, Y0), zp), send(at(2, 1, 1, Y1), zm)))
-    yield 48
-    received(*dz[3])
-    df.append((send(at(2, 3, 2, Y0), zp), send(at(2, 1, 2, Y1), zm)))
-    received(*gx[3])
-    gf.append((send(at(0, 2, 3), xp), send(at(1, 2, 1), xm)))
-    yield 60
-    for pair in gf + df:
-        received(*pair)
+    ]
+    if count == 2:
+        rings.append(
+            two_rings(
+                links, lambda a, b, y=every: place(1, b, a, y), along_x, along_z, (15, 23, 29, 34, 39, 44)
+            )
+        )
+    due = [[next(ring), i, ring] for i, ring in enumerate(rings)]
+    while due:
+        due.sort(key=lambda entry: entry[:2])
+        yield due[0][0]
+        try:
+            due[0][0] = next(due[0][2])
+        except StopIteration:
+            due.pop(0)
     sent(copies)
 
 
@@ -451,7 +462,7 @@
     lax.fori_loop(0, count, step, 0)
 
 
-def reduce(links, bufs, shard):
+def reduce(links, bufs, make, shard):
     g, fx, nx, fz, nz, fz2, nz2, fx2, nx2 = bufs
     xp, xm, zp, zm = links.to(x=1), links.to(x=3), links.to(z=1), links.to(z=3)
     copies = []
@@ -483,34 +494,38 @@
 
     here = links.part(0)
     whole = pl.ds(0, FF)
-    c1, c2 = send(along_x(0, 2), fx.at[0], xp), send(along_x(1, 2), fx.at[1], xm)
+    yield from make(0)
+    c1, c4 = send(along_x(0, 2), fx.at[0], xp), send(along_x(0, 3), nx.at[1, 0], xm)
+    yield from make(1)
+    c2, c3 = send(along_x(1, 2), fx.at[1], xm), send(along_x(1, 1), nx.at[0, 1], xp)
+    yield from make(2)
     e1 = send(along_z(2, 2, Y0), fz2.at[Y0], zp)
     e2 = send(along_z(2, 2, Y1), fz2.at[Y1], zm)
-    c3, c4 = send(along_x(1, 1), nx.at[0, 1], xp), send(along_x(0, 3), nx.at[1, 0], xm)
     e3 = send(along_z(2, 1, Y1), nz2.at[0, Y1], zp)
     e4 = send(along_z(2, 3, Y0), nz2.at[1, Y0], zm)
-    yield 9
+    yield 31
+    received(c1)
+    accumulate(16, block_x(0, 1), plain(fx.at[0]))
+    c5 = send(along_x(0, 1), nx.at[0, 0], xp)
+    yield 36
     received(e1)
     accumulate(2, block_z(2, 1, whole), shift(fz2))
     e5 = send(along_z(2, 1, Y0), nz2.at[0, Y0], zp)
     received(e2)
     accumulate(2, block_z(2, 3, whole, 2), shift(fz2, 2))
     e6 = send(along_z(2, 3, Y1), nz2.at[1, Y1], zm)
-    yield 17
-    received(c1)
-    accumulate(16, block_x(0, 1), plain(fx.at[0]))
-    c5 = send(along_x(0, 1), nx.at[0, 0], xp)
+    yield 42
     received(c2)
     accumulate(16, block_x(1, 3), plain(fx.at[1]))
     c6 = send(along_x(1, 3), nx.at[1, 1], xm)
-    yield 26
+    yield 53
     received(e3, e4, e5, e6)
     accumulate(4, block_z(2, 0, whole), shift(nz2.at[0]), shift(nz2.at[1]))
     d1 = send(along_z(2, 0, Y0, links.part(2)), fx2.at[Y0], xp)
     d2 = send(along_z(2, 0, Y1, links.part(2)), fx2.at[Y1], xm)
     d3 = send(along_z(2, 0, Y1, links.part(1)), nx2.at[0, Y1], xp)
     d4 = send(along_z(2, 0, Y0, links.part(3)), nx2.at[1, Y0], xm)
-    yield 46
+    yield 62
     received(c3, c4, c5, c6)
     for k in range(2):
         accumulate(16, block_x(k, 0), plain(nx.at[0, k]), plain(nx.at[1, k]))
@@ -524,14 +539,14 @@
     received(d2)
     accumulate(2, block_z(2, 0, links.part(3), 2), shift(fx2, 2))
     d6 = send(along_z(2, 0, Y1, links.part(3)), nx2.at[1, Y1], xm)
-    yield 52
+    yield 68
     received(f1)
     accumulate(4, block_z(0, 1, here), shift(fz.at[0]))
     f5 = send(along_z(0, 1, every, here), nz.at[0, 0], zp)
     received(f2)
     accumulate(4, block_z(1, 3, here), shift(fz.at[1]))
     f6 = send(along_z(1, 3, every, here), nz.at[1, 1], zm)
-    yield 58
+    yield 75
     received(d3, d4, d5, d6)
     accumulate(4, block_z(2, 0, here), shift(nx2.at[0]), shift(nx2.at[1]))
     received(f3, f4, f5, f6)
@@ -792,7 +807,8 @@
 
 
 def project_kernel(
-    x_ref, w_ref, cos_ref, sin_ref, piece_ref, all_ref, q_ref, k_ref, v_ref, w_all_ref, local, send, recv
+    x_ref, w_ref, cos_ref, sin_ref, piece_ref, out_ref, q_ref, k_ref, v_ref, w_all_ref,
+    all_ref, local, out_sem, send, recv,
 ):
     links = Links(send, recv)
     all_ref[0] = x_ref[...]
@@ -817,7 +833,14 @@
                         turned = turned * HEAD_DIM**-0.5
                     out[at, lanes] = turned.astype(BF16)
 
-    together(gather(links, all_ref, work), spread(links, piece_ref, w_all_ref, local))
+    written = pltpu.make_async_copy(all_ref, out_ref, out_sem)
+
+    def tokens():
+        yield from gather(links, all_ref, work)
+        written.start()
+
+    together(tokens(), spread(links, piece_ref, w_all_ref, GU, local))
+    written.wait()
 
 
 def attend_kernel(prefix_ref, q_ref, k_ref, v_ref, out_ref, lse_ref):
@@ -860,70 +883,14 @@
     )(prefix, q, k, v)
 
 
-def attend_back_kernel(
-    prefix_ref, q_ref, k_ref, v_ref, g_ref, lse_ref, cos_ref, sin_ref, cosq_ref, sinq_ref,
-    dq_ref, dk_ref, dv_ref, dk_sum, dv_sum
-):
-    block = q_ref.shape[0]
-    step = pl.program_id(1)
-    scores = dot_t(k_ref[...], q_ref[...])
-    key = lax.broadcasted_iota(jnp.int32, scores.shape, 0)
-    query = lax.broadcasted_iota(jnp.int32, (1, block), 1) + step * block
-    limit = jnp.maximum(query, prefix_ref[0] - 1)
-    weights = jnp.where(key <= limit, jnp.exp(scores - lse_ref[0]), 0.0)
-    grad_weights = dot_t(v_ref[...], g_ref[...])
-    inner = jnp.sum(weights * grad_weights, axis=0, keepdims=True)
-    grad_scores = (weights * (grad_weights - inner)).astype(BF16)
-    d_query = dot_rows(grad_scores, k_ref[...]) * HEAD_DIM**-0.5
-    dq_ref[...] = (d_query * cosq_ref[...] - pltpu.roll(d_query, 64, 1) * sinq_ref[...]).astype(BF16)
-    d_key = dot(grad_scores, q_ref[...])
-    d_value = dot(weights.astype(BF16), g_ref[...])
-
-    @pl.when(step == 0)
-    def _():
-        dk_sum[...] = d_key
-        dv_sum[...] = d_value
-
-    @pl.when(step > 0)
-    def _():
-        dk_sum[...] += d_key
-        dv_sum[...] += d_value
-
-    @pl.when(step == pl.num_programs(1) - 1)
-    def _():
-        total = dk_sum[...]
-        dk_ref[...] = (total * cos_ref[...] - pltpu.roll(total, 64, 1) * sin_ref[...]).astype(BF16)
-        dv_ref[...] = dv_sum[...].astype(BF16)
-
-
-def attend_back(prefix, q, k, v, g, lse, cosine, sine):
-    block = 512
-    part = pl.BlockSpec((block, 128), lambda h, b: (b, h))
-    whole = pl.BlockSpec((LEN, 128), lambda h, b: (0, h))
-    table = pl.BlockSpec((LEN, 128), lambda h, b: (0, 0))
-    table_part = pl.BlockSpec((block, 128), lambda h, b: (b, 0))
-    return pl.pallas_call(
-        attend_back_kernel,
-        name="attend_back",
-        grid=(2, LEN // block),
-        in_specs=[
-            SMEM, part, whole, whole, part,
-            pl.BlockSpec((1, 1, block), lambda h, b: (h, 0, b)),
-            table, table, table_part, table_part,
-        ],
-        out_specs=(part, whole, whole),
-        out_shape=tuple(jax.ShapeDtypeStruct((LEN, 256), BF16) for _ in range(3)),
-        scratch_shapes=[pltpu.VMEM((LEN, 128), F32), pltpu.VMEM((LEN, 128), F32)],
-        compiler_params=pltpu.CompilerParams(vmem_limit_bytes=VMEM_BYTES),
-    )(prefix, q, k, v, g, lse, cosine, sine, cosine, sine)
-
-
 def attended_kernel(
-    heads_ref, w_ref, x_ref, gain_ref, bias_ref, normed_ref, unit_ref, inverse_ref, total, *rest
+    heads_ref, w_ref, x_ref, gain_ref, bias_ref, piece_ref, normed_ref, unit_ref, inverse_ref, w_all_ref,
+    total, local, *rest,
 ):
     bufs, (send, recv) = rest[:7], rest[7:]
     links = Links(send, recv)
-    links.barrier(links.to(y=1), links.to(y=3), links.to(z=2))
+    to = links.to
+    links.barrier(to(y=1), to(y=3), to(z=2), to(y=2), to(x=1), to(x=3), to(z=1), to(z=3))
 
     def compute(pair):
         rows = jnp.concatenate([heads_ref[pl.ds(links.first_row(s), ROWS)] for s in pair], axis=0)
@@ -931,50 +898,63 @@
         for i, slot in enumerate(pair):
             bufs[0][slot] = result[i * ROWS : (i + 1) * ROWS]
 
-    together(scatter(links, bufs, compute, total))
-
     def finish(at):
         unit, inverse = norm_parts(deep_alpha * x_ref[at].astype(F32) + total[at])
         unit_ref[at] = unit
         inverse_ref[at] = jnp.broadcast_to(inverse, (16, 128))
         normed_ref[at] = unit * gain_ref[...] + bias_ref[...]
 
-    by_chunks(finish)
-
-
-def load_weights(w_hbm, w, sem, parts):
-    copies = []
+    def chain():
+        yield from scatter(links, bufs, compute, total)
+        by_chunks(finish)
+
+    together(chain(), spread(links, piece_ref, w_all_ref, pl.ds(2, 1), local))
+
+
+class Loads:
+    def __init__(self):
+        self.copies = []
+
+    def start(self, src, dst, sem):
+        copy = pltpu.make_async_copy(src, dst, sem)
+        copy.start()
+        self.copies.append(copy)
+
+    def wait(self):
+        while self.copies:
+            self.copies.pop().wait()
+
+
+def load_weights(w_hbm, w, sem, first, parts):
+    loads = Loads()
     for k in range(parts):
         for i in range(16):
             src = w_hbm.at[k, lax.rem(i // 2, 2), i // 4, lax.rem(i, 2)]
-            copies.append(
-                pltpu.make_async_copy(src, w.at[k, pl.ds(0, FF), pl.ds(i * 128, 128)], sem.at[k, i])
-            )
-    for copy in copies:
-        copy.start()
+            loads.start(src, w.at[first + k, pl.ds(0, FF), pl.ds(i * 128, 128)], sem.at[first + k, i])
     for k in range(parts):
-        w[k, FF:COLS] = jnp.zeros((COLS - FF, WIDE), BF16)
-    return copies
+        w[first + k, FF:COLS] = jnp.zeros((COLS - FF, WIDE), BF16)
+    return loads
 
 
 def feed_kernel(
-    normed_ref, cot_ref, weight_ref, w_hbm, gain_ref, bias_ref,
-    out_ref, all_ref, gz_all_ref, act_ref, gz_ref, vec_ref,
-    w, gelu_ref, slope, total, w_sem, *rest,
+    clusters_ref, normed_ref, cot_ref, gu_hbm, down_hbm, gain_ref, bias_ref,
+    out_ref, all_out, gz_all_out, act_out, gz_ref, vec_ref,
+    w, all_ref, gz_all_ref, act_ref, gelu_ref, slope, total, w_sem, out_sem, *rest,
 ):
     bufs, (send, recv) = rest[:4], rest[4:]
     links = Links(send, recv)
-    loads = load_weights(w_hbm, w, w_sem, 3)
 
     def to_low(at):
         all_ref[0, at] = normed_ref[at].astype(BF16)
 
     by_chunks(to_low)
+    load_gu = load_weights(gu_hbm, w, w_sem, 0, 2)
+    load_down = load_weights(down_hbm, w, w_sem, 2, 1)
     links.barrier(links.to(y=1), links.to(y=3), links.to(sibling=True))
-    for copy in loads:
-        copy.wait()
+    written = Loads()
 
     def forward(pair):
+        load_gu.wait()
         rows = pair_of(all_ref, pair)
         for c in range(0, COLS, 256):
             cols = slice(c, c + 256)
@@ -992,8 +972,10 @@
                 act_ref[slot, :, 2 * COLS + c : 2 * COLS + c + 256] = hidden[part]
 
     together(gather_near(links, all_ref, forward))
+    written.start(all_ref, all_out, out_sem.at[8])
 
     def compute(pair):
+        load_down.wait()
         rows = jnp.concatenate([act_ref[slot, :, 2 * COLS :] for slot in pair], axis=0)
         for d in range(0, WIDE, 512):
             result = dot(rows, w[2, :, d : d + 512]).astype(BF16)
@@ -1002,11 +984,15 @@
 
     together(scatter_near(links, bufs, compute, total))
     vec_ref[...] = jnp.zeros_like(vec_ref)
+    own, same = clusters_ref[lax.axis_index("dp")], np.float32(0.0)
+    for i in range(clusters_ref.shape[0]):
+        same = same + jnp.where(clusters_ref[i] == own, np.float32(1.0), np.float32(0.0))
+    seq_weight = 1.0 / jnp.full((1, WIDE), same, F32)
 
     def finish(at):
         unit, inverse = norm_parts(deep_alpha * normed_ref[at] + total[at])
         out_ref[at] = (unit * gain_ref[...] + bias_ref[...]).astype(BF16)
-        grad = cot_ref[at].astype(F32) * weight_ref[0]
+        grad = cot_ref[at].astype(F32) * seq_weight
         grad_z = norm_backward(grad, unit, inverse, gain_ref[...])
         gz_ref[at] = grad_z
         gz_all_ref[0, at] = grad_z.astype(BF16)
@@ -1024,30 +1010,31 @@
                 part = grad_hidden[i * ROWS : (i + 1) * ROWS]
                 act_ref[slot, :, cols] = (part * slope[slot, :, cols]).astype(BF16)
                 act_ref[slot, :, COLS + c : COLS + c + 256] = (part * gelu_ref[slot, :, cols]).astype(BF16)
+        for slot in pair:
+            written.start(act_ref.at[slot], act_out.at[slot], out_sem.at[slot])
 
     together(gather_near(links, gz_all_ref, backward))
+    written.start(gz_all_ref, gz_all_out, out_sem.at[9])
+    written.wait()
 
 
 def feed_back_kernel(
-    act_ref, gz_ref, w_hbm, g_hbm, unit_ref, inverse_ref, gain_ref, w_out_ref,
-    gz1_ref, all_ref, grad_heads_ref, vec_ref, shard_ref,
-    w, total, w_sem, g_sem, *rest,
+    act_hbm, gz_ref, w_hbm, normed_hbm, gz_all_hbm, unit_ref, inverse_ref, gain_ref, w_out_ref,
+    gz1_ref, all_out, grad_heads_ref, vec_ref, shard_ref,
+    act_ref, rows_ref, all_ref, w, total, w_sem, sem, *rest,
 ):
     bufs, more, (send, recv) = rest[:4], rest[4:13], rest[13:]
     links = Links(send, recv)
-    loads = load_weights(w_hbm, w, w_sem, 2)
-    for k in range(3):
-        for i in range(16):
-            dst = more[0].at[k, lax.rem(i // 2, 2), i // 4, lax.rem(i, 2)]
-            src = g_hbm.at[k, pl.ds(0, FF), pl.ds(i * 128, 128)]
-            loads.append(pltpu.make_async_copy(src, dst, g_sem.at[k, i]))
-            loads[-1].start()
+    load_act, load_rows = Loads(), Loads()
+    load_act.start(act_hbm, act_ref, sem.at[0])
+    load_w = load_weights(w_hbm, w, w_sem, 0, 2)
+    load_rows.start(normed_hbm, rows_ref, sem.at[1])
     to = links.to
     links.barrier(
         to(y=1), to(y=3), to(z=2), to(x=1), to(x=3), to(z=1), to(z=3), to(sibling=True)
     )
-    for copy in loads:
-        copy.wait()
+    load_act.wait()
+    load_w.wait()
 
     def compute(pair):
         rows = jnp.concatenate([act_ref[slot, :, : 2 * COLS] for slot in pair], axis=0)
@@ -1072,34 +1059,87 @@
         for i, slot in enumerate(pair):
             grad_heads_ref[pl.ds(links.first_row(slot), ROWS)] = result[i * ROWS : (i + 1) * ROWS]
 
+    written = Loads()
+
     def chain():
         yield from scatter_near(links, bufs, compute, total)
         vec_ref[...] = jnp.zeros_like(vec_ref)
         by_chunks(finish)
         for time in gather(links, all_ref, work):
-            yield time + 22
-
-    together(reduce(links, more, shard_ref), chain())
+            yield time + 24
+        written.start(all_ref, all_out, sem.at[3])
+
+    g = more[0]
+
+    def make(k):
+        load_rows.wait()
+        for c in range(0, COLS, 256):
+            left = act_ref[:, :, k * COLS + c : k * COLS + c + 256].reshape(LEN, 256)
+            height = min(256, FF - c)
+            for d in range(0, WIDE, 512):
+                right = rows_ref[:, :, d : d + 512].reshape(LEN, 512)
+                result = dot_rows(left, right)[:height].astype(BF16)
+                for i in range(4):
+                    at = d // 128 + i
+                    g[k, at // 2 % 2, at // 4, at % 2, c : c + height] = result[:, i * 128 : i * 128 + 128]
+            if k == 1 and c == 512:
+                load_rows.start(gz_all_hbm, rows_ref, sem.at[2])
+            yield 8 + 6 * k + c // 128
+
+    together(chain(), reduce(links, more, make, shard_ref))
+    written.wait()
 
 
 def input_kernel(
-    dq_ref, dk_ref, dv_ref, w_ref, gz1_ref, tokens_ref, heads_ref, gz_all_ref, shard_ref, vec_in_ref,
+    prefix_ref, q_ref, k_ref, v_ref, g_ref, lse_ref, cos_ref, sin_ref,
+    w_hbm, gz1_ref, tokens_hbm, heads_ref, gz_all_hbm, shard_ref, vec_in_ref,
     out_ref, q_out_ref, vec_ref, feed_ref,
-    total, grads, heads, held, got, local, *rest,
+    total, w_ref, tokens_ref, gz_all_ref, back, grads, heads, key_sum, value_sum, held, got, local, sem, *rest,
 ):
     bufs, more, (send, recv) = rest[:7], rest[7:12], rest[12:]
     links = Links(send, recv)
     to = links.to
+    loads = Loads()
+    loads.start(w_hbm, w_ref, sem.at[0])
+    loads.start(tokens_hbm, tokens_ref, sem.at[1])
+    loads.start(gz_all_hbm, gz_all_ref, sem.at[2])
     beside = (lax.rem(lax.axis_index("dp") + 8, 16), lax.axis_index("seq"))
     links.barrier(
         to(y=1), to(y=2), to(y=3), to(z=2), to(x=1), to(x=2), to(x=3), to(sibling=True), beside
     )
-    for slot in range(8):
-        at = pl.ds(links.first_row(slot), ROWS)
-        heads[slot] = heads_ref[at]
-        for part, ref in enumerate((dq_ref, dk_ref, dv_ref)):
-            grads[slot, :, part * 256 : part * 256 + 256] = ref[at]
     vec_ref[...] = vec_in_ref[...]
+    block = 512
+
+    def attend_back():
+        for head in range(2):
+            lanes = slice(head * 128, head * 128 + 128)
+            for first in range(0, LEN, block):
+                at = slice(first, first + block)
+                query, grad = q_ref[at, lanes], g_ref[at, lanes]
+                scores = dot_t(k_ref[:, lanes], query)
+                key = lax.broadcasted_iota(jnp.int32, scores.shape, 0)
+                limit = lax.broadcasted_iota(jnp.int32, (1, block), 1) + first
+                limit = jnp.maximum(limit, prefix_ref[0] - 1)
+                weights = jnp.where(key <= limit, jnp.exp(scores - lse_ref[head, :, at]), 0.0)
+                grad_weights = dot_t(v_ref[:, lanes], grad)
+                inner = jnp.sum(weights * grad_weights, axis=0, keepdims=True)
+                grad_scores = (weights * (grad_weights - inner)).astype(BF16)
+                turned = dot_rows(grad_scores, k_ref[:, lanes]) * HEAD_DIM**-0.5
+                turned = turned * cos_ref[at] - pltpu.roll(turned, 64, 1) * sin_ref[at]
+                back[at, lanes] = turned.astype(BF16)
+                grad_key = dot(grad_scores, query)
+                grad_value = dot(weights.astype(BF16), grad)
+                if first == 0:
+                    key_sum[...] = grad_key
+                    value_sum[...] = grad_value
+                else:
+                    key_sum[...] += grad_key
+                    value_sum[...] += grad_value
+                yield 4 * head + first // 200
+            turned = key_sum[...]
+            turned = turned * cos_ref[...] - pltpu.roll(turned, 64, 1) * sin_ref[...]
+            back[:, 256 + head * 128 : 384 + head * 128] = turned.astype(BF16)
+            back[:, 512 + head * 128 : 640 + head * 128] = value_sum[...].astype(BF16)
 
     def compute(pair):
         rows = pair_of(grads, pair)
@@ -1109,6 +1149,22 @@
         result = result.astype(BF16)
         for i, slot in enumerate(pair):
             bufs[0][slot] = result[i * ROWS : (i + 1) * ROWS]
+
+    def finish(at):
+        value = deep_alpha * gz1_ref[at] + total[at]
+        for lane in range(WIDE // 128):
+            out_ref[at, lane] = value[:, lane * 128 : lane * 128 + 128]
+
+    def chain():
+        yield from attend_back()
+        for slot in range(8):
+            at = pl.ds(links.first_row(slot), ROWS)
+            heads[slot] = heads_ref[at]
+            grads[slot] = back[at]
+        loads.wait()
+        for time in scatter(links, bufs, compute, total):
+            yield time + 14
+        by_chunks(finish)
 
     def qkv():
         flat = more[0]
@@ -1129,70 +1185,52 @@
             ]
 
     def shared():
-        yield 9
+        yield 18
         qkv()
-        yield from share(links, more, q_out_ref, 16)
+        yield from share(links, more, q_out_ref, 31)
 
     together(
         collect(links, shard_ref, feed_ref, local, 0),
-        scatter(links, bufs, compute, total),
+        chain(),
         shared(),
         agree(links, vec_ref, (held, got)),
     )
 
-    def finish(at):
-        out_ref[at] = deep_alpha * gz1_ref[at] + total[at]
-
-    by_chunks(finish)
-
-
-def feed_weight_kernel(act_ref, normed_ref, gz_ref, out_ref):
-    @pl.when(pl.program_id(0) < 6)
-    def _():
-        out_ref[0] = dot_rows(act_ref[...], normed_ref[...]).astype(BF16)
-
-    @pl.when(pl.program_id(0) >= 6)
-    def _():
-        out_ref[0] = dot_rows(act_ref[...], gz_ref[...]).astype(BF16)
-
-
-def feed_weights(act, normed_all, gz_all):
-    flat = lambda v: v.reshape(LEN, v.shape[-1])
-    return pl.pallas_call(
-        feed_weight_kernel,
-        name="feed_weights",
-        grid=(9,),
-        in_specs=[pl.BlockSpec((LEN, 256), lambda i: (0, i)), VMEM, VMEM],
-        out_specs=pl.BlockSpec((1, 256, WIDE), lambda i: (i // 3, i % 3, 0)),
-        out_shape=jax.ShapeDtypeStruct((3, COLS, WIDE), BF16),
-        compiler_params=pltpu.CompilerParams(vmem_limit_bytes=VMEM_BYTES),
-    )(flat(act), flat(normed_all), flat(gz_all))
-
-
-def feed_out_kernel(feed_ref, gate_up_ref, down_ref):
+
+def outputs_kernel(feed_ref, qkv_ref, out_ref, gate_up_ref, down_ref, grad_qkv_ref, grad_out_ref):
     for z in range(2):
         lanes = slice(z * 128, z * 128 + 128)
         gate_up_ref[:, 0, lanes] = feed_ref[0, 0, 0, z].astype(F32)
         gate_up_ref[:, 1, lanes] = feed_ref[1, 0, 0, z].astype(F32)
         down_ref[:, lanes] = feed_ref[2, 0, 0, z].astype(F32)
-
-
-def feed_out(feed, total):
+    grad_qkv_ref[...] = qkv_ref[...].astype(F32)
+    grad_out_ref[...] = out_ref[...].astype(F32)
+
+
+def outputs(feed, attention, total):
     return pl.pallas_call(
-        feed_out_kernel,
-        name="feed_out",
+        outputs_kernel,
+        name="outputs",
         grid=(8,),
-        in_specs=[pl.BlockSpec((3, 1, 1, 2, FF, 128), lambda i: (0, i // 2, i % 2, 0, 0, 0))],
+        in_specs=[
+            pl.BlockSpec((3, 1, 1, 2, FF, 128), lambda i: (0, i // 2, i % 2, 0, 0, 0)),
+            pl.BlockSpec((768, 256), lambda i: (i, 0)),
+            pl.BlockSpec((256, 256), lambda i: (24 + i, 0)),
+        ],
         out_specs=(
             pl.BlockSpec((FF, 2, 256), lambda i: (i, 0, 0)),
             pl.BlockSpec((FF, 256), lambda i: (i, 0)),
+            pl.BlockSpec((768, 256), lambda i: (i, 0)),
+            pl.BlockSpec((256, 256), lambda i: (0, i)),
         ),
         out_shape=(
             jax.ShapeDtypeStruct((total, 2, 256), F32),
             jax.ShapeDtypeStruct((total, 256), F32),
+            jax.ShapeDtypeStruct((6144, 256), F32),
+            jax.ShapeDtypeStruct((256, WIDE), F32),
         ),
         compiler_params=pltpu.CompilerParams(vmem_limit_bytes=VMEM_BYTES),
-    )(feed)
+    )(feed, attention, attention)
 
 
 def on_device(
@@ -1202,8 +1240,6 @@
     x = tokens.reshape(ROWS, WIDE)
     cot = cotangent.reshape(ROWS, WIDE)
     dp, seq = lax.axis_index("dp"), lax.axis_index("seq")
-    own_id = lax.dynamic_slice_in_dim(clusters, dp, 1)
-    seq_weight = 1.0 / jnp.sum((own_id[:, None] == clusters[None, :]).astype(F32), axis=1)
     cosine, sine = (jnp.asarray(t) for t in rotary_tables(LEN, HEAD_DIM))
     row = lambda v: v.reshape(1, WIDE)
     ff_total = w_down.shape[1]
@@ -1212,75 +1248,86 @@
     w_in = w_qkv.transpose(1, 0, 2)
     low, full = BF16, F32
     blocks = (8, ROWS, WIDE)
-
-    tokens_all, q, k, v, ffn_w = call(
+    one = pltpu.SemaphoreType.DMA
+    some = lambda *n: pltpu.SemaphoreType.DMA(n)
+    rows_f32 = pltpu.VMEM((ROWS, WIDE), F32)
+    blocks_low = pltpu.VMEM(blocks, BF16)
+
+    tokens_all, q, k, v, w_gu = call(
         project_kernel, "project", 0,
-        [(blocks, low, "v")] + [((LEN, 256), low, "v")] * 3 + [((3, 2, 4, 2, FF, 128), low, "h")],
-        (x, w_in, cosine, sine, piece), "vvvvv", (pltpu.SemaphoreType.DMA,), 67,
+        [(blocks, low, "h")] + [((LEN, 256), low, "v")] * 3 + [((2, 2, 4, 2, FF, 128), low, "h")],
+        (x, w_in, cosine, sine, piece), "vvvvv", (blocks_low, one, one), 60,
         2 * LEN * WIDE * 768,
     )
     heads_out, lse = attend(prefix_len, q, k, v)
-    normed, unit_one, inverse_one = call(
+    normed, unit_one, inverse_one, w_dn = call(
         attended_kernel, "attended", 1,
-        [((ROWS, WIDE), full, "v"), ((ROWS, WIDE), full, "v"), ((ROWS, 128), full, "v")],
-        (heads_out, w_out, x, row(attn_gain), row(attn_bias)), "vvvvv",
-        (pltpu.VMEM((ROWS, WIDE), F32), *SCATTER_SCRATCH), 19, 2 * LEN * WIDE * 256,
+        [
+            ((ROWS, WIDE), full, "v"), ((ROWS, WIDE), full, "v"), ((ROWS, 128), full, "v"),
+            ((1, 2, 4, 2, FF, 128), low, "h"),
+        ],
+        (heads_out, w_out, x, row(attn_gain), row(attn_bias), piece), "vvvvvv",
+        (rows_f32, one, *SCATTER_SCRATCH), 42, 2 * LEN * WIDE * 256,
     )
     output, normed_all, gz_all, act, grad_z2, ffn_vec = call(
         feed_kernel, "feed", 2,
         [
-            ((ROWS, WIDE), low, "v"), (blocks, low, "v"), (blocks, low, "v"),
-            ((8, ROWS, 3 * COLS), low, "v"), ((ROWS, WIDE), full, "v"), ((2, 8, WIDE), full, "v"),
+            ((ROWS, WIDE), low, "v"), (blocks, low, "h"), (blocks, low, "h"),
+            ((8, ROWS, 3 * COLS), low, "h"), ((ROWS, WIDE), full, "v"), ((2, 8, WIDE), full, "v"),
         ],
-        (normed, cot, seq_weight, ffn_w, row(ffn_gain), row(ffn_bias)), "vvshvv",
+        (clusters, normed, cot, w_gu, w_dn, row(ffn_gain), row(ffn_bias)), "svvhhvv",
         (
-            pltpu.VMEM((3, COLS, WIDE), BF16), pltpu.VMEM((8, ROWS, COLS), F32),
-            pltpu.VMEM((8, ROWS, COLS), F32), pltpu.VMEM((ROWS, WIDE), F32),
-            pltpu.SemaphoreType.DMA((3, 16)), *NEAR_SCRATCH,
+            pltpu.VMEM((3, COLS, WIDE), BF16), blocks_low, blocks_low,
+            pltpu.VMEM((8, ROWS, 3 * COLS), BF16), pltpu.VMEM((8, ROWS, COLS), F32),
+            pltpu.VMEM((8, ROWS, COLS), F32), rows_f32, some(3, 16), some(10), *NEAR_SCRATCH,
         ),
         34, 2 * LEN * WIDE * COLS * 4,
     )
-    ffn_grad = feed_weights(act, normed_all, gz_all)
     grad_z1, gz1_all, grad_heads, attn_vec, shard = call(
         feed_back_kernel, "feed_back", 3,
         [
-            ((ROWS, WIDE), full, "v"), (blocks, low, "v"), ((LEN, 256), low, "v"),
+            ((ROWS, WIDE), full, "v"), (blocks, low, "h"), ((LEN, 256), low, "v"),
             ((2, 8, WIDE), full, "v"), ((3, 4, PART, 128), low, "v"),
         ],
-        (act, grad_z2, ffn_w, ffn_grad, unit_one, inverse_one, row(attn_gain), w_out), "vvhhvvvv",
+        (act, grad_z2, w_gu, normed_all, gz_all, unit_one, inverse_one, row(attn_gain), w_out),
+        "hvhhhvvvv",
         (
-            pltpu.VMEM((2, COLS, WIDE), BF16), pltpu.VMEM((ROWS, WIDE), F32),
-            pltpu.SemaphoreType.DMA((2, 16)), pltpu.SemaphoreType.DMA((3, 16)),
+            pltpu.VMEM((8, ROWS, 3 * COLS), BF16), blocks_low, blocks_low,
+            pltpu.VMEM((2, COLS, WIDE), BF16), rows_f32, some(2, 16), some(4),
             *NEAR_SCRATCH, *REDUCE_SCRATCH,
         ),
-        52, 2 * LEN * WIDE * COLS * 2,
-    )
-    dq, dk, dv = attend_back(prefix_len, q, k, v, grad_heads, lse, cosine, sine)
+        52, 2 * LEN * WIDE * COLS * 5,
+    )
     vec = jnp.concatenate([attn_vec.sum(1), ffn_vec.sum(1), jnp.zeros((4, WIDE), F32)], axis=0)
     steps = pltpu.VMEM((7, 8, WIDE), F32)
-    input_grad, qkv_out, vec, ffn_whole = call(
+    head_sum = pltpu.VMEM((LEN, 128), F32)
+    input_grad, attention, vec, ffn_whole = call(
         input_kernel, "input", 4,
         [
-            ((ROWS, WIDE), full, "v"), ((2, 2, 4, 512, 256), low, "v"), ((8, WIDE), full, "v"),
+            ((ROWS, WIDE // 128, 128), full, "v"), ((2, 2, 4, 512, 256), low, "v"), ((8, WIDE), full, "v"),
             ((3, 4, 2, 2, FF, 128), low, "h"),
         ],
-        (dq, dk, dv, w_in, grad_z1, tokens_all, heads_out, gz1_all, shard, vec), "vvvvvvvvvv",
         (
-            pltpu.VMEM((ROWS, WIDE), F32), pltpu.VMEM((8, ROWS, 768), BF16),
-            pltpu.VMEM((8, ROWS, 256), BF16), steps, steps, pltpu.SemaphoreType.DMA,
+            prefix_len, q, k, v, grad_heads, lse, cosine, sine,
+            w_in, grad_z1, tokens_all, heads_out, gz1_all, shard, vec,
+        ),
+        "svvvvvvvhvhvhvv",
+        (
+            rows_f32, pltpu.VMEM((3, WIDE, 256), BF16), blocks_low, blocks_low,
+            pltpu.VMEM((LEN, 768), BF16), pltpu.VMEM((8, ROWS, 768), BF16),
+            pltpu.VMEM((8, ROWS, 256), BF16), head_sum, head_sum, steps, steps, one, some(3),
             *SCATTER_SCRATCH, *SHARE_SCRATCH,
         ),
         77, 2 * LEN * WIDE * 768,
     )
-    grad_gate_up, grad_down = feed_out(ffn_whole, ff_total)
-    qkv_out = qkv_out.reshape(8192, 256).astype(F32)
-    grad_qkv = qkv_out[:6144].reshape(3, WIDE, 256).transpose(1, 0, 2)
-    grad_out = qkv_out[6144:].reshape(8, 256, 256).transpose(1, 0, 2).reshape(256, WIDE)
+    grad_gate_up, grad_down, grad_qkv, grad_out = outputs(
+        ffn_whole, attention.reshape(8192, 256), ff_total
+    )
     own = lax.dynamic_slice_in_dim(vec, seq * 256, 256, axis=1)
     return (
         output.reshape(tokens.shape),
         input_grad.reshape(tokens.shape),
-        grad_qkv,
+        grad_qkv.reshape(3, WIDE, 256).transpose(1, 0, 2),
         grad_out,
         grad_gate_up.transpose(2, 1, 0),
         grad_down.T,

time: 484 us -> 439 us (0.907)
  Pallas kernels: 454 us -> 424 us
  local copies, waits for them, and re-layouts: 11.7 us -> 3.36 us
  other arithmetic: 7.95 us -> 2.29 us
    pallas_call x3 -> x1, Pallas kernels: 43.5 us -> 16.1 us  [outputs(): pl.pallas_call(outputs_kernel, name='outputs', grid=(8,), in_specs=[pl.Bl...]
where the time goes in v3:
time: 439 us; the launch traced here: 431 us
  Pallas kernels  424 us (97%)
    pallas_call x5, Pallas kernels, call(): pl.pallas_call(body, name=name, out_shape=tuple((jax.ShapeDtypeStruct(s,...  395 us
    pallas_call x1, Pallas kernels, outputs(): pl.pallas_call(outputs_kernel, name='outputs', grid=(8,), in_specs=[pl.Bl...  16.1 us

profile of v3, /device:TPU:1, one launch (start us, length us, event | category | flops | bytes accessed | tf_op | source)
XLA Modules:
  0.0 431.2 jit_solution(5445659916112071343)
XLA Ops:
  1.3 0.6 pad_add_fusion.place_ref
  1.9 0.1 pad.2.clone
  2.0 4.2 piece.1.piece_ref
  6.2 59.2 %project.1 = (bf16[8,128,2048]{2,1,0:T(8,128)(2,1)}, bf16[1024,256]{1,0:T(8,128)(2,1)}, bf16[1024,256]{1,0:T(8,128)(2,1)}, bf16[1024,256]{1,0:T(8,128)(2,1)}, bf16[2,2,4,2,704,128]{5,4,3,2,1,0:T(8,128)(2,1)}) custom-call(bf16[128,2048]{1,0:T(8,128)(2,1)} %bitcast.39, bf16[3,2048,256]{2,1,0:T(8,128)(2,1)} %bitcast.27, f32[1024,128]{1,0:T(8,128)} %constant.67.clone.cos_ref, ...), custom_call_target="tpu_custom_call" | custom-call | flops 3221225472 | bytes 20000000 | tf_op jit(solution)/shard_map/project/pallas_call | solution.py:764
  65.4 8.4 %attend.1 = (bf16[1024,256]{1,0:T(8,128)(2,1)}, f32[2,1,1024]{2,1,0:T(1,128)}) custom-call(s32[1]{0:T(128)S(6)} %copy.27.prefix_ref, bf16[1024,256]{1,0:T(8,128)(2,1)} %get-tuple-element.40.q_ref, bf16[1024,256]{1,0:T(8,128)(2,1)} %get-tuple-element.41.k_ref, bf16[1024,256]{1,0:T(8,128)(2,1)} %get-tuple-element.42.v_ref), custom_call_target="tpu_custom_call" | custom-call | tf_op jit(solution)/shard_map/attend/pallas_call | solution.py:864
  73.8 45.1 %attended.1 = (f32[128,2048]{1,0:T(8,128)}, f32[128,2048]{1,0:T(8,128)}, f32[128,128]{1,0:T(8,128)}, bf16[1,2,4,2,704,128]{5,4,3,2,1,0:T(8,128)(2,1)}) custom-call(bf16[1024,256]{1,0:T(8,128)(2,1)} %get-tuple-element.43.heads_ref, bf16[256,2048]{1,0:T(8,128)(2,1)} %w_out_ref.1, bf16[128,2048]{1,0:T(8,128)(2,1)} %bitcast.40, f32[1,2048]{1,0:T(1,128)} %bitcast.45, ...), custom_call_target="tpu_custom_call" | custom-call | flops 1073741824 | bytes 20000000 | tf_op jit(solution)/shard_map/attended/pallas_call | solution.py:764
  118.9 84.4 %feed.1 = (bf16[128,2048]{1,0:T(8,128)(2,1)}, bf16[8,128,2048]{2,1,0:T(8,128)(2,1)}, bf16[8,128,2048]{2,1,0:T(8,128)(2,1)}, bf16[8,128,2304]{2,1,0:T(8,128)(2,1)...) custom-call(s32[16]{0:T(128)} %clusters_ref.1, f32[128,2048]{1,0:T(8,128)} %get-tuple-element.44.normed_ref, ...), custom_call_target="tpu_custom_call" | custom-call | flops 12884901888 | bytes 20000000 | tf_op jit(solution)/shard_map/feed/pallas_call | solution.py:764
  203.3 0.0 copy-start.2
  203.3 87.0 %feed_back.1 = (f32[128,2048]{1,0:T(8,128)}, bf16[8,128,2048]{2,1,0:T(8,128)(2,1)}, bf16[1024,256]{1,0:T(8,128)(2,1)}, f32[2,8,2048]{2,1,0:T(8,128)}, bf16[3,4,176,128]{3,2,1,0:T(8,128)(2,1)}) custom-call(bf16[8,128,2304]{2,1,0:T(8,128)(2,1)} %get-tuple-element.48.act_hbm, f32[128,2048]{1,0:T(8,128)} %get-tuple-element.49.gz_ref, ...), custom_call_target="tpu_custom_call" | custom-call | flops 16106127360 | bytes 20000000 | tf_op jit(solution)/shard_map/feed_back/pallas_call | solution.py:764
  290.3 1.0 reduce_sum.18
  291.2 0.0 copy-done.2
  291.3 0.7 maximum_maximum_fusion.vec_in_ref
  292.0 119.4 %input.1 = (f32[128,16,128]{2,1,0:T(8,128)}, bf16[2,2,4,512,256]{4,3,2,1,0:T(8,128)(2,1)}, f32[8,2048]{1,0:T(8,128)}, bf16[3,4,2,2,704,128]{5,4,3,2,1,0:T(8,128)(2,1)}) custom-call(s32[1]{0:T(128)S(6)} %copy.27.prefix_ref, bf16[1024,256]{1,0:T(8,128)(2,1)} %get-tuple-element.40.q_ref, bf16[1024,256]{1,0:T(8,128)(2,1)} %get-tuple-element.41.k_ref, ...), custom_call_target="tpu_custom_call" | custom-call | flops 3221225472 | bytes 20000000 | tf_op jit(solution)/shard_map/input/pallas_call | solution.py:764
  411.4 1.5 fusion
  412.9 0.0 copy-start.1
  412.9 0.0 copy-start
  412.9 16.1 %outputs.1 = (f32[5461,2,256]{2,1,0:T(2,128)}, f32[5461,256]{1,0:T(8,128)}, f32[6144,256]{1,0:T(8,128)}, f32[256,2048]{1,0:T(8,128)}) custom-call(bf16[3,4,2,2,704,128]{5,4,3,2,1,0:T(8,128)(2,1)} %get-tuple-element.63.feed_ref, bf16[8192,256]{1,0:T(8,128)(2,1)} %bitcast.24, bf16[8192,256]{1,0:T(8,128)(2,1)} %bitcast.25), custom_call_target="tpu_custom_call" | custom-call | tf_op jit(solution)/shard_map/outputs/pallas_call | solution.py:1211
  429.0 0.0 copy-done.1
  429.0 0.8 copy.28
  429.8 0.0 copy-done
  429.8 1.0 copy.29
  (2 shorter events, 0.1 us)
Async XLA Ops:
  203.3 88.0 %copy-start.2 = (f32[2,8,2048]{2,1,0:T(8,128)S(1)}, f32[2,8,2048]{2,1,0:T(8,128)}, u32[]{:S(2)}) copy-start(f32[2,8,2048]{2,1,0:T(8,128)} %get-tuple-element.61) | copy-start | bytes 393220
  412.9 16.1 %copy-start.1 = (bf16[128,2048]{1,0:T(8,128)(2,1)S(1)}, bf16[128,2048]{1,0:T(8,128)(2,1)}, u32[]{:S(2)}) copy-start(bf16[128,2048]{1,0:T(8,128)(2,1)} %get-tuple-element.47) | copy-start | bytes 1572868
  412.9 16.9 %copy-start = (f32[128,16,128]{2,1,0:T(8,128)S(1)}, f32[128,16,128]{2,1,0:T(8,128)}, u32[]{:S(2)}) copy-start(f32[128,16,128]{2,1,0:T(8,128)} %get-tuple-element.62) | copy-start | bytes 3145732

commit v4 on v3

--- a/solution.py
+++ b/solution.py
@@ -53,6 +53,9 @@
         core = 1 - self.core if sibling else self.core
         return (z_lo * 8 + x * 2 + core, y * 2 + z_hi)
 
+    def beside(self):
+        return (lax.rem(lax.axis_index("dp") + 8, 16), lax.axis_index("seq"))
+
     def z_at(self, offset):
         z = lax.rem(self.z + offset, 4)
         return z // 2, lax.rem(z, 2)
@@ -67,6 +70,7 @@
         pl.semaphore_wait(gate, len(where))
 
     def start(self, src, dst, where):
+        assert self.count < self.send.shape[0]
         copy = pltpu.make_async_remote_copy(
             src_ref=src,
             dst_ref=dst,
@@ -85,14 +89,44 @@
         return pl.multiple_of((lax.rem(self.y + step, 4) * 2 + half) * ROWS, ROWS)
 
 
-def together(*tasks):
-    due = [[next(task), i, task] for i, task in enumerate(tasks)]
-    while due:
-        due.sort(key=lambda entry: entry[:2])
+class Once:
+    def __init__(self, *copies):
+        self.copies = list(copies)
+
+    def wait_recv(self):
+        while self.copies:
+            self.copies.pop().wait_recv()
+
+
+class Mark:
+    done = False
+
+
+class Local:
+    def __init__(self, src, dst, sem):
+        self.copy = pltpu.make_async_copy(src, dst, sem)
+        self.copy.start()
+
+    def wait_recv(self):
+        self.copy.wait()
+
+
+def together(order, *tasks):
+    tasks = list(tasks)
+    for task in tasks:
+        next(task)
+    left = len(tasks)
+    for which in order:
         try:
-            due[0][0] = next(due[0][2])
+            next(tasks[which])
         except StopIteration:
-            due.pop(0)
+            left -= 1
+    assert left == 0
+
+
+def alone(task):
+    for _ in task:
+        pass
 
 
 def received(*copies):
@@ -119,31 +153,32 @@
     u0, d1 = send(0, H0, 1, up), send(0, H1, 2, down)
     z0, z1 = send(0, H0, 4, across), send(0, H1, 4, across)
     u1, d0 = send(0, H1, 1, up), send(0, H0, 2, down)
-    yield 6
+    yield u0, d1
     received(u0)
     fu = send(1, H0, 3, up)
     received(d1)
     fd = send(2, H1, 3, down)
-    yield 12
+    yield z0, z1
     received(z0)
     pu0 = send(4, H0, 5, up)
     received(z1)
     pd1 = send(4, H1, 6, down)
     pu1, pd0 = send(4, H1, 5, up), send(4, H0, 6, down)
+    yield u1, d0
     received(u1, d0)
     work((0, 1))
-    yield 19
+    yield fu, fd
     received(fu, fd)
     work((2, 3))
-    yield 24
+    yield pu0, pd1
     received(pu0)
     gu = send(5, H0, 7, up)
     received(pd1)
     gd = send(6, H1, 7, down)
-    yield 29
+    yield pu1, pd0
     received(pu1, pd0)
     work((4, 5))
-    yield 36
+    yield gu, gd
     received(gu, gd)
     work((6, 7))
     sent(copies)
@@ -245,34 +280,36 @@
     compute((5, 6))
     z1, z2 = cross_b(1), cross_b(2)
     compute((1, 2))
-    yield 8
+    yield far_other
+    near_other = near_a(4, far_other)
+    compute((4, 0))
+    z0 = cross_b(0)
+    yield (z3,)
     received(z3)
     add_rows(sums, 3, B, from_z[3])
     far_b = (
         send(sums.at[3, B0], b_far.at[pl.ds(0, 16)], up),
         send(sums.at[3, B1], b_far.at[pl.ds(16, 32)], down),
     )
-    near_other = near_a(4, far_other)
-    compute((4, 0))
-    z0 = cross_b(0)
-    yield 12
+    yield far_own
     near_own = near_a(0, far_own)
-    yield 18
+    yield z1, z2
+    received(z2)
+    add_rows(sums, 2, B, from_z[2])
+    received(z1)
+    add_rows(sums, 1, B, from_z[1])
+    yield far_b
+    received(far_b[0])
+    add_rows(sums, 2, B0, b_far[0:16])
+    near_b0 = send(sums.at[2, B], b_near.at[0], up)
+    received(far_b[1])
+    add_rows(sums, 1, B1, b_far[16:48])
+    near_b1 = send(sums.at[1, B], b_near.at[1], down)
+    yield near_other
     received(*near_other)
     add_rows(sums, 4, A, a_near[1, 0], a_near[1, 1])
     z_a = send(sums.at[4, A], a_z, across)
-    yield 20
-    received(z2)
-    add_rows(sums, 2, B, from_z[2])
-    received(far_b[0])
-    add_rows(sums, 2, B0, b_far[0:16])
-    near_b0 = send(sums.at[2, B], b_near.at[0], up)
-    received(z1)
-    add_rows(sums, 1, B, from_z[1])
-    received(far_b[1])
-    add_rows(sums, 1, B1, b_far[16:48])
-    near_b1 = send(sums.at[1, B], b_near.at[1], down)
-    yield 27
+    yield z0, near_b0, near_b1
     received(z0, near_b0, near_b1)
     total[80:128] = (
         sums[0, B].astype(F32)
@@ -280,8 +317,8 @@
         + b_near[0].astype(F32)
         + b_near[1].astype(F32)
     )
+    yield (z_a, *near_own)
     received(*near_own)
-    yield 30
     received(z_a)
     total[0:80] = (
         sums[0, A].astype(F32)
@@ -327,14 +364,14 @@
     nd0 = send(sums.at[1, H0], near.at[1, H0], down)
     compute((4, 0))
     s0 = send(sums.at[4], from_side.at[0], side)
-    yield 8
+    yield fu, fd
     received(fu)
     add_rows(sums, 2, H0, far[0:64])
     nu0 = send(sums.at[2, H0], near.at[0, H0], up)
     received(fd)
     add_rows(sums, 1, H1, far[64:128])
     nd1 = send(sums.at[1, H1], near.at[1, H1], down)
-    yield 17
+    yield s0, nu1, nd0, nu0, nd1
     received(s0, nu1, nd0, nu0, nd1)
     total[...] = (
         sums[0].astype(F32)
@@ -349,52 +386,54 @@
 GU = pl.ds(0, 2)
 
 
-def two_rings(links, at, first, second, times):
-    up, down = first
-    right, left = second
-    copies = []
-
-    def send(ref, where):
-        copies.append(links.start(ref, ref, where))
-        return copies[-1]
-
-    def both(a):
-        return send(at(a, 0), right), send(at(a, 0), left)
-
-    def onward(a):
-        return send(at(a, 3, Y0), right), send(at(a, 1, Y1), left)
-
-    u, d = send(at(0, 0), up), send(at(0, 0), down)
-    near = [both(0)]
-    yield times[0]
-    received(u)
-    fu = send(at(3, 0, Y0), up)
-    near.append(both(3))
-    received(d)
-    fd = send(at(1, 0, Y1), down)
-    near.append(both(1))
-    yield times[1]
-    received(*near[0])
-    far = [*onward(0)]
-    received(fu, fd)
-    near.append(both(2))
-    for i, a in enumerate((3, 1, 2)):
-        yield times[2 + i]
-        received(*near[1 + i])
-        far += onward(a)
-    yield times[5]
-    received(*far)
-    sent(copies)
-
-
 def across_y(links, piece, own, local):
-    keep = pltpu.make_async_copy(piece(links.y), own(), local)
-    keep.start()
     copies = []
     for step in (2, 1, 3):
         there = lax.rem(links.y + step, 4)
         copies.append(links.start(piece(there), own(), links.to(y=step)))
-    return keep, copies
+    keep = Local(piece(links.y), own(), local)
+    return Once(keep, *copies), copies
+
+
+def ring_gather(links, arrived, at, first, second):
+    up, down = first
+    right, left = second
+    copies = []
+
+    def send(ref, where):
+        copies.append(links.start(ref, ref, where))
+        return copies[-1]
+
+    def both(a):
+        return send(at(a, 0), right), send(at(a, 0), left)
+
+    def onward(a):
+        return send(at(a, 3, Y0), right), send(at(a, 1, Y1), left)
+
+    yield (arrived,)
+    received(arrived)
+    u, d = send(at(0, 0), up), send(at(0, 0), down)
+    near = [both(0)]
+    yield u, d
+    received(u)
+    fu = send(at(3, 0, Y0), up)
+    received(d)
+    fd = send(at(1, 0, Y1), down)
+    near.append(both(3))
+    near.append(both(1))
+    yield near[0]
+    received(*near[0])
+    far = [*onward(0)]
+    yield fu, fd
+    received(fu, fd)
+    near.append(both(2))
+    for i, a in enumerate((3, 1, 2)):
+        yield near[1 + i]
+        received(*near[1 + i])
+        far += onward(a)
+    yield far
+    received(*far)
+    sent(copies)
 
 
 def spread(links, piece, w, matrices, local):
@@ -409,44 +448,27 @@
     def own():
         return w.at[:, links.z_hi, links.y, links.z_lo, links.part(0)]
 
-    keep, copies = across_y(links, lambda y: piece.at[y, matrices], own, local)
-    yield 8
-    keep.wait()
-    received(*copies)
-    count = matrices.size
-    rings = [
-        two_rings(
-            links, lambda a, b, y=every: place(0, a, b, y), along_z, along_x, (14, 19, 24, 29, 34, 39)
-        )
-    ]
-    if count == 2:
-        rings.append(
-            two_rings(
-                links, lambda a, b, y=every: place(1, b, a, y), along_x, along_z, (15, 23, 29, 34, 39, 44)
-            )
-        )
-    due = [[next(ring), i, ring] for i, ring in enumerate(rings)]
-    while due:
-        due.sort(key=lambda entry: entry[:2])
-        yield due[0][0]
-        try:
-            due[0][0] = next(due[0][2])
-        except StopIteration:
-            due.pop(0)
-    sent(copies)
-
-
-BLOCKS = pltpu.VMEM((2, 2, 4, 2, PART, 128), BF16)
+    arrived, copies = across_y(links, lambda y: piece.at[y, matrices], own, local)
+
+    def one():
+        yield from ring_gather(links, arrived, lambda a, b, y=every: place(0, a, b, y), along_z, along_x)
+        sent(copies)
+
+    def two():
+        yield from ring_gather(links, arrived, lambda a, b, y=every: place(1, b, a, y), along_x, along_z)
+
+    return (one(),) if matrices.size == 1 else (one(), two())
+
+
+def ring_scratch(*block):
+    return [pltpu.VMEM(block, BF16), pltpu.VMEM((2, *block), BF16)]
+
+
 REDUCE_SCRATCH = (
-    pltpu.VMEM((3, 2, 4, 2, FF, 128), BF16),
-    BLOCKS,
-    pltpu.VMEM((2, 2, 2, 4, 2, PART, 128), BF16),
-    pltpu.VMEM((2, 4, PART, 128), BF16),
-    pltpu.VMEM((2, 2, 4, PART, 128), BF16),
-    pltpu.VMEM((4, FF, 128), BF16),
-    pltpu.VMEM((2, 4, FF, 128), BF16),
-    pltpu.VMEM((4, PART, 128), BF16),
-    pltpu.VMEM((2, 4, PART, 128), BF16),
+    pltpu.VMEM((3, 4, 2, 2, FF, 128), BF16),
+    *ring_scratch(4, 2, 2, PART, 128), *ring_scratch(4, PART, 128),
+    *ring_scratch(4, 2, 2, PART, 128), *ring_scratch(4, PART, 128),
+    *ring_scratch(4, FF, 128), *ring_scratch(4, PART, 128),
 )
 
 
@@ -462,9 +484,8 @@
     lax.fori_loop(0, count, step, 0)
 
 
-def reduce(links, bufs, make, shard):
-    g, fx, nx, fz, nz, fz2, nz2, fx2, nx2 = bufs
-    xp, xm, zp, zm = links.to(x=1), links.to(x=3), links.to(z=1), links.to(z=3)
+def ring_reduce(links, at, blocks, ring, far, near, devices):
+    up, down = devices
     copies = []
     every = pl.ds(0, 4)
 
@@ -472,94 +493,73 @@
         copies.append(links.start(src, dst, where))
         return copies[-1]
 
-    def along_x(k, x):
-        return g.at[k, :, :, :, links.part(x)]
-
-    def block_x(k, x):
-        return lambda i: g.at[k, i // 8, lax.rem(i // 2, 4), lax.rem(i, 2), links.part(x)]
-
-    def plain(ref):
-        return lambda i: ref.at[i // 8, lax.rem(i // 2, 4), lax.rem(i, 2)]
-
-    def along_z(k, z, y=every, rows=pl.ds(0, FF)):
-        z_hi, z_lo = links.z_at(z)
-        return g.at[k, z_hi, y, z_lo, rows]
-
-    def block_z(k, z, rows, first=0):
-        z_hi, z_lo = links.z_at(z)
-        return lambda i: g.at[k, z_hi, i + first, z_lo, rows]
-
-    def shift(ref, first=0):
-        return lambda i: ref.at[i + first]
-
-    here = links.part(0)
-    whole = pl.ds(0, FF)
-    yield from make(0)
-    c1, c4 = send(along_x(0, 2), fx.at[0], xp), send(along_x(0, 3), nx.at[1, 0], xm)
-    yield from make(1)
-    c2, c3 = send(along_x(1, 2), fx.at[1], xm), send(along_x(1, 1), nx.at[0, 1], xp)
-    yield from make(2)
-    e1 = send(along_z(2, 2, Y0), fz2.at[Y0], zp)
-    e2 = send(along_z(2, 2, Y1), fz2.at[Y1], zm)
-    e3 = send(along_z(2, 1, Y1), nz2.at[0, Y1], zp)
-    e4 = send(along_z(2, 3, Y0), nz2.at[1, Y0], zm)
-    yield 31
-    received(c1)
-    accumulate(16, block_x(0, 1), plain(fx.at[0]))
-    c5 = send(along_x(0, 1), nx.at[0, 0], xp)
-    yield 36
-    received(e1)
-    accumulate(2, block_z(2, 1, whole), shift(fz2))
-    e5 = send(along_z(2, 1, Y0), nz2.at[0, Y0], zp)
-    received(e2)
-    accumulate(2, block_z(2, 3, whole, 2), shift(fz2, 2))
-    e6 = send(along_z(2, 3, Y1), nz2.at[1, Y1], zm)
-    yield 42
-    received(c2)
-    accumulate(16, block_x(1, 3), plain(fx.at[1]))
-    c6 = send(along_x(1, 3), nx.at[1, 1], xm)
-    yield 53
-    received(e3, e4, e5, e6)
-    accumulate(4, block_z(2, 0, whole), shift(nz2.at[0]), shift(nz2.at[1]))
-    d1 = send(along_z(2, 0, Y0, links.part(2)), fx2.at[Y0], xp)
-    d2 = send(along_z(2, 0, Y1, links.part(2)), fx2.at[Y1], xm)
-    d3 = send(along_z(2, 0, Y1, links.part(1)), nx2.at[0, Y1], xp)
-    d4 = send(along_z(2, 0, Y0, links.part(3)), nx2.at[1, Y0], xm)
-    yield 62
-    received(c3, c4, c5, c6)
-    for k in range(2):
-        accumulate(16, block_x(k, 0), plain(nx.at[0, k]), plain(nx.at[1, k]))
-    f1 = send(along_z(0, 2, every, here), fz.at[0], zp)
-    f2 = send(along_z(1, 2, every, here), fz.at[1], zm)
-    f3 = send(along_z(1, 1, every, here), nz.at[0, 1], zp)
-    f4 = send(along_z(0, 3, every, here), nz.at[1, 0], zm)
-    received(d1)
-    accumulate(2, block_z(2, 0, links.part(1)), shift(fx2))
-    d5 = send(along_z(2, 0, Y0, links.part(1)), nx2.at[0, Y0], xp)
-    received(d2)
-    accumulate(2, block_z(2, 0, links.part(3), 2), shift(fx2, 2))
-    d6 = send(along_z(2, 0, Y1, links.part(3)), nx2.at[1, Y1], xm)
-    yield 68
-    received(f1)
-    accumulate(4, block_z(0, 1, here), shift(fz.at[0]))
-    f5 = send(along_z(0, 1, every, here), nz.at[0, 0], zp)
-    received(f2)
-    accumulate(4, block_z(1, 3, here), shift(fz.at[1]))
-    f6 = send(along_z(1, 3, every, here), nz.at[1, 1], zm)
-    yield 75
-    received(d3, d4, d5, d6)
-    accumulate(4, block_z(2, 0, here), shift(nx2.at[0]), shift(nx2.at[1]))
-    received(f3, f4, f5, f6)
-    for k in range(2):
-        accumulate(4, block_z(k, 0, here), shift(nz.at[0, k]), shift(nz.at[1, k]))
-    for k in range(3):
-        shard[k] = along_z(k, 0, every, here)[...]
+    half = ring // 2
+    fu, fd = send(at(2, Y0), far.at[Y0], up), send(at(2, Y1), far.at[Y1], down)
+    nu, nd = send(at(1, Y1), near.at[0, Y1], up), send(at(3, Y0), near.at[1, Y0], down)
+    yield fu, fd
+    received(fu)
+    accumulate(half, lambda i: blocks(at(1, every), i), lambda i: blocks(far, i))
+    mu = send(at(1, Y0), near.at[0, Y0], up)
+    received(fd)
+    accumulate(half, lambda i: blocks(at(3, every), i + half), lambda i: blocks(far, i + half))
+    md = send(at(3, Y1), near.at[1, Y1], down)
+    yield nu, nd, mu, md
+    received(nu, nd, mu, md)
+    accumulate(
+        ring, lambda i: blocks(at(0, every), i), lambda i: blocks(near.at[0], i), lambda i: blocks(near.at[1], i)
+    )
     sent(copies)
 
 
-def regather(links, at, half, times):
+def reduce(links, bufs, make, shard):
+    g = bufs[0]
+    along_x = (links.to(x=1), links.to(x=3))
+    along_z = (links.to(z=1), links.to(z=3))
+    made = [Mark(), Mark()]
+
+    def one(k, x_first):
+        far, near, far2, near2 = bufs[1 + 4 * k : 5 + 4 * k]
+        z_hi, z_lo = links.z_at(0)
+
+        def along_z_at(a, y):
+            hi, lo = links.z_at(a)
+            return g.at[k, y, hi, lo]
+
+        def along_x_at(a, y):
+            return g.at[k, y, :, :, links.part(a)]
+
+        def rest_z(a, y):
+            hi, lo = links.z_at(a)
+            return g.at[k, y, hi, lo, links.part(0)]
+
+        def rest_x(a, y):
+            return g.at[k, y, z_hi, z_lo, links.part(a)]
+
+        def four(ref, i):
+            return ref.at[i // 4, lax.rem(i // 2, 2), lax.rem(i, 2)]
+
+        def plain(ref, i):
+            return ref.at[i]
+
+        if k:
+            yield (made[k - 1],)
+        yield from make(k)
+        if k < 2:
+            made[k].done = True
+        if x_first:
+            yield from ring_reduce(links, along_x_at, four, 16, far, near, along_x)
+            yield from ring_reduce(links, rest_z, plain, 4, far2, near2, along_z)
+        else:
+            yield from ring_reduce(links, along_z_at, plain, 4, far, near, along_z)
+            yield from ring_reduce(links, rest_x, plain, 4, far2, near2, along_x)
+        shard[k] = g[k, :, z_hi, z_lo, links.part(0)]
+
+    return one(0, True), one(1, True), one(2, False)
+
+
+def regather(links, at, half):
     xp, xm, side = links.to(x=1), links.to(x=3), links.to(sibling=True)
-    beside = (lax.rem(lax.axis_index("dp") + 8, 16), lax.axis_index("seq"))
+    beside = links.beside()
     copies, sides = [], []
 
     def send(ref, where):
@@ -572,39 +572,35 @@
     z = send(at(0, 0), beside)
     near = [(send(at(0, 0), xp), send(at(0, 0), xm))]
     share(at(0, 0))
-    yield times[0]
+    yield (z,)
     received(z)
     near.append((send(at(1, 0), xp), send(at(1, 0), xm)))
     share(at(1, 0))
+    far = []
     for i in range(2):
-        yield times[1 + 2 * i]
+        yield near[i]
         received(near[i][0])
         far_up = send(half(at(i, 3), 0), xp)
+        received(near[i][1])
+        far.append((far_up, send(half(at(i, 1), 1), xm)))
         share(at(i, 3))
-        received(near[i][1])
-        far_down = send(half(at(i, 1), 1), xm)
         share(at(i, 1))
-        yield times[2 + 2 * i]
-        received(far_up, far_down)
+    for i in range(2):
+        yield far[i]
+        received(*far[i])
         share(at(i, 2))
+    yield sides
     received(*sides)
     sent(copies)
 
 
-def collect(links, shard, out, local, late):
-    copies = []
-
-    def own(y):
-        return out.at[:, y, links.core, links.z_lo, links.part(0)]
-
-    keep = pltpu.make_async_copy(shard.at[:, links.y], own(links.y), local)
-    keep.start()
-    for step in (2, 1, 3):
-        there = lax.rem(links.y + step, 4)
-        copies.append(links.start(shard.at[:, there], own(links.y), links.to(y=step)))
-    yield 7
-    keep.wait()
-    received(*copies)
+def collect(links, shard, out, local):
+    def own():
+        return out.at[:, links.y, links.core, links.z_lo, links.part(0)]
+
+    arrived, copies = across_y(links, lambda y: shard.at[:, y], own, local)
+    yield (arrived,)
+    received(arrived)
 
     def at(z, x):
         return out.at[:, :, links.core, lax.rem(links.z_lo + z, 2), links.part(x)]
@@ -612,24 +608,26 @@
     def half(ref, i):
         return ref.at[:, pl.ds(2 * i, 2)]
 
-    yield from regather(links, at, half, [t + late for t in (12, 18, 24, 32, 45)])
+    yield from regather(links, at, half)
     sent(copies)
 
 
-SHARE_SCRATCH = (
-    pltpu.VMEM((2, 2, 4, 512, 256), BF16),
-    pltpu.VMEM((2, 4, 512, 256), BF16),
-    pltpu.VMEM((2, 512, 256), BF16),
-    pltpu.VMEM((2, 2, 512, 256), BF16),
-    pltpu.VMEM((512, 256), BF16),
-)
-
-
-def share(links, bufs, out, late):
+def share_scratch(rows, lanes):
+    return [
+        pltpu.VMEM((2, 2, 4, rows, lanes), BF16),
+        pltpu.VMEM((2, 4, rows, lanes), BF16),
+        pltpu.VMEM((2, rows, lanes), BF16),
+        pltpu.VMEM((2, 2, rows, lanes), BF16),
+        pltpu.VMEM((rows, lanes), BF16),
+    ]
+
+
+def share(links, bufs, out):
     q, from_side, far, near, from_z = bufs
     xp, xm, side = links.to(x=1), links.to(x=3), links.to(sibling=True)
-    beside = (lax.rem(lax.axis_index("dp") + 8, 16), lax.axis_index("seq"))
+    beside = links.beside()
     core, z_lo = links.core, links.z_lo
+    count = q.shape[3]
     copies = []
 
     def send(src, dst, where):
@@ -642,28 +640,32 @@
     def rows(ref):
         return lambda i: ref.at[pl.ds(pl.multiple_of(i * 64, 64), 64)]
 
+    def add(target, *others):
+        accumulate(count // 64, rows(target), *(rows(other) for other in others))
+
     s = send(q.at[1 - core], from_side, side)
-    yield late
+    yield (s,)
     received(s)
+    for x in (2, 1, 3, 0):
+        for z in range(2):
+            add(q.at[core, z, there(x)], from_side.at[z, there(x)])
+        if x == 2:
+            fu, fd = send(q.at[core, 0, there(2)], far.at[0], xp), send(q.at[core, 1, there(2)], far.at[1], xm)
+    nu = send(q.at[core, 1, there(1)], near.at[0, 1], xp)
+    nd = send(q.at[core, 0, there(3)], near.at[1, 0], xm)
+    yield fu, fd
+    received(fu)
+    add(q.at[core, 0, there(1)], far.at[0])
+    mu = send(q.at[core, 0, there(1)], near.at[0, 0], xp)
+    received(fd)
+    add(q.at[core, 1, there(3)], far.at[1])
+    md = send(q.at[core, 1, there(3)], near.at[1, 1], xm)
+    yield nu, nd, mu, md
+    received(nu, nd, mu, md)
     for z in range(2):
-        for x in range(4):
-            accumulate(8, rows(q.at[core, z, x]), rows(from_side.at[z, x]))
-    a1, a2 = send(q.at[core, 0, there(2)], far.at[0], xp), send(q.at[core, 1, there(2)], far.at[1], xm)
-    a3 = send(q.at[core, 1, there(1)], near.at[0, 1], xp)
-    a4 = send(q.at[core, 0, there(3)], near.at[1, 0], xm)
-    yield late + 8
-    received(a1)
-    accumulate(8, rows(q.at[core, 0, there(1)]), rows(far.at[0]))
-    a5 = send(q.at[core, 0, there(1)], near.at[0, 0], xp)
-    received(a2)
-    accumulate(8, rows(q.at[core, 1, there(3)]), rows(far.at[1]))
-    a6 = send(q.at[core, 1, there(3)], near.at[1, 1], xm)
-    yield late + 20
-    received(a3, a4, a5, a6)
-    for z in range(2):
-        accumulate(8, rows(q.at[core, z, there(0)]), rows(near.at[0, z]), rows(near.at[1, z]))
+        add(q.at[core, z, there(0)], near.at[0, z], near.at[1, z])
     b = send(q.at[core, 1 - z_lo, there(0)], from_z, beside)
-    yield late + 26
+    yield (b,)
     received(b)
 
     def finish(i, carry):
@@ -672,15 +674,15 @@
         out[core, z_lo, links.x, at] = value.astype(BF16)
         return carry
 
-    lax.fori_loop(0, 8, finish, 0)
+    lax.fori_loop(0, count // 64, finish, 0)
 
     def at(z, x):
         return out.at[core, lax.rem(z_lo + z, 2), there(x)]
 
     def half(ref, i):
-        return ref.at[pl.ds(256 * i, 256)]
-
-    yield from regather(links, at, half, [t + late for t in (33, 36, 42, 46, 54)])
+        return ref.at[pl.ds(count // 2 * i, count // 2)]
+
+    yield from regather(links, at, half)
     sent(copies)
 
 
@@ -694,13 +696,13 @@
         links.to(z=2),
         links.to(x=1 + 2 * lax.rem(x, 2)),
         links.to(x=2),
-        (lax.rem(lax.axis_index("dp") + 8, 16), lax.axis_index("seq")),
+        links.beside(),
     )
     held, got = bufs
     held[0] = vec[...]
     for i, where in enumerate(steps):
         copies.append(links.start(held.at[i], got.at[i], where))
-        yield 6 + 6 * i
+        yield (copies[-1],)
         received(copies[-1])
         if i < len(steps) - 1:
             held[i + 1] = held[i] + got[i]
@@ -773,6 +775,12 @@
         ),
         cost_estimate=pl.CostEstimate(flops=flops, bytes_accessed=20_000_000, transcendentals=0),
     )(*operands)
+
+
+PROJECT = (1, 2, 0, 0, 1, 2, 1, 0, 2, 1, 1, 0, 1, 0, 2, 2, 2, 0, 1, 2, 0, 1, 2)
+ATTENDED = (1, 0, 0, 0, 0, 1, 1, 0, 0, 1, 1, 1, 0, 0, 1, 1)
+FEED_BACK = (1, 1, 2, 2, 2, 3, 3, 3, 0, 1, 0, 3, 2, 0, 0, 0, 0, 1, 3, 1, 0, 2, 3, 1, 0, 2, 3, 0, 2)
+INPUT = (2, 1, 0, 5, 2, 1, 2, 3, 3, 5, 2, 3, 0, 2, 0, 3, 2, 4, 4, 2, 5, 1, 4, 0, 2, 2, 2, 0, 3, 2, 2, 4, 5, 1, 3, 0, 0, 4, 2, 2, 1, 5, 3, 1, 3, 4, 1, 5, 3, 4, 3, 5, 1, 4, 1, 3, 3, 4, 1, 4, 4, 4)
 
 
 def piece_kernel(place_ref, gate_up_ref, down_ref, out_ref):
@@ -839,7 +847,7 @@
         yield from gather(links, all_ref, work)
         written.start()
 
-    together(tokens(), spread(links, piece_ref, w_all_ref, GU, local))
+    together(PROJECT, tokens(), *spread(links, piece_ref, w_all_ref, GU, local))
     written.wait()
 
 
@@ -908,7 +916,7 @@
         yield from scatter(links, bufs, compute, total)
         by_chunks(finish)
 
-    together(chain(), spread(links, piece_ref, w_all_ref, pl.ds(2, 1), local))
+    together(ATTENDED, chain(), *spread(links, piece_ref, w_all_ref, pl.ds(2, 1), local))
 
 
 class Loads:
@@ -971,7 +979,7 @@
                 slope[slot, :, cols] = turn[part]
                 act_ref[slot, :, 2 * COLS + c : 2 * COLS + c + 256] = hidden[part]
 
-    together(gather_near(links, all_ref, forward))
+    alone(gather_near(links, all_ref, forward))
     written.start(all_ref, all_out, out_sem.at[8])
 
     def compute(pair):
@@ -982,7 +990,7 @@
             for i, slot in enumerate(pair):
                 bufs[0][slot, :, d : d + 512] = result[i * ROWS : (i + 1) * ROWS]
 
-    together(scatter_near(links, bufs, compute, total))
+    alone(scatter_near(links, bufs, compute, total))
     vec_ref[...] = jnp.zeros_like(vec_ref)
     own, same = clusters_ref[lax.axis_index("dp")], np.float32(0.0)
     for i in range(clusters_ref.shape[0]):
@@ -1013,7 +1021,7 @@
         for slot in pair:
             written.start(act_ref.at[slot], act_out.at[slot], out_sem.at[slot])
 
-    together(gather_near(links, gz_all_ref, backward))
+    alone(gather_near(links, gz_all_ref, backward))
     written.start(gz_all_ref, gz_all_out, out_sem.at[9])
     written.wait()
 
@@ -1023,7 +1031,7 @@
     gz1_ref, all_out, grad_heads_ref, vec_ref, shard_ref,
     act_ref, rows_ref, all_ref, w, total, w_sem, sem, *rest,
 ):
-    bufs, more, (send, recv) = rest[:4], rest[4:13], rest[13:]
+    bufs, more, (send, recv) = rest[:4], rest[4:17], rest[17:]
     links = Links(send, recv)
     load_act, load_rows = Loads(), Loads()
     load_act.start(act_hbm, act_ref, sem.at[0])
@@ -1065,8 +1073,7 @@
         yield from scatter_near(links, bufs, compute, total)
         vec_ref[...] = jnp.zeros_like(vec_ref)
         by_chunks(finish)
-        for time in gather(links, all_ref, work):
-            yield time + 24
+        yield from gather(links, all_ref, work)
         written.start(all_ref, all_out, sem.at[3])
 
     g = more[0]
@@ -1081,71 +1088,82 @@
                 result = dot_rows(left, right)[:height].astype(BF16)
                 for i in range(4):
                     at = d // 128 + i
-                    g[k, at // 2 % 2, at // 4, at % 2, c : c + height] = result[:, i * 128 : i * 128 + 128]
+                    g[k, at // 4, at // 2 % 2, at % 2, c : c + height] = result[:, i * 128 : i * 128 + 128]
             if k == 1 and c == 512:
                 load_rows.start(gz_all_hbm, rows_ref, sem.at[2])
-            yield 8 + 6 * k + c // 128
-
-    together(chain(), reduce(links, more, make, shard_ref))
+            if c < 512:
+                yield ()
+
+    together(FEED_BACK, chain(), *reduce(links, more, make, shard_ref))
     written.wait()
 
 
 def input_kernel(
     prefix_ref, q_ref, k_ref, v_ref, g_ref, lse_ref, cos_ref, sin_ref,
     w_hbm, gz1_ref, tokens_hbm, heads_ref, gz_all_hbm, shard_ref, vec_in_ref,
-    out_ref, q_out_ref, vec_ref, feed_ref,
-    total, w_ref, tokens_ref, gz_all_ref, back, grads, heads, key_sum, value_sum, held, got, local, sem, *rest,
+    out_ref, one_ref, two_ref, whole_ref, vec_ref, feed_ref,
+    total, w_ref, tokens_ref, gz_all_ref, grads, heads, key_sum, value_sum, held, got, local, sem, *rest,
 ):
-    bufs, more, (send, recv) = rest[:7], rest[7:12], rest[12:]
+    bufs, more, (send, recv) = rest[:7], rest[7:22], rest[22:]
     links = Links(send, recv)
     to = links.to
-    loads = Loads()
-    loads.start(w_hbm, w_ref, sem.at[0])
-    loads.start(tokens_hbm, tokens_ref, sem.at[1])
-    loads.start(gz_all_hbm, gz_all_ref, sem.at[2])
-    beside = (lax.rem(lax.axis_index("dp") + 8, 16), lax.axis_index("seq"))
+    load_gz, load_tokens, load_w = Loads(), Loads(), Loads()
+    load_gz.start(gz_all_hbm, gz_all_ref, sem.at[2])
+    load_tokens.start(tokens_hbm, tokens_ref, sem.at[1])
+    load_w.start(w_hbm, w_ref, sem.at[0])
     links.barrier(
-        to(y=1), to(y=2), to(y=3), to(z=2), to(x=1), to(x=2), to(x=3), to(sibling=True), beside
+        to(y=1), to(y=2), to(y=3), to(z=2), to(x=1), to(x=2), to(x=3), to(sibling=True), links.beside()
     )
     vec_ref[...] = vec_in_ref[...]
     block = 512
-
-    def attend_back():
-        for head in range(2):
-            lanes = slice(head * 128, head * 128 + 128)
-            for first in range(0, LEN, block):
-                at = slice(first, first + block)
-                query, grad = q_ref[at, lanes], g_ref[at, lanes]
-                scores = dot_t(k_ref[:, lanes], query)
-                key = lax.broadcasted_iota(jnp.int32, scores.shape, 0)
-                limit = lax.broadcasted_iota(jnp.int32, (1, block), 1) + first
-                limit = jnp.maximum(limit, prefix_ref[0] - 1)
-                weights = jnp.where(key <= limit, jnp.exp(scores - lse_ref[head, :, at]), 0.0)
-                grad_weights = dot_t(v_ref[:, lanes], grad)
-                inner = jnp.sum(weights * grad_weights, axis=0, keepdims=True)
-                grad_scores = (weights * (grad_weights - inner)).astype(BF16)
-                turned = dot_rows(grad_scores, k_ref[:, lanes]) * HEAD_DIM**-0.5
-                turned = turned * cos_ref[at] - pltpu.roll(turned, 64, 1) * sin_ref[at]
-                back[at, lanes] = turned.astype(BF16)
-                grad_key = dot(grad_scores, query)
-                grad_value = dot(weights.astype(BF16), grad)
-                if first == 0:
-                    key_sum[...] = grad_key
-                    value_sum[...] = grad_value
-                else:
-                    key_sum[...] += grad_key
-                    value_sum[...] += grad_value
-                yield 4 * head + first // 200
-            turned = key_sum[...]
-            turned = turned * cos_ref[...] - pltpu.roll(turned, 64, 1) * sin_ref[...]
-            back[:, 256 + head * 128 : 384 + head * 128] = turned.astype(BF16)
-            back[:, 512 + head * 128 : 640 + head * 128] = value_sum[...].astype(BF16)
+    ready = [Mark(), Mark(), Mark()]
+
+    def attend_back(head):
+        lanes = slice(head * 128, head * 128 + 128)
+
+        def keep(part, first, value):
+            for i in range(value.shape[0] // ROWS):
+                seq = first // ROWS + i
+                d = lax.rem(seq // 2 + 4 - links.y, 4)
+                slot = 2 * d - d * (d - 1) // 2 - d * (d - 1) * (d - 2) // 3
+                slot = slot + 4 * lax.rem(links.z_hi + seq, 2)
+                at = head * 384 + part * 128
+                grads[slot, :, at : at + 128] = value[i * ROWS : (i + 1) * ROWS].astype(BF16)
+
+        for first in range(0, LEN, block):
+            at = slice(first, first + block)
+            query, grad = q_ref[at, lanes], g_ref[at, lanes]
+            scores = dot_t(k_ref[:, lanes], query)
+            key = lax.broadcasted_iota(jnp.int32, scores.shape, 0)
+            limit = lax.broadcasted_iota(jnp.int32, (1, block), 1) + first
+            limit = jnp.maximum(limit, prefix_ref[0] - 1)
+            weights = jnp.where(key <= limit, jnp.exp(scores - lse_ref[head, :, at]), 0.0)
+            grad_weights = dot_t(v_ref[:, lanes], grad)
+            inner = jnp.sum(weights * grad_weights, axis=0, keepdims=True)
+            grad_scores = (weights * (grad_weights - inner)).astype(BF16)
+            turned = dot_rows(grad_scores, k_ref[:, lanes]) * HEAD_DIM**-0.5
+            keep(0, first, turned * cos_ref[at] - pltpu.roll(turned, 64, 1) * sin_ref[at])
+            grad_key = dot(grad_scores, query)
+            grad_value = dot(weights.astype(BF16), grad)
+            if first == 0:
+                key_sum[...] = grad_key
+                value_sum[...] = grad_value
+            else:
+                key_sum[...] += grad_key
+                value_sum[...] += grad_value
+            yield ()
+        turned = key_sum[...]
+        keep(1, 0, turned * cos_ref[...] - pltpu.roll(turned, 64, 1) * sin_ref[...])
+        keep(2, 0, value_sum[...])
 
     def compute(pair):
+        load_w.wait()
         rows = pair_of(grads, pair)
         result = 0.0
         for part in range(3):
-            result = result + dot_t(rows[:, part * 256 : part * 256 + 256], w_ref[part])
+            for head in range(2):
+                at = head * 384 + part * 128
+                result = result + dot_t(rows[:, at : at + 128], w_ref[part, :, head * 128 : head * 128 + 128])
         result = result.astype(BF16)
         for i, slot in enumerate(pair):
             bufs[0][slot] = result[i * ROWS : (i + 1) * ROWS]
@@ -1156,66 +1174,86 @@
             out_ref[at, lane] = value[:, lane * 128 : lane * 128 + 128]
 
     def chain():
-        yield from attend_back()
-        for slot in range(8):
-            at = pl.ds(links.first_row(slot), ROWS)
-            heads[slot] = heads_ref[at]
-            grads[slot] = back[at]
-        loads.wait()
-        for time in scatter(links, bufs, compute, total):
-            yield time + 14
+        yield (ready[2],)
+        for head in range(2):
+            yield from attend_back(head)
+            ready[head].done = True
+            if head == 0:
+                yield ()
+        yield from scatter(links, bufs, compute, total)
         by_chunks(finish)
 
-    def qkv():
-        flat = more[0]
-        right = grads[...].reshape(LEN, 768)
+    def qkv(head):
+        flat = more[5 * head]
+        yield (ready[head],)
+        load_tokens.wait()
+        right = grads[:, :, head * 384 : head * 384 + 384].reshape(LEN, 384)
         for d in range(8):
             left = tokens_ref[:, :, d * 256 : d * 256 + 256].reshape(LEN, 256)
             result = dot_rows(left, right).astype(BF16)
             for part in range(3):
-                chunk = part * 4 + d // 2
-                flat[chunk // 8, chunk // 4 % 2, chunk % 4, d % 2 * 256 : d % 2 * 256 + 256] = result[
-                    :, part * 256 : part * 256 + 256
-                ]
-        result = dot_rows(heads[...].reshape(LEN, 256), gz_all_ref[...].reshape(LEN, WIDE)).astype(BF16)
-        for d in range(8):
-            chunk = 12 + d // 2
-            flat[chunk // 8, chunk // 4 % 2, chunk % 4, d % 2 * 256 : d % 2 * 256 + 256] = result[
-                :, d * 256 : d * 256 + 256
-            ]
-
-    def shared():
-        yield 18
-        qkv()
-        yield from share(links, more, q_out_ref, 31)
+                for i in range(2):
+                    row = part * WIDE + d * 256 + i * 128
+                    chunk, at = row // 384, row % 384
+                    flat[chunk // 8, chunk // 4 % 2, chunk % 4, at : at + 128] = result[
+                        i * 128 : i * 128 + 128, part * 128 : part * 128 + 128
+                    ]
+            if d == 3:
+                yield ()
+
+    def first_shared():
+        for slot in range(8):
+            heads[slot] = heads_ref[pl.ds(links.first_row(slot), ROWS)]
+        load_gz.wait()
+        left = heads[...].reshape(LEN, 256)
+        for d in range(0, WIDE, 512):
+            result = dot_rows(left, gz_all_ref[:, :, d : d + 512].reshape(LEN, 512)).astype(BF16)
+            for i in range(4):
+                lane = d // 128 + i
+                for j in range(2):
+                    chunk = lane // 2 * 2 + j
+                    more[10][chunk // 8, chunk // 4 % 2, chunk % 4, :, lane % 2 * 128 : lane % 2 * 128 + 128] = result[
+                        j * 128 : j * 128 + 128, i * 128 : i * 128 + 128
+                    ]
+        ready[2].done = True
+        yield from share(links, more[10:15], whole_ref)
+
+    def shared(head):
+        yield from qkv(head)
+        yield from share(links, more[5 * head : 5 * head + 5], (one_ref, two_ref)[head])
 
     together(
-        collect(links, shard_ref, feed_ref, local, 0),
+        INPUT,
+        collect(links, shard_ref, feed_ref, local),
+        first_shared(),
         chain(),
-        shared(),
+        shared(0),
+        shared(1),
         agree(links, vec_ref, (held, got)),
     )
 
 
-def outputs_kernel(feed_ref, qkv_ref, out_ref, gate_up_ref, down_ref, grad_qkv_ref, grad_out_ref):
+def outputs_kernel(feed_ref, one_ref, two_ref, out_ref, gate_up_ref, down_ref, grad_qkv_ref, grad_out_ref):
     for z in range(2):
         lanes = slice(z * 128, z * 128 + 128)
         gate_up_ref[:, 0, lanes] = feed_ref[0, 0, 0, z].astype(F32)
         gate_up_ref[:, 1, lanes] = feed_ref[1, 0, 0, z].astype(F32)
         down_ref[:, lanes] = feed_ref[2, 0, 0, z].astype(F32)
-    grad_qkv_ref[...] = qkv_ref[...].astype(F32)
+    grad_qkv_ref[:, 0:128] = one_ref[...].astype(F32)
+    grad_qkv_ref[:, 128:256] = two_ref[...].astype(F32)
     grad_out_ref[...] = out_ref[...].astype(F32)
 
 
-def outputs(feed, attention, total):
+def outputs(feed, one, two, out, total):
     return pl.pallas_call(
         outputs_kernel,
         name="outputs",
         grid=(8,),
         in_specs=[
             pl.BlockSpec((3, 1, 1, 2, FF, 128), lambda i: (0, i // 2, i % 2, 0, 0, 0)),
-            pl.BlockSpec((768, 256), lambda i: (i, 0)),
-            pl.BlockSpec((256, 256), lambda i: (24 + i, 0)),
+            pl.BlockSpec((768, 128), lambda i: (i, 0)),
+            pl.BlockSpec((768, 128), lambda i: (i, 0)),
+            pl.BlockSpec((256, 256), lambda i: (i, 0)),
         ],
         out_specs=(
             pl.BlockSpec((FF, 2, 256), lambda i: (i, 0, 0)),
@@ -1230,7 +1268,7 @@
             jax.ShapeDtypeStruct((256, WIDE), F32),
         ),
         compiler_params=pltpu.CompilerParams(vmem_limit_bytes=VMEM_BYTES),
-    )(feed, attention, attention)
+    )(feed, one, two, out)
 
 
 def on_device(
@@ -1296,15 +1334,16 @@
             pltpu.VMEM((2, COLS, WIDE), BF16), rows_f32, some(2, 16), some(4),
             *NEAR_SCRATCH, *REDUCE_SCRATCH,
         ),
-        52, 2 * LEN * WIDE * COLS * 5,
+        60, 2 * LEN * WIDE * COLS * 5,
     )
     vec = jnp.concatenate([attn_vec.sum(1), ffn_vec.sum(1), jnp.zeros((4, WIDE), F32)], axis=0)
     steps = pltpu.VMEM((7, 8, WIDE), F32)
     head_sum = pltpu.VMEM((LEN, 128), F32)
-    input_grad, attention, vec, ffn_whole = call(
+    input_grad, one, two, out_whole, vec, ffn_whole = call(
         input_kernel, "input", 4,
         [
-            ((ROWS, WIDE // 128, 128), full, "v"), ((2, 2, 4, 512, 256), low, "v"), ((8, WIDE), full, "v"),
+            ((ROWS, WIDE // 128, 128), full, "v"), ((2, 2, 4, 384, 128), low, "v"),
+            ((2, 2, 4, 384, 128), low, "v"), ((2, 2, 4, 128, 256), low, "v"), ((8, WIDE), full, "v"),
             ((3, 4, 2, 2, FF, 128), low, "h"),
         ],
         (
@@ -1314,14 +1353,14 @@
         "svvvvvvvhvhvhvv",
         (
             rows_f32, pltpu.VMEM((3, WIDE, 256), BF16), blocks_low, blocks_low,
-            pltpu.VMEM((LEN, 768), BF16), pltpu.VMEM((8, ROWS, 768), BF16),
-            pltpu.VMEM((8, ROWS, 256), BF16), head_sum, head_sum, steps, steps, one, some(3),
-            *SCATTER_SCRATCH, *SHARE_SCRATCH,
+            pltpu.VMEM((8, ROWS, 768), BF16), pltpu.VMEM((8, ROWS, 256), BF16),
+            head_sum, head_sum, steps, steps, pltpu.SemaphoreType.DMA, some(3),
+            *SCATTER_SCRATCH, *share_scratch(384, 128), *share_scratch(384, 128), *share_scratch(128, 256),
         ),
-        77, 2 * LEN * WIDE * 768,
+        130, 2 * LEN * WIDE * 768,
     )
     grad_gate_up, grad_down, grad_qkv, grad_out = outputs(
-        ffn_whole, attention.reshape(8192, 256), ff_total
+        ffn_whole, one.reshape(6144, 128), two.reshape(6144, 128), out_whole.reshape(2048, 256), ff_total
     )
     own = lax.dynamic_slice_in_dim(vec, seq * 256, 256, axis=1)
     return (

time: 439 us -> 395 us (0.90)
  Pallas kernels: 424 us -> 380 us
    pallas_call x5, Pallas kernels: 395 us -> 352 us  [call(): pl.pallas_call(body, name=name, out_shape=tuple((jax.ShapeDtypeStruct(s,...]
where the time goes in v4:
time: 395 us; the launch traced here: 388 us
  Pallas kernels  380 us (96%)
    pallas_call x5, Pallas kernels, call(): pl.pallas_call(body, name=name, out_shape=tuple((jax.ShapeDtypeStruct(s,...  352 us
    pallas_call x1, Pallas kernels, outputs(): pl.pallas_call(outputs_kernel, name='outputs', grid=(8,), in_specs=[pl.Bl...  16.1 us
    pallas_call x1, Pallas kernels, attend(): pl.pallas_call(attend_kernel, name='attend', grid=(2, LEN // block), in_s...  8.43 us

profile of v4, /device:TPU:1, one launch (start us, length us, event | category | flops | bytes accessed | tf_op | source)
XLA Modules:
  0.0 388.0 jit_solution(119669161110444638)
XLA Ops:
  1.3 0.6 pad_add_fusion.place_ref
  1.9 0.1 pad.2.clone
  2.0 4.2 %piece.1.piece_ref = bf16[4,3,176,128]{3,2,1,0:T(8,128)(2,1)} custom-call(s32[4]{0:T(128)} %pad_add_fusion.place_ref, bf16[5461,2,256]{2,1,0:T(2,128)(2,1)} %bitcast.26, bf16[5461,256]{1,0:T(8,128)(2,1)} %bitcast.29), custom_call_target="tpu_custom_call" | custom-call | tf_op jit(solution)/shard_map/piece/pallas_call | solution.py:801
  6.2 54.1 %project.1 = (bf16[8,128,2048]{2,1,0:T(8,128)(2,1)}, bf16[1024,256]{1,0:T(8,128)(2,1)}, bf16[1024,256]{1,0:T(8,128)(2,1)}, bf16[1024,256]{1,0:T(8,128)(2,1)}, bf16[2,2,4,2,704,128]{5,4,3,2,1,0:T(8,128)(2,1)}) custom-call(bf16[128,2048]{1,0:T(8,128)(2,1)} %bitcast.42, bf16[3,2048,256]{2,1,0:T(8,128)(2,1)} %bitcast.27, f32[1024,128]{1,0:T(8,128)} %constant.67.clone.cos_ref, ...), custom_call_target="tpu_custom_call" | custom-call | flops 3221225472 | bytes 20000000 | tf_op jit(solution)/shard_map/project/pallas_call | solution.py:766
  60.3 8.4 %attend.1 = (bf16[1024,256]{1,0:T(8,128)(2,1)}, f32[2,1,1024]{2,1,0:T(1,128)}) custom-call(s32[1]{0:T(128)S(6)} %copy.27.prefix_ref, bf16[1024,256]{1,0:T(8,128)(2,1)} %get-tuple-element.42.q_ref, bf16[1024,256]{1,0:T(8,128)(2,1)} %get-tuple-element.43.k_ref, bf16[1024,256]{1,0:T(8,128)(2,1)} %get-tuple-element.44.v_ref), custom_call_target="tpu_custom_call" | custom-call | tf_op jit(solution)/shard_map/attend/pallas_call | solution.py:872
  68.8 48.2 %attended.1 = (f32[128,2048]{1,0:T(8,128)}, f32[128,2048]{1,0:T(8,128)}, f32[128,128]{1,0:T(8,128)}, bf16[1,2,4,2,704,128]{5,4,3,2,1,0:T(8,128)(2,1)}) custom-call(bf16[1024,256]{1,0:T(8,128)(2,1)} %get-tuple-element.45.heads_ref, bf16[256,2048]{1,0:T(8,128)(2,1)} %w_out_ref.1, bf16[128,2048]{1,0:T(8,128)(2,1)} %bitcast.43, f32[1,2048]{1,0:T(1,128)} %bitcast.48, ...), custom_call_target="tpu_custom_call" | custom-call | flops 1073741824 | bytes 20000000 | tf_op jit(solution)/shard_map/attended/pallas_call | solution.py:766
  117.0 80.0 %feed.1 = (bf16[128,2048]{1,0:T(8,128)(2,1)}, bf16[8,128,2048]{2,1,0:T(8,128)(2,1)}, bf16[8,128,2048]{2,1,0:T(8,128)(2,1)}, bf16[8,128,2304]{2,1,0:T(8,128)(2,1)...) custom-call(s32[16]{0:T(128)} %clusters_ref.1, f32[128,2048]{1,0:T(8,128)} %get-tuple-element.46.normed_ref, ...), custom_call_target="tpu_custom_call" | custom-call | flops 12884901888 | bytes 20000000 | tf_op jit(solution)/shard_map/feed/pallas_call | solution.py:766
  196.9 0.0 copy-start.2
  196.9 76.7 %feed_back.1 = (f32[128,2048]{1,0:T(8,128)}, bf16[8,128,2048]{2,1,0:T(8,128)(2,1)}, bf16[1024,256]{1,0:T(8,128)(2,1)}, f32[2,8,2048]{2,1,0:T(8,128)}, bf16[3,4,176,128]{3,2,1,0:T(8,128)(2,1)}) custom-call(bf16[8,128,2304]{2,1,0:T(8,128)(2,1)} %get-tuple-element.50.act_hbm, f32[128,2048]{1,0:T(8,128)} %get-tuple-element.51.gz_ref, ...), custom_call_target="tpu_custom_call" | custom-call | flops 16106127360 | bytes 20000000 | tf_op jit(solution)/shard_map/feed_back/pallas_call | solution.py:766
  273.6 1.0 reduce_sum.18
  274.6 0.0 copy-done.2
  274.6 0.7 maximum_maximum_fusion.vec_in_ref
  275.3 92.8 %input.1 = (f32[128,16,128]{2,1,0:T(8,128)}, bf16[2,2,4,384,128]{4,3,2,1,0:T(8,128)(2,1)}, bf16[2,2,4,384,128]{4,3,2,1,0:T(8,128)(2,1)}, bf16[2,2,4,128,256]{4,3...) custom-call(s32[1]{0:T(128)S(6)} %copy.27.prefix_ref, ...), custom_call_target="tpu_custom_call" | custom-call | flops 3221225472 | bytes 20000000 | tf_op jit(solution)/shard_map/input/pallas_call | solution.py:766
  368.2 1.5 fusion
  369.7 0.0 copy-start.1
  369.7 0.0 copy-start
  369.7 16.1 %outputs.1 = (f32[5461,2,256]{2,1,0:T(2,128)}, f32[5461,256]{1,0:T(8,128)}, f32[6144,256]{1,0:T(8,128)}, f32[256,2048]{1,0:T(8,128)}) custom-call(bf16[3,4,2,2,704,128]{5,4,3,2,1,0:T(8,128)(2,1)} %get-tuple-element.65.feed_ref, bf16[6144,128]{1,0:T(8,128)(2,1)} %bitcast.30, bf16[6144,128]{1,0:T(8,128)(2,1)} %bitcast.31, bf16[2048,256]{1,0:T(8,128)(2,1)} %bitcast.32), custom_call_target="tpu_custom_call" | custom-call | tf_op jit(solution)/shard_map/outputs/pallas_call | solution.py:1248
  385.7 0.0 copy-done.1
  385.7 0.8 copy.28
  386.5 0.0 copy-done
  386.5 1.0 copy.29
  (2 shorter events, 0.1 us)
Async XLA Ops:
  196.9 77.6 %copy-start.2 = (f32[2,8,2048]{2,1,0:T(8,128)S(1)}, f32[2,8,2048]{2,1,0:T(8,128)}, u32[]{:S(2)}) copy-start(f32[2,8,2048]{2,1,0:T(8,128)} %get-tuple-element.63) | copy-start | bytes 393220
  369.7 16.1 %copy-start.1 = (bf16[128,2048]{1,0:T(8,128)(2,1)S(1)}, bf16[128,2048]{1,0:T(8,128)(2,1)}, u32[]{:S(2)}) copy-start(bf16[128,2048]{1,0:T(8,128)(2,1)} %get-tuple-element.49) | copy-start | bytes 1572868
  369.7 16.9 %copy-start = (f32[128,16,128]{2,1,0:T(8,128)S(1)}, f32[128,16,128]{2,1,0:T(8,128)}, u32[]{:S(2)}) copy-start(f32[128,16,128]{2,1,0:T(8,128)} %get-tuple-element.64) | copy-start | bytes 3145732
